TPU v7x, 256 devices: a whole 4x4x8 slice. The times are simulated.
256 devices in a mesh: rep: 32 (over z_hi, y, core), shard: 8 (over x, z_lo).
Axes of the slice: x: 4, y: 4, z: 8 (z_hi: 4, z_lo: 2; z = z_hi * 2 + z_lo), core: 2. Of those that a mesh axis runs over, the one named last changes fastest.
Arguments:
- tokens: bfloat16 [32768, 2048], P(('rep', 'shard')), may hold values from -6 to 6
- routes: int32 [32768, 2], P(('rep', 'shard')), may hold values from 0 to 7, all different within a row; in each aligned block of 128 rows (0 to 127, 128 to 255, ...) at most 48 rows name the same one
- route_weight: float32 [32768, 2], P(('rep', 'shard')), may hold values from 0.2 to 1
- w_gate: bfloat16 [8, 2048, 768], P('shard'), may hold values from -0.125 to 0.125
- w_up: bfloat16 [8, 2048, 768], P('shard'), may hold values from -0.125 to 0.125
- w_down: bfloat16 [8, 768, 2048], P('shard'), may hold values from -0.21875 to 0.21875
- pseudo_grad: float32 [32, 768, 2048], P('rep', 'shard'), may hold values from -5400 to 5400
- global_params: float32 [768, 2048], P('shard'), may hold values from -6 to 6
- momentum: float32 [768, 2048], P('shard', 'rep'), may hold values from -3 to 3
- local_params: bfloat16 [32, 768, 2048], P('rep', 'shard'), may hold values from -6 to 6
Outputs:
- moe_out: bfloat16 [32768, 2048], P(('rep', 'shard'))
- momentum_next: float32 [768, 2048], P('shard', 'rep')
- local_next: bfloat16 [32, 768, 2048], P('rep', 'shard')
Inputs may be any that keep to these rules, and one draw needn't show every extreme that they name: `routes`: each token names 2 different experts. Within the rows of one device no expert is named by more than 48 rows, and on some device one is named by exactly 48.
All inputs are finite; a program needn't handle non-finite values.
Results may differ from a plain program's by a relative error of at most 0.0057.
Values may be sent and summed in bfloat16 or wider, within the bound.
No kernel may reach another device: no remote copies, remote signals or barrier semaphores. Data moves between devices by JAX's collectives and lax.ppermute only.
A program may use at most 64 MiB of HBM per device.

v0:
```python
import jax
import jax.numpy as jnp
from jax import lax
from jax.sharding import PartitionSpec as P

outer_momentum = 0.9
outer_rate = 0.7
merge_weight = 0.5
clip_epsilon = 1e-06


def slot_table(flat_routes, experts, capacity):
    one_hot = (flat_routes[:, None] == jnp.arange(experts, dtype=jnp.int32)[None, :]).astype(
        jnp.int32
    )
    earlier = jnp.cumsum(one_hot, axis=0) - one_hot
    position = jnp.sum(earlier * one_hot, axis=1)
    return flat_routes * capacity + position


def local(
    tokens,
    routes,
    route_weight,
    w_gate,
    w_up,
    w_down,
    pseudo_grad,
    global_params,
    momentum,
    local_params,
):
    tok_rows, feat_width = tokens.shape
    top_count = routes.shape[1]
    local_experts = w_gate.shape[0]
    experts = local_experts * lax.axis_size("shard")
    capacity = tok_rows * 3 // 8
    slot_index = slot_table(routes.reshape(-1), experts, capacity)
    matches = (
        jnp.arange(experts * capacity, dtype=jnp.int32)[:, None] == slot_index[None, :]
    ).astype(jnp.bfloat16)
    placement = jnp.sum(matches.reshape(experts * capacity, tok_rows, top_count), axis=2)
    outgoing = jnp.dot(placement, tokens, preferred_element_type=jnp.float32).astype(jnp.bfloat16)
    outgoing = outgoing.reshape(experts, capacity, feat_width)
    received = lax.all_to_all(outgoing, "shard", split_axis=0, concat_axis=0, tiled=True)
    total_rows = received.shape[0]
    slot_count = received.shape[1]
    grouped = received.reshape(total_rows // local_experts, local_experts, slot_count, feat_width)
    gate = jnp.einsum("spcd,pdf->spcf", grouped, w_gate, preferred_element_type=jnp.float32)
    upward = jnp.einsum("spcd,pdf->spcf", grouped, w_up, preferred_element_type=jnp.float32)
    hidden = (jax.nn.silu(gate) * upward).astype(jnp.bfloat16)
    result = jnp.einsum(
        "spcf,pfd->spcd", hidden, w_down, preferred_element_type=jnp.float32
    ).astype(jnp.bfloat16)
    result = result.reshape(total_rows, slot_count, feat_width)
    returned = lax.all_to_all(result, "shard", split_axis=0, concat_axis=0, tiled=True)
    picked = returned.reshape(experts * capacity, feat_width)[slot_index]
    picked = picked.reshape(tok_rows, top_count, feat_width).astype(jnp.float32)
    moe_out = jnp.sum(route_weight[:, :, None] * picked, axis=1).astype(jnp.bfloat16)
    replicas = lax.axis_size("rep")
    own_delta = pseudo_grad[0]
    frag_rows = own_delta.shape[0]
    entry_count = float(frag_rows * lax.axis_size("shard") * feat_width)
    col_width = momentum.shape[1]
    col_start = lax.axis_index("rep") * col_width
    delta_total = lax.psum(own_delta, "rep")
    mean_delta = delta_total / replicas
    square_sum = lax.psum(jnp.sum(mean_delta * mean_delta), "shard")
    clip_factor = jnp.minimum(1.0, lax.rsqrt(square_sum / entry_count + clip_epsilon))
    clipped = clip_factor * mean_delta
    full_momentum = lax.all_gather(momentum, "rep", axis=1, tiled=True)
    momentum_full = outer_momentum * full_momentum + clipped
    global_next = global_params - outer_rate * (outer_momentum * momentum_full + clipped)
    momentum_next = lax.dynamic_slice_in_dim(momentum_full, col_start, col_width, 1)
    local_next = (
        merge_weight * local_params.astype(jnp.float32) + (1.0 - merge_weight) * global_next[None]
    ).astype(jnp.bfloat16)
    return (moe_out, momentum_next, local_next)


def solution(mesh):
    in_specs = (
        P(("rep", "shard"), None),
        P(("rep", "shard"), None),
        P(("rep", "shard"), None),
        P("shard", None, None),
        P("shard", None, None),
        P("shard", None, None),
        P("rep", "shard", None),
        P("shard", None),
        P("shard", "rep"),
        P("rep", "shard", None),
    )
    out_specs = (P(("rep", "shard"), None), P("shard", "rep"), P("rep", "shard", None))
    return jax.shard_map(local, mesh=mesh, in_specs=in_specs, out_specs=out_specs, check_vma=False)
```

profile of v0, /device:TPU:0, one launch (start us, length us, event | category | flops | bytes accessed | tf_op | source)
XLA Modules:
  0.0 397.6 jit_solution(12872445767069901383)
XLA Ops:
  7.2 0.0 copy-start
  7.2 0.9 copy.32
  8.1 0.1 eq.44
  8.3 0.1 eq.40
  8.4 0.6 reduce-window.6
  9.0 0.2 slice_reduce_fusion
  9.3 0.1 fusion.32
  9.3 0.1 reduce_sum.44
  9.5 0.6 broadcast_multiply_fusion
  10.1 0.1 copy.35
  10.2 0.1 fusion.30
  10.3 1.6 convolution_convert_fusion
  11.9 0.0 copy-start.5
  11.9 25.5 %all_to_all.10 = bf16[8,48,2048]{2,1,0:T(8,128)(2,1)S(1)} all-to-all(bf16[8,48,2048]{2,1,0:T(8,128)(2,1)S(1)} %bitcast.73), channel_id=1, replica_groups=mesh['rep'=32,'shard'=8] {'shard'}, dimensions={0} | all-to-all | bytes 3145728 | tf_op jit(solution)/shard_map/all_to_all | solution.py:45
  37.4 0.0 copy-start.1
  37.4 1.1 copy-done.1
  38.6 0.0 copy-done.5
  38.6 2.4 fusion.9
  41.0 0.0 copy-done
  41.0 6.9 %fusion.6 = bf16[8,48,2048]{2,1,0:T(8,128)(2,1)} fusion(bf16[1,768,2048]{2,1,0:T(8,128)(2,1)S(1)} %copy-done, bf16[8,48,2048]{2,1,0:T(8,128)(2,1)} %copy-done.1, bf16[1,2048,768]{2,1,0:T(8,128)(2,1)} %param.14, f32[8,1,48,768]{3,2,0,1:T(8,128)} %fusion.9), kind=kOutput, calls=%fused_computation.7 | convolution fusion | flops 2418475008 | bytes 10616832 | tf_op jit(solution)/shard_map/spcf,pfd->spcd/dot_general | solution.py:52
  47.9 4.3 %all-to-all-start.1 = ((bf16[8,48,2048]{2,1,0:T(8,128)(2,1)}), bf16[8,48,2048]{2,1,0:T(8,128)(2,1)}, u32[]{:S(2)}, u32[]{:S(2)}) async-start(bf16[8,48,2048]{2,1,0:T(8,128)(2,1)} %fusion.6), calls=%async_computation.1 | async-start | bytes 3145728 | tf_op jit(solution)/shard_map/all_to_all | solution.py:56
  52.1 0.0 copy-start.4
  52.2 0.0 all-reduce.2.cloned.1.call-start
  52.2 2.5 copy.36
  54.7 0.0 copy-start.2
  54.7 0.0 all-reduce.2.cloned.1.call-update
  54.7 1.0 mul.74
  55.7 0.0 copy-done.4
  55.7 0.7 copy.31
  56.5 2.5 copy.38
  58.9 0.0 copy-done.2
  58.9 1.0 copy.37
  60.0 54.1 %all_gather.3 = f32[96,2048]{0,1:T(8,128)} all-gather(f32[96,64]{0,1:T(8,128)} %param.18), channel_id=1, replica_groups=mesh['rep'=32,'shard'=8] {'rep'}, dimensions={1}, use_global_device_ids=true | all-gather | bytes 811008 | tf_op jit(solution)/shard_map/all_gather | solution.py:71
  114.0 232.4 %all-reduce.2.cloned.1.call-done = f32[96,2048]{0,1:T(8,128)} async-done(((f32[96,2048]{0,1:T(8,128)}), f32[96,2048]{0,1:T(8,128)}) %all-reduce.2.cloned.1.call-update) | async-done | bytes 786448 | tf_op jit(solution)/shard_map/psum | solution.py:66
  346.5 2.1 multiply_reduce_fusion.1
  348.6 20.1 %psum.15 = f32[]{:T(128)} all-reduce(f32[]{:T(128)} %multiply_reduce_fusion.1), channel_id=1, replica_groups=mesh['rep'=32,'shard'=8] {'shard'}, use_global_device_ids=true, to_apply=%region_7.8 | all-reduce | flops 1 | bytes 8 | tf_op jit(solution)/shard_map/psum | solution.py:68
  369.3 3.2 fusion.25
  372.5 2.0 copy.39
  374.5 1.7 multiply_add_fusion
  376.2 0.6 constant_dynamic-slice_fusion
  376.8 0.0 all-to-all-done.1
  376.8 5.0 %gather_fusion = bf16[256,2048]{1,0:T(8,128)(2,1)} fusion(bf16[384,2048]{1,0:T(8,128)(2,1)} %bitcast.18, s32[1024]{0:T(1024)S(1)} %pad_clamp_fusion), kind=kCustom, calls=%fused_computation | custom fusion | bytes 2098176 | tf_op jit(solution)/shard_map/gather | solution.py:57
  381.7 0.0 copy-start.3
  381.7 3.4 reshape.108
  385.2 0.0 copy-done.3
  385.2 5.6 %multiply_reduce_fusion = bf16[128,2048]{1,0:T(8,128)(2,1)} fusion(f32[128,2,2048]{2,1,0:T(2,128)} %reshape.108, f32[128,2]{1,0:T(8,128)S(1)} %copy-done.3), kind=kLoop, calls=%fused_computation.9 | loop fusion | flops 786432 | bytes 2622464 | tf_op jit(solution)/shard_map/reduce_sum | solution.py:59
  (5 shorter events, 0.1 us)
Async XLA Ops:
  7.2 33.8 %copy-start = (bf16[1,768,2048]{2,1,0:T(8,128)(2,1)S(1)}, bf16[1,768,2048]{2,1,0:T(8,128)(2,1)}, u32[]{:S(2)}) copy-start(bf16[1,768,2048]{2,1,0:T(8,128)(2,1)} %param.15) | copy-start | bytes 9437188
  11.9 26.7 %copy-start.5 = (bf16[1,2048,768]{2,1,0:T(8,128)(2,1)S(1)}, bf16[1,2048,768]{2,1,0:T(8,128)(2,1)}, u32[]{:S(2)}) copy-start(bf16[1,2048,768]{2,1,0:T(8,128)(2,1)} %param.13) | copy-start | bytes 9437188
  37.4 1.1 copy-start.1
  47.9 328.9 %all-to-all-start.1 = ((bf16[8,48,2048]{2,1,0:T(8,128)(2,1)}), bf16[8,48,2048]{2,1,0:T(8,128)(2,1)}, u32[]{:S(2)}, u32[]{:S(2)}) async-start(bf16[8,48,2048]{2,1,0:T(8,128)(2,1)} %fusion.6), calls=%async_computation.1 | async-start | bytes 3145728 | tf_op jit(solution)/shard_map/all_to_all | solution.py:56
  52.1 3.6 copy-start.4
  52.2 294.3 %all-reduce.2.cloned.1.call-start = ((), (), s32[]{:S(2)}) async-start(), calls=%async_computation.2 | async-start | bytes 2097152 | tf_op jit(solution)/shard_map/psum | solution.py:66
  54.7 4.3 %copy-start.2 = (bf16[1,96,2048]{2,1,0:T(8,128)(2,1)S(1)}, bf16[1,96,2048]{2,1,0:T(8,128)(2,1)}, u32[]{:S(2)}) copy-start(bf16[1,96,2048]{2,1,0:T(8,128)(2,1)} %param.19) | copy-start | bytes 1179652
  381.7 3.4 copy-start.3
Sparse Core Ops, SparseCore 0:
  55.6 290.7 all-reduce.1
where the time goes:
time: 398 us
  waiting for transfers between devices  232 us (58%)
  blocking collectives  99.6 us (25%)
  local copies, waits for them, and re-layouts  21.5 us (5%)
  between operations  14.8 us (4%)
  other arithmetic  14 us (4%)
  matrix products  10.9 us (3%)
  starting transfers between devices  4.33 us (1%)
    psum x1, waiting for transfers between devices, local(): delta_total = lax.psum(own_delta, 'rep')  232 us
    all_gather x1, blocking collectives, local(): full_momentum = lax.all_gather(momentum, 'rep', axis=1, tiled=True)  54.1 us
    all_to_all x1, blocking collectives, local(): lax.all_to_all(outgoing, 'shard', split_axis=0, concat_axis=0, tiled=True)  25.5 us
    psum x1, blocking collectives, local(): square_sum = lax.psum(jnp.sum(mean_delta * mean_delta), 'shard')  20.1 us
    unnamed x18, local copies, waits for them, and re-layouts  10.8 us
  transfers between devices with their start and end apart: 2, of which 1 were waited for; matrix products, arithmetic and copies ran while one was open for 4% of the time, Pallas kernels for 0%

commit v1 on v0

v1 whole, which is shorter than its diff:
```python
import jax
import jax.numpy as jnp
from jax import lax
from jax.experimental import pallas as pl
from jax.experimental.pallas import tpu as pltpu
from jax.sharding import Mesh
from jax.sharding import PartitionSpec as P

f32 = jnp.float32
bf16 = jnp.bfloat16

outer_momentum = 0.9
outer_rate = 0.7
merge_weight = 0.5
clip_epsilon = 1e-06

EXPERTS = 8
REP = ("zh", "y", "c")
SHARD = ("x", "zl")
VMEM_LIMIT = 48 * 1024 * 1024


def params(**more):
    return pltpu.CompilerParams(vmem_limit_bytes=VMEM_LIMIT, **more)


def whole(count):
    return [pl.BlockSpec(memory_space=pltpu.VMEM)] * count


def slots(routes, tokens, capacity):
    ids = lax.broadcasted_iota(jnp.int32, (EXPERTS, tokens), 0)
    named = jnp.logical_or(routes[0:1, :] == ids, routes[1:2, :] == ids)
    before = lax.broadcasted_iota(jnp.int32, (tokens, tokens), 0) < lax.broadcasted_iota(
        jnp.int32, (tokens, tokens), 1
    )
    place = jnp.dot(
        named.astype(f32).astype(bf16), before.astype(f32).astype(bf16), preferred_element_type=f32
    )
    return jnp.where(named, place.astype(jnp.int32), capacity)


def dispatch_kernel(routes_ref, tokens_ref, out_ref):
    tokens = tokens_ref.shape[0]
    capacity = out_ref.shape[1]
    place = slots(routes_ref[...], tokens, capacity)
    row = lax.broadcasted_iota(jnp.int32, (capacity, tokens), 0)
    table = jnp.concatenate(
        [(row == place[e : e + 1, :]).astype(f32) for e in range(EXPERTS)], axis=0
    ).astype(bf16)
    width = 512
    for j in range(tokens_ref.shape[1] // width):
        cols = pl.ds(j * width, width)
        part = jnp.dot(table, tokens_ref[:, cols], preferred_element_type=f32).astype(bf16)
        out_ref[:, :, cols] = part.reshape(EXPERTS, capacity, width)


def combine_table_kernel(routes_ref, weight_ref, high_ref, low_ref):
    tokens = routes_ref.shape[1]
    capacity = high_ref.shape[1] // EXPERTS
    routes = routes_ref[...]
    place = slots(routes, tokens, capacity)
    row = lax.broadcasted_iota(jnp.int32, (capacity, tokens), 0)
    parts = []
    for e in range(EXPERTS):
        weight = jnp.where(routes[0:1, :] == e, weight_ref[0:1, :], weight_ref[1:2, :])
        parts.append(jnp.where(row == place[e : e + 1, :], weight, 0.0))
    table = jnp.concatenate(parts, axis=0).T
    high = table.astype(bf16)
    high_ref[...] = high
    low_ref[...] = (table - high.astype(f32)).astype(bf16)


def combine_kernel(high_ref, low_ref, rows_ref, out_ref):
    width = 512
    for j in range(out_ref.shape[1] // width):
        cols = pl.ds(j * width, width)
        rows = rows_ref[:, cols]
        out_ref[:, cols] = (
            jnp.dot(high_ref[...], rows, preferred_element_type=f32)
            + jnp.dot(low_ref[...], rows, preferred_element_type=f32)
        ).astype(bf16)


def ffn_kernel(x_ref, gate_ref, up_ref, down_ref, out_ref, total):
    step = pl.program_id(0)
    x = x_ref[...]
    gate = jnp.dot(x, gate_ref[0], preferred_element_type=f32)
    up = jnp.dot(x, up_ref[0], preferred_element_type=f32)
    hidden = (gate / (1.0 + jnp.exp(-gate)) * up).astype(bf16)
    width = 512
    for j in range(out_ref.shape[1] // width):
        cols = pl.ds(j * width, width)
        part = jnp.dot(hidden, down_ref[0, :, cols], preferred_element_type=f32)

        @pl.when(step == 0)
        def _():
            total[:, cols] = part

        @pl.when(step > 0)
        def _():
            total[:, cols] += part

    @pl.when(step == pl.num_programs(0) - 1)
    def _():
        out_ref[...] = total[...].astype(bf16)


def ffn(x, w_gate, w_up, w_down):
    rows, width = x.shape
    hidden = w_gate.shape[2]
    block = 256
    return pl.pallas_call(
        ffn_kernel,
        grid=(hidden // block,),
        in_specs=[
            pl.BlockSpec((rows, width), lambda i: (0, 0)),
            pl.BlockSpec((1, width, block), lambda i: (0, 0, i)),
            pl.BlockSpec((1, width, block), lambda i: (0, 0, i)),
            pl.BlockSpec((1, block, width), lambda i: (0, i, 0)),
        ],
        out_specs=pl.BlockSpec((rows, width), lambda i: (0, 0)),
        out_shape=jax.ShapeDtypeStruct((rows, width), bf16),
        scratch_shapes=[pltpu.VMEM((rows, width), f32)],
        compiler_params=params(),
        cost_estimate=pl.CostEstimate(
            flops=6 * rows * width * hidden,
            bytes_accessed=6 * width * hidden + 4 * rows * width,
            transcendentals=rows * hidden,
        ),
        name="expert_ffn",
    )(x, w_gate, w_up, w_down)


def split_y_kernel(at_ref, own_ref, got_ref, keep_ref, *send_refs):
    core, me = at_ref[0], at_ref[1]
    width = keep_ref.shape[1]
    half = got_ref.shape[1]
    for k, ref in enumerate((keep_ref,) + send_refs):
        start = jnp.bitwise_xor(me, k) * width
        mine = own_ref[:, pl.ds(pl.multiple_of(core * half + start, width), width)]
        other = got_ref[:, pl.ds(pl.multiple_of(start, width), width)]
        ref[...] = (mine + other).astype(ref.dtype)


def split_z_kernel(at_ref, own_ref, a_ref, b_ref, c_ref, keep_ref, s1_ref, s2_ref, s3_ref, total):
    me = at_ref[2]
    rows, width = keep_ref.shape
    full = (own_ref[...] + a_ref[...].astype(f32)) + (
        b_ref[...].astype(f32) + c_ref[...].astype(f32)
    )
    for p in range(4):
        total[p] = full[(p & 1) * rows : (p & 1) * rows + rows, (p >> 1) * width : (p >> 1) * width + width]
    for k, ref in enumerate((keep_ref, s1_ref, s2_ref, s3_ref)):
        ref[...] = total[jnp.bitwise_xor(me, k)].astype(ref.dtype)


def mean_kernel(replicas, own_ref, a_ref, b_ref, c_ref, mom_ref, out_ref):
    full = (own_ref[...] + a_ref[...].astype(f32)) + (
        b_ref[...].astype(f32) + c_ref[...].astype(f32)
    )
    out_ref[0, 0] = (full * (1.0 / replicas)).astype(bf16)
    out_ref[0, 1] = mom_ref[...].astype(bf16)


def square_kernel(a_ref, b_ref, out_ref):
    total = jnp.zeros(out_ref.shape, f32)
    step = out_ref.shape[0]
    for ref in (a_ref, b_ref):
        for j in range(ref.shape[0]):
            block = ref[j, 0].astype(f32)
            block = block * block
            for i in range(block.shape[0] // step):
                total += block[i * step : i * step + step]
    out_ref[...] = total


def outer_kernel(
    entries, at_ref, s0, s1, s2, s3, near_ref, far_ref, params_ref, local_ref, mom_ref, next_ref, mom_out, scratch
):
    me = at_ref[3]
    squares = (s0[...] + s1[...]) + (s2[...] + s3[...])
    squares = jnp.sum(jnp.sum(squares, axis=1, keepdims=True), axis=0, keepdims=True)
    clip = jnp.minimum(1.0, lax.rsqrt(squares * (1.0 / entries) + clip_epsilon))

    def block(piece, which):
        j = jnp.bitwise_xor(piece, me)
        low = jnp.bitwise_and(j, 15)
        return jnp.where(
            j < 16, near_ref[low, which].astype(f32), far_ref[low, which].astype(f32)
        )

    def piece_of(rep):
        return (rep & 1) * 16 + ((rep >> 1) & 3) * 4 + (rep >> 3)

    for cb in range(16):
        m0 = block(piece_of(2 * cb), 1)
        m1 = block(piece_of(2 * cb + 1), 1)
        for h in range(2):
            rows, cols = pl.ds(h * 48, 48), pl.ds(cb * 128, 128)
            mom = jnp.concatenate([m0[:, h * 64 : h * 64 + 64], m1[:, h * 64 : h * 64 + 64]], axis=1)
            clipped = clip * block(cb * 2 + h, 0)
            after = outer_momentum * mom + clipped
            outer = params_ref[rows, cols] - outer_rate * (outer_momentum * after + clipped)
            local = local_ref[rows, cols].astype(f32)
            next_ref[rows, cols] = (merge_weight * local + (1.0 - merge_weight) * outer).astype(bf16)
    rep = at_ref[4]
    first = jnp.right_shift(rep, 1) * 2
    scratch[...] = jnp.zeros_like(scratch)
    scratch[0:48, :] = block(first, 0)
    scratch[48:96, :] = block(first + 1, 0)
    scratch[...] = scratch[...].T
    start = pl.multiple_of(jnp.bitwise_and(rep, 1) * 64, 64)
    mom_out[...] = outer_momentum * mom_ref[...] + clip * scratch[pl.ds(start, 64), 0:96]


def smem():
    return pl.BlockSpec(memory_space=pltpu.SMEM)


def swap(value, axis, bits):
    size = lax.axis_size(axis)
    return lax.ppermute(value, axis, [(i, i ^ bits) for i in range(size)])


def outer_step(pseudo_grad, global_params, momentum, local_params):
    own = pseudo_grad[0]
    rows, width = own.shape
    core, y, zh = lax.axis_index("c"), lax.axis_index("y"), lax.axis_index("zh")
    rep = (zh * 4 + y) * 2 + core
    at = jnp.stack([core, y, zh, core * 16 + y * 4 + zh, rep]).astype(jnp.int32)
    half = width // 2
    other = lax.dynamic_slice_in_dim(own, (1 - core) * half, half, 1)
    got = swap(other, "c", 1)
    quarter = half // 4
    keep, *sends = pl.pallas_call(
        split_y_kernel,
        in_specs=[smem()] + whole(2),
        out_specs=whole(4),
        out_shape=[jax.ShapeDtypeStruct((rows, quarter), f32)]
        + [jax.ShapeDtypeStruct((rows, quarter), bf16)] * 3,
        compiler_params=params(),
        name="delta_split_y",
    )(at, own, got)
    got = [swap(s, "y", k + 1) for k, s in enumerate(sends)]
    keep, *sends = pl.pallas_call(
        split_z_kernel,
        in_specs=[smem()] + whole(4),
        out_specs=whole(4),
        out_shape=[jax.ShapeDtypeStruct((rows // 2, quarter // 2), f32)] * 4,
        scratch_shapes=[pltpu.VMEM((4, rows // 2, quarter // 2), f32)],
        compiler_params=params(),
        name="delta_split_z",
    )(at, keep, *got)
    got = [swap(s, "zh", k + 1) for k, s in enumerate(sends)]
    mom_block = jnp.concatenate([momentum[: rows // 2], momentum[rows // 2 :]], axis=1)
    block = pl.pallas_call(
        lambda *refs: mean_kernel(32, *refs),
        in_specs=whole(5),
        out_specs=whole(1)[0],
        out_shape=jax.ShapeDtypeStruct((1, 2, rows // 2, quarter // 2), bf16),
        compiler_params=params(),
        name="delta_mean",
    )(keep, *got, mom_block)
    block = jnp.concatenate([block] + [swap(block, "zh", k) for k in (1, 2, 3)], axis=0)
    block = jnp.concatenate([block] + [swap(block, "y", k) for k in (1, 2, 3)], axis=0)
    far = swap(block, "c", 1)
    squares = pl.pallas_call(
        square_kernel,
        in_specs=whole(2),
        out_specs=whole(1)[0],
        out_shape=jax.ShapeDtypeStruct((8, 128), f32),
        compiler_params=params(),
        name="delta_squares",
    )(block, far)
    squares = squares + swap(squares, "zl", 1)
    parts = [squares] + [swap(squares, "x", k) for k in (1, 2, 3)]
    entries = float(rows * 8 * width)
    local_next, momentum_next = pl.pallas_call(
        lambda *refs: outer_kernel(entries, *refs),
        in_specs=[smem()] + whole(9),
        out_specs=whole(2),
        out_shape=[
            jax.ShapeDtypeStruct((rows, width), bf16),
            jax.ShapeDtypeStruct((momentum.shape[1], rows), f32),
        ],
        scratch_shapes=[pltpu.VMEM((128, 128), f32)],
        compiler_params=params(),
        name="outer_update",
    )(at, *parts, block, far, global_params, local_params[0], momentum.T)
    return momentum_next.T, local_next[None]


def local(
    tokens, routes, route_weight, w_gate, w_up, w_down, pseudo_grad, global_params, momentum, local_params
):
    tok_rows, feat_width = tokens.shape
    capacity = tok_rows * 3 // 8
    routes_t, weight_t = routes.T, route_weight.T
    outgoing = pl.pallas_call(
        dispatch_kernel,
        in_specs=whole(2),
        out_specs=whole(1)[0],
        out_shape=jax.ShapeDtypeStruct((EXPERTS, capacity, feat_width), bf16),
        compiler_params=params(),
        name="dispatch",
    )(routes_t, tokens)
    high, low = pl.pallas_call(
        combine_table_kernel,
        in_specs=whole(2),
        out_specs=whole(2),
        out_shape=[jax.ShapeDtypeStruct((tok_rows, EXPERTS * capacity), bf16)] * 2,
        compiler_params=params(),
        name="combine_table",
    )(routes_t, weight_t)
    received = lax.all_to_all(outgoing, SHARD, split_axis=0, concat_axis=0, tiled=True)
    result = ffn(received.reshape(EXPERTS * capacity, feat_width), w_gate, w_up, w_down)
    result = result.reshape(EXPERTS, capacity, feat_width)
    returned = lax.all_to_all(result, SHARD, split_axis=0, concat_axis=0, tiled=True)
    moe_out = pl.pallas_call(
        combine_kernel,
        in_specs=whole(3),
        out_specs=whole(1)[0],
        out_shape=jax.ShapeDtypeStruct((tok_rows, feat_width), bf16),
        compiler_params=params(),
        name="combine",
    )(high, low, returned.reshape(EXPERTS * capacity, feat_width))
    momentum_next, local_next = outer_step(pseudo_grad, global_params, momentum, local_params)
    return (moe_out, momentum_next, local_next)


def solution(mesh):
    fine = Mesh(mesh.devices.reshape(4, 4, 2, 4, 2), REP + SHARD)
    in_specs = (
        P(REP + SHARD, None),
        P(REP + SHARD, None),
        P(REP + SHARD, None),
        P(SHARD, None, None),
        P(SHARD, None, None),
        P(SHARD, None, None),
        P(REP, SHARD, None),
        P(SHARD, None),
        P(SHARD, REP),
        P(REP, SHARD, None),
    )
    out_specs = (P(REP + SHARD, None), P(SHARD, REP), P(REP, SHARD, None))
    return jax.shard_map(local, mesh=fine, in_specs=in_specs, out_specs=out_specs, check_vma=False)
```

time: 398 us -> 110 us (0.28)
  the two profiles are of different devices: /device:TPU:0 before, /device:TPU:24 now
where the time goes in v1:
time: 110 us
  starting transfers between devices  34.5 us (31%)
  blocking collectives  27 us (25%)
  waiting for transfers between devices  25.2 us (23%)
  Pallas kernels  14.9 us (14%)
  local copies, waits for them, and re-layouts  7.43 us (7%)
    ppermute x18, starting transfers between devices, swap(): return lax.ppermute(value, axis, [(i, i ^ bits) for i in range(size)])  30.8 us
    all_to_all x1, blocking collectives, local(): lax.all_to_all(outgoing, SHARD, split_axis=0, concat_axis=0, tiled=True)  27 us
    ppermute x18, waiting for transfers between devices, swap(): return lax.ppermute(value, axis, [(i, i ^ bits) for i in range(size)])  25.2 us
    pallas_call x1, Pallas kernels, ffn(): pl.pallas_call(ffn_kernel, grid=(hidden // block,), in_specs=[pl.BlockSpe...  8.59 us
    unnamed x34, local copies, waits for them, and re-layouts  6.39 us
    all_to_all x1, starting transfers between devices, local(): lax.all_to_all(result, SHARD, split_axis=0, concat_axis=0, tiled=True)  3.71 us
  transfers between devices with their start and end apart: 19, of which 13 were waited for; matrix products, arithmetic and copies ran while one was open for 1% of the time, Pallas kernels for 4%

profile of v1, /device:TPU:24, one launch (start us, length us, event | category | flops | bytes accessed | tf_op | source)
XLA Modules:
  0.0 110.0 jit_solution(2978597815110986176)
XLA Ops:
  0.6 0.0 copy-start.3
  0.6 1.0 copy-done.3
  1.7 0.7 copy-done.10
  2.4 0.7 dispatch.1
  3.0 27.0 %all_to_all.10 = bf16[8,48,2048]{2,1,0:T(8,128)(2,1)S(1)} all-to-all(bf16[8,48,2048]{2,1,0:T(8,128)(2,1)S(1)} %dispatch.1), channel_id=1, replica_groups=mesh['zh'=4,'y'=4,'c'=2,'x'=4,'zl'=2] {'x','zl'}, dimensions={0} | all-to-all | bytes 3145728 | tf_op jit(solution)/shard_map/all_to_all | solution.py:316
  30.0 8.6 %expert_ffn.1 = bf16[384,2048]{1,0:T(8,128)(2,1)S(1)} custom-call(bf16[384,2048]{1,0:T(8,128)(2,1)S(1)} %bitcast.20, bf16[1,2048,768]{2,1,0:T(8,128)(2,1)} %gate_ref.1, bf16[1,2048,768]{2,1,0:T(8,128)(2,1)} %up_ref.1, bf16[1,768,2048]{2,1,0:T(8,128)(2,1)} %down_ref.1), custom_call_target="tpu_custom_call" | custom-call | flops 3623878656 | bytes 12582912 | tf_op jit(solution)/shard_map/expert_ffn/pallas_call | solution.py:113
  38.6 0.0 copy-start.1
  38.6 1.2 %copy-done.1 = bf16[384,2048]{1,0:T(8,128)(2,1)} copy-done((bf16[384,2048]{1,0:T(8,128)(2,1)}, bf16[384,2048]{1,0:T(8,128)(2,1)S(1)}, u32[]{:S(2)}) %copy-start.1) | copy-done | bytes 1572888
  39.8 3.7 %all-to-all-start.1 = ((bf16[8,48,2048]{2,1,0:T(8,128)(2,1)}), bf16[8,48,2048]{2,1,0:T(8,128)(2,1)S(1)}, u32[]{:S(2)}, u32[]{:S(2)}) async-start(bf16[8,48,2048]{2,1,0:T(8,128)(2,1)} %bitcast.19), calls=%async_computation.1 | async-start | bytes 3145728 | tf_op jit(solution)/shard_map/all_to_all | solution.py:319
  43.5 0.0 copy-done
  43.6 0.1 collective-permute-start
  43.7 0.1 stack.23.at_ref.refs_0_
  43.8 1.6 %collective-permute-done.got_ref = f32[96,1024]{1,0:T(8,128)S(1)} collective-permute-done((f32[96,1024]{1,0:T(8,128)S(1)}, f32[96,1024]{1,0:T(8,128)S(1)}, u32[]{:S(2)}, u32[]{:S(2)}) %collective-permute-start) | collective-permute-done | bytes 393248 | tf_op jit(solution)/shard_map/ppermute | solution.py:223
  45.4 0.7 copy-done.5
  46.1 1.0 copy-done.6
  47.2 1.2 %delta_split_y.1 = (f32[96,256]{1,0:T(8,128)S(1)}, bf16[96,256]{1,0:T(8,128)(2,1)}, bf16[96,256]{1,0:T(8,128)(2,1)}, bf16[96,256]{1,0:T(8,128)(2,1)}) custom-call(s32[5]{0:T(128)S(1)} %stack.23.at_ref.refs_0_, f32[96,2048]{1,0:T(8,128)S(1)} %bitcast.18, f32[96,1024]{1,0:T(8,128)S(1)} %copy-done.6), custom_call_target="tpu_custom_call" | custom-call | tf_op jit(solution)/shard_map/delta_split_y/pallas_call | solution.py:236
  48.4 0.6 copy-done.8
  49.0 0.7 collective-permute-start.1
  49.8 0.9 collective-permute-start.2
  50.7 3.0 %collective-permute-start.3 = (bf16[96,256]{1,0:T(8,128)(2,1)}, bf16[96,256]{1,0:T(8,128)(2,1)S(1)}, u32[]{:S(2)}, u32[]{:S(2)}) collective-permute-start(bf16[96,256]{1,0:T(8,128)(2,1)} %get-tuple-element.20), channel_id=1, source_target_pairs={{0,48},{16,32},{32,16},{48,0},{1,49},{17,33},{33,17},{49,1},{2,50}... | collective-permute-start | bytes 147464 | tf_op jit(solution)/shard_map/ppermute | solution.py:223
  53.7 0.9 fusion
  54.6 0.1 copy.16
  54.7 0.1 copy.15
  54.8 0.0 collective-permute-done.1.a_ref
  54.8 0.8 collective-permute-done.2.b_ref
  55.6 0.6 collective-permute-done.3.c_ref
  56.2 0.9 copy-done.9
  57.1 0.6 delta_split_z.1
  57.7 3.4 %collective-permute-start.4 = (f32[48,128]{1,0:T(8,128)S(1)}, f32[48,128]{1,0:T(8,128)S(1)}, u32[]{:S(2)}, u32[]{:S(2)}) collective-permute-start(f32[48,128]{1,0:T(8,128)S(1)} %get-tuple-element.22), channel_id=1, source_target_pairs={{0,64},{64,0},{128,192},{192,128},{1,65},{65,1},{129,193},{193,129... | collective-permute-start | bytes 73736 | tf_op jit(solution)/shard_map/ppermute | solution.py:223
  61.1 4.5 %collective-permute-start.5 = (f32[48,128]{1,0:T(8,128)S(1)}, f32[48,128]{1,0:T(8,128)S(1)}, u32[]{:S(2)}, u32[]{:S(2)}) collective-permute-start(f32[48,128]{1,0:T(8,128)S(1)} %get-tuple-element.23), channel_id=1, source_target_pairs={{0,128},{64,192},{128,0},{192,64},{1,129},{65,193},{129,1},{193,65... | collective-permute-start | bytes 73736 | tf_op jit(solution)/shard_map/ppermute | solution.py:223
  65.5 0.0 collective-permute-start.6
  65.6 0.1 pad_maximum_fusion.1.refs_4_
  65.6 0.0 collective-permute-done.4.refs_1_
  65.6 3.2 %collective-permute-done.5.refs_2_ = f32[48,128]{1,0:T(8,128)S(1)} collective-permute-done((f32[48,128]{1,0:T(8,128)S(1)}, f32[48,128]{1,0:T(8,128)S(1)}, u32[]{:S(2)}, u32[]{:S(2)}) %collective-permute-start.5) | collective-permute-done | bytes 24608 | tf_op jit(solution)/shard_map/ppermute | solution.py:223
  68.8 2.7 %collective-permute-done.6.refs_3_ = f32[48,128]{1,0:T(8,128)S(1)} collective-permute-done((f32[48,128]{1,0:T(8,128)S(1)}, f32[48,128]{1,0:T(8,128)S(1)}, u32[]{:S(2)}, u32[]{:S(2)}) %collective-permute-start.6) | collective-permute-done | bytes 24608 | tf_op jit(solution)/shard_map/ppermute | solution.py:223
  71.5 1.5 %collective-permute-start.7 = (bf16[1,2,48,128]{3,2,1,0:T(8,128)(2,1)S(1)}, bf16[1,2,48,128]{3,2,1,0:T(8,128)(2,1)S(1)}, u32[]{:S(2)}, u32[]{:S(2)}) collective-permute-start(bf16[1,2,48,128]{3,2,1,0:T(8,128)(2,1)S(1)} %delta_mean.1), channel_id=1, source_target_pairs={{0,64},{64,0},{128,192},{192,128},{1,65},{65,1},{129,193},{193,129... | collective-permute-start | bytes 73736 | tf_op jit(solution)/shard_map/ppermute | solution.py:223
  73.0 1.8 %collective-permute-start.8 = (bf16[1,2,48,128]{3,2,1,0:T(8,128)(2,1)S(1)}, bf16[1,2,48,128]{3,2,1,0:T(8,128)(2,1)S(1)}, u32[]{:S(2)}, u32[]{:S(2)}) collective-permute-start(bf16[1,2,48,128]{3,2,1,0:T(8,128)(2,1)S(1)} %delta_mean.1), channel_id=1, source_target_pairs={{0,128},{64,192},{128,0},{192,64},{1,129},{65,193},{129,1},{193,65... | collective-permute-start | bytes 73736 | tf_op jit(solution)/shard_map/ppermute | solution.py:223
  74.8 3.2 %collective-permute-start.9 = (bf16[1,2,48,128]{3,2,1,0:T(8,128)(2,1)S(1)}, bf16[1,2,48,128]{3,2,1,0:T(8,128)(2,1)S(1)}, u32[]{:S(2)}, u32[]{:S(2)}) collective-permute-start(bf16[1,2,48,128]{3,2,1,0:T(8,128)(2,1)S(1)} %delta_mean.1), channel_id=1, source_target_pairs={{0,192},{64,128},{128,64},{192,0},{1,193},{65,129},{129,65},{193,1... | collective-permute-start | bytes 73736 | tf_op jit(solution)/shard_map/ppermute | solution.py:223
  78.1 0.0 collective-permute-done.7
  78.1 2.7 %collective-permute-done.8 = bf16[1,2,48,128]{3,2,1,0:T(8,128)(2,1)S(1)} collective-permute-done((bf16[1,2,48,128]{3,2,1,0:T(8,128)(2,1)S(1)}, bf16[1,2,48,128]{3,2,1,0:T(8,128)(2,1)S(1)}, u32[]{:S(2)}, u32[]{:S(2)}) %collective-permute-start.8) | collective-permute-done | bytes 24608 | tf_op jit(solution)/shard_map/ppermute | solution.py:223
  80.8 0.2 collective-permute-done.9
  81.1 0.7 collective-permute-start.10
  81.8 3.8 %collective-permute-start.11 = (bf16[4,2,48,128]{3,2,1,0:T(8,128)(2,1)S(1)}, bf16[4,2,48,128]{3,2,1,0:T(8,128)(2,1)S(1)}, u32[]{:S(2)}, u32[]{:S(2)}) collective-permute-start(bf16[4,2,48,128]{3,2,1,0:T(8,128)(2,1)S(1)} %pad_maximum_fusion), channel_id=1, source_target_pairs={{0,32},{16,48},{32,0},{48,16},{1,33},{17,49},{33,1},{49,17},{2,34}... | collective-permute-start | bytes 294920 | tf_op jit(solution)/shard_map/ppermute | solution.py:223
  85.6 0.2 collective-permute-start.12
  85.9 0.0 collective-permute-done.10
  85.9 3.4 %collective-permute-done.11 = bf16[4,2,48,128]{3,2,1,0:T(8,128)(2,1)S(1)} collective-permute-done((bf16[4,2,48,128]{3,2,1,0:T(8,128)(2,1)S(1)}, bf16[4,2,48,128]{3,2,1,0:T(8,128)(2,1)S(1)}, u32[]{:S(2)}, u32[]{:S(2)}) %collective-permute-start.11) | collective-permute-done | bytes 98336 | tf_op jit(solution)/shard_map/ppermute | solution.py:223
  89.3 2.2 %collective-permute-done.12 = bf16[4,2,48,128]{3,2,1,0:T(8,128)(2,1)S(1)} collective-permute-done((bf16[4,2,48,128]{3,2,1,0:T(8,128)(2,1)S(1)}, bf16[4,2,48,128]{3,2,1,0:T(8,128)(2,1)S(1)}, u32[]{:S(2)}, u32[]{:S(2)}) %collective-permute-start.12) | collective-permute-done | bytes 98336 | tf_op jit(solution)/shard_map/ppermute | solution.py:223
  91.5 0.1 collective-permute-start.13
  91.6 1.7 %collective-permute-done.13.b_ref.refs_6_ = bf16[16,2,48,128]{3,2,1,0:T(8,128)(2,1)S(1)} collective-permute-done((bf16[16,2,48,128]{3,2,1,0:T(8,128)(2,1)S(1)}, bf16[16,2,48,128]{3,2,1,0:T(8,128)(2,1)S(1)}, u32[]{:S(2)}, u32[]{:S(2)}) %collective-permute-start.13) | collective-permute-done | bytes 393248 | tf_op jit(solution)/shard_map/ppermute | solution.py:223
  93.3 0.2 delta_squares.1
  93.5 2.0 %collective-permute-start.14 = (f32[8,128]{1,0:T(8,128)S(1)}, f32[8,128]{1,0:T(8,128)S(1)}, u32[]{:S(2)}, u32[]{:S(2)}) collective-permute-start(f32[8,128]{1,0:T(8,128)S(1)} %delta_squares.1), channel_id=1, source_target_pairs={{0,1},{1,0},{2,3},{3,2},{4,5},{5,4},{6,7},{7,6},{8,9},{9,8},{10,11... | collective-permute-start | bytes 12296 | tf_op jit(solution)/shard_map/ppermute | solution.py:223
  95.5 1.7 %collective-permute-done.14 = f32[8,128]{1,0:T(8,128)S(1)} collective-permute-done((f32[8,128]{1,0:T(8,128)S(1)}, f32[8,128]{1,0:T(8,128)S(1)}, u32[]{:S(2)}, u32[]{:S(2)}) %collective-permute-start.14) | collective-permute-done | bytes 4128 | tf_op jit(solution)/shard_map/ppermute | solution.py:223
  97.2 1.9 %collective-permute-start.15 = (f32[8,128]{1,0:T(8,128)S(1)}, f32[8,128]{1,0:T(8,128)S(1)}, u32[]{:S(2)}, u32[]{:S(2)}) collective-permute-start(f32[8,128]{1,0:T(8,128)S(1)} %add.23.refs_1_), channel_id=1, source_target_pairs={{0,2},{2,0},{4,6},{6,4},{1,3},{3,1},{5,7},{7,5},{8,10},{10,8},{12,... | collective-permute-start | bytes 12296 | tf_op jit(solution)/shard_map/ppermute | solution.py:223
  99.1 2.7 %collective-permute-start.16 = (f32[8,128]{1,0:T(8,128)S(1)}, f32[8,128]{1,0:T(8,128)S(1)}, u32[]{:S(2)}, u32[]{:S(2)}) collective-permute-start(f32[8,128]{1,0:T(8,128)S(1)} %add.23.refs_1_), channel_id=1, source_target_pairs={{0,4},{2,6},{4,0},{6,2},{1,5},{3,7},{5,1},{7,3},{8,12},{10,14},{12... | collective-permute-start | bytes 12296 | tf_op jit(solution)/shard_map/ppermute | solution.py:223
  101.8 0.1 collective-permute-start.17
  101.9 0.0 copy-done.11
  101.9 0.3 combine_table.1
  102.2 0.0 collective-permute-done.15.refs_2_
  102.2 2.0 %collective-permute-done.16.refs_3_ = f32[8,128]{1,0:T(8,128)S(1)} collective-permute-done((f32[8,128]{1,0:T(8,128)S(1)}, f32[8,128]{1,0:T(8,128)S(1)}, u32[]{:S(2)}, u32[]{:S(2)}) %collective-permute-start.16) | collective-permute-done | bytes 4128 | tf_op jit(solution)/shard_map/ppermute | solution.py:223
  104.2 2.4 %collective-permute-done.17.refs_4_ = f32[8,128]{1,0:T(8,128)S(1)} collective-permute-done((f32[8,128]{1,0:T(8,128)S(1)}, f32[8,128]{1,0:T(8,128)S(1)}, u32[]{:S(2)}, u32[]{:S(2)}) %collective-permute-start.17) | collective-permute-done | bytes 4128 | tf_op jit(solution)/shard_map/ppermute | solution.py:223
  106.6 0.0 copy-done.4
  106.6 1.9 %outer_update.1 = (bf16[96,2048]{1,0:T(8,128)(2,1)}, f32[64,96]{1,0:T(8,128)}) custom-call(s32[5]{0:T(128)S(1)} %stack.23.at_ref.refs_0_, f32[8,128]{1,0:T(8,128)S(1)} %add.23.refs_1_, f32[8,128]{1,0:T(8,128)S(1)} %collective-permute-done.15.refs_2_, f32[8,128]{1,0:T(8,128)S(1)} %collective-permute-done.16.refs_3_, ...), custom_call_target="tpu_custom_call" | custom-call | tf_op jit(solution)/shard_map/outer_update/pallas_call | solution.py:279
  108.5 0.0 all-to-all-done.1
  108.5 1.5 %combine.1 = bf16[128,2048]{1,0:T(8,128)(2,1)} custom-call(bf16[128,384]{1,0:T(8,128)(2,1)S(1)} %get-tuple-element.15.high_ref, bf16[128,384]{1,0:T(8,128)(2,1)S(1)} %get-tuple-element.16.low_ref, bf16[384,2048]{1,0:T(8,128)(2,1)S(1)} %bitcast.17), custom_call_target="tpu_custom_call" | custom-call | tf_op jit(solution)/shard_map/combine/pallas_call | solution.py:320
  (25 shorter events, 0.2 us)
Async XLA Ops:
  0.6 1.0 copy-start.3
  1.7 0.7 copy-start.10
  38.6 1.2 %copy-start.1 = (bf16[384,2048]{1,0:T(8,128)(2,1)}, bf16[384,2048]{1,0:T(8,128)(2,1)S(1)}, u32[]{:S(2)}) copy-start(bf16[384,2048]{1,0:T(8,128)(2,1)S(1)} %expert_ffn.1) | copy-start | bytes 4718596
  39.8 3.7 %copy-start = (f32[1,96,2048]{2,1,0:T(8,128)S(1)}, f32[1,96,2048]{2,1,0:T(8,128)}, u32[]{:S(2)}) copy-start(f32[1,96,2048]{2,1,0:T(8,128)} %param.16) | copy-start | bytes 2359300
  39.8 68.7 %all-to-all-start.1 = ((bf16[8,48,2048]{2,1,0:T(8,128)(2,1)}), bf16[8,48,2048]{2,1,0:T(8,128)(2,1)S(1)}, u32[]{:S(2)}, u32[]{:S(2)}) async-start(bf16[8,48,2048]{2,1,0:T(8,128)(2,1)} %bitcast.19), calls=%async_computation.1 | async-start | bytes 3145728 | tf_op jit(solution)/shard_map/all_to_all | solution.py:319
  43.6 1.8 %collective-permute-start = (f32[96,1024]{1,0:T(8,128)S(1)}, f32[96,1024]{1,0:T(8,128)S(1)}, u32[]{:S(2)}, u32[]{:S(2)}) collective-permute-start(f32[96,1024]{1,0:T(8,128)S(1)} %dynamic-slice_bitcast_fusion), channel_id=1, source_target_pairs={{0,8},{8,0},{1,9},{9,1},{2,10},{10,2},{3,11},{11,3},{4,12},{12,4},... | collective-permute-start | bytes 1179656 | tf_op jit(solution)/shard_map/ppermute | solution.py:223
  45.4 0.7 copy-start.5
  46.1 1.0 copy-start.6
  47.1 54.7 %copy-start.11 = (s32[128,2]{0,1:T(2,128)S(1)}, s32[128,2]{0,1:T(2,128)}, u32[]{:S(2)}) copy-start(s32[128,2]{0,1:T(2,128)} %param.11) | copy-start | bytes 3076
  47.1 54.7 %copy-start.12 = (f32[128,2]{0,1:T(2,128)S(1)}, f32[128,2]{0,1:T(2,128)}, u32[]{:S(2)}) copy-start(f32[128,2]{0,1:T(2,128)} %param.12) | copy-start | bytes 3076
  47.1 59.4 %copy-start.2 = (f32[96,2048]{1,0:T(8,128)S(1)}, f32[96,2048]{1,0:T(8,128)}, u32[]{:S(2)}) copy-start(f32[96,2048]{1,0:T(8,128)} %refs_7_.1) | copy-start | bytes 2359300
  47.1 59.4 %copy-start.4 = (bf16[1,96,2048]{2,1,0:T(8,128)(2,1)S(1)}, bf16[1,96,2048]{2,1,0:T(8,128)(2,1)}, u32[]{:S(2)}) copy-start(bf16[1,96,2048]{2,1,0:T(8,128)(2,1)} %param.19) | copy-start | bytes 1179652
  48.4 0.6 copy-start.8
  49.0 57.6 %copy-start.7 = (f32[96,64]{0,1:T(8,128)S(1)}, f32[96,64]{0,1:T(8,128)}, u32[]{:S(2)}) copy-start(f32[96,64]{0,1:T(8,128)} %param.18) | copy-start | bytes 73732
  49.0 5.8 %collective-permute-start.1 = (bf16[96,256]{1,0:T(8,128)(2,1)}, bf16[96,256]{1,0:T(8,128)(2,1)S(1)}, u32[]{:S(2)}, u32[]{:S(2)}) collective-permute-start(bf16[96,256]{1,0:T(8,128)(2,1)} %get-tuple-element.18), channel_id=1, source_target_pairs={{0,16},{16,0},{32,48},{48,32},{1,17},{17,1},{33,49},{49,33},{2,18}... | collective-permute-start | bytes 147464 | tf_op jit(solution)/shard_map/ppermute | solution.py:223
  49.8 5.8 %collective-permute-start.2 = (bf16[96,256]{1,0:T(8,128)(2,1)}, bf16[96,256]{1,0:T(8,128)(2,1)S(1)}, u32[]{:S(2)}, u32[]{:S(2)}) collective-permute-start(bf16[96,256]{1,0:T(8,128)(2,1)} %get-tuple-element.19), channel_id=1, source_target_pairs={{0,32},{16,48},{32,0},{48,16},{1,33},{17,49},{33,1},{49,17},{2,34}... | collective-permute-start | bytes 147464 | tf_op jit(solution)/shard_map/ppermute | solution.py:223
  50.7 5.5 %collective-permute-start.3 = (bf16[96,256]{1,0:T(8,128)(2,1)}, bf16[96,256]{1,0:T(8,128)(2,1)S(1)}, u32[]{:S(2)}, u32[]{:S(2)}) collective-permute-start(bf16[96,256]{1,0:T(8,128)(2,1)} %get-tuple-element.20), channel_id=1, source_target_pairs={{0,48},{16,32},{32,16},{48,0},{1,49},{17,33},{33,17},{49,1},{2,50}... | collective-permute-start | bytes 147464 | tf_op jit(solution)/shard_map/ppermute | solution.py:223
  56.2 0.9 copy-start.9
  57.7 7.9 %collective-permute-start.4 = (f32[48,128]{1,0:T(8,128)S(1)}, f32[48,128]{1,0:T(8,128)S(1)}, u32[]{:S(2)}, u32[]{:S(2)}) collective-permute-start(f32[48,128]{1,0:T(8,128)S(1)} %get-tuple-element.22), channel_id=1, source_target_pairs={{0,64},{64,0},{128,192},{192,128},{1,65},{65,1},{129,193},{193,129... | collective-permute-start | bytes 73736 | tf_op jit(solution)/shard_map/ppermute | solution.py:223
  61.1 7.8 %collective-permute-start.5 = (f32[48,128]{1,0:T(8,128)S(1)}, f32[48,128]{1,0:T(8,128)S(1)}, u32[]{:S(2)}, u32[]{:S(2)}) collective-permute-start(f32[48,128]{1,0:T(8,128)S(1)} %get-tuple-element.23), channel_id=1, source_target_pairs={{0,128},{64,192},{128,0},{192,64},{1,129},{65,193},{129,1},{193,65... | collective-permute-start | bytes 73736 | tf_op jit(solution)/shard_map/ppermute | solution.py:223
  65.5 5.9 %collective-permute-start.6 = (f32[48,128]{1,0:T(8,128)S(1)}, f32[48,128]{1,0:T(8,128)S(1)}, u32[]{:S(2)}, u32[]{:S(2)}) collective-permute-start(f32[48,128]{1,0:T(8,128)S(1)} %get-tuple-element.24), channel_id=1, source_target_pairs={{0,192},{64,128},{128,64},{192,0},{1,193},{65,129},{129,65},{193,1... | collective-permute-start | bytes 73736 | tf_op jit(solution)/shard_map/ppermute | solution.py:223
  71.5 6.6 %collective-permute-start.7 = (bf16[1,2,48,128]{3,2,1,0:T(8,128)(2,1)S(1)}, bf16[1,2,48,128]{3,2,1,0:T(8,128)(2,1)S(1)}, u32[]{:S(2)}, u32[]{:S(2)}) collective-permute-start(bf16[1,2,48,128]{3,2,1,0:T(8,128)(2,1)S(1)} %delta_mean.1), channel_id=1, source_target_pairs={{0,64},{64,0},{128,192},{192,128},{1,65},{65,1},{129,193},{193,129... | collective-permute-start | bytes 73736 | tf_op jit(solution)/shard_map/ppermute | solution.py:223
  73.0 7.8 %collective-permute-start.8 = (bf16[1,2,48,128]{3,2,1,0:T(8,128)(2,1)S(1)}, bf16[1,2,48,128]{3,2,1,0:T(8,128)(2,1)S(1)}, u32[]{:S(2)}, u32[]{:S(2)}) collective-permute-start(bf16[1,2,48,128]{3,2,1,0:T(8,128)(2,1)S(1)} %delta_mean.1), channel_id=1, source_target_pairs={{0,128},{64,192},{128,0},{192,64},{1,129},{65,193},{129,1},{193,65... | collective-permute-start | bytes 73736 | tf_op jit(solution)/shard_map/ppermute | solution.py:223
  74.8 6.2 %collective-permute-start.9 = (bf16[1,2,48,128]{3,2,1,0:T(8,128)(2,1)S(1)}, bf16[1,2,48,128]{3,2,1,0:T(8,128)(2,1)S(1)}, u32[]{:S(2)}, u32[]{:S(2)}) collective-permute-start(bf16[1,2,48,128]{3,2,1,0:T(8,128)(2,1)S(1)} %delta_mean.1), channel_id=1, source_target_pairs={{0,192},{64,128},{128,64},{192,0},{1,193},{65,129},{129,65},{193,1... | collective-permute-start | bytes 73736 | tf_op jit(solution)/shard_map/ppermute | solution.py:223
  81.1 4.8 %collective-permute-start.10 = (bf16[4,2,48,128]{3,2,1,0:T(8,128)(2,1)S(1)}, bf16[4,2,48,128]{3,2,1,0:T(8,128)(2,1)S(1)}, u32[]{:S(2)}, u32[]{:S(2)}) collective-permute-start(bf16[4,2,48,128]{3,2,1,0:T(8,128)(2,1)S(1)} %pad_maximum_fusion), channel_id=1, source_target_pairs={{0,16},{16,0},{32,48},{48,32},{1,17},{17,1},{33,49},{49,33},{2,18}... | collective-permute-start | bytes 294920 | tf_op jit(solution)/shard_map/ppermute | solution.py:223
  81.8 7.5 %collective-permute-start.11 = (bf16[4,2,48,128]{3,2,1,0:T(8,128)(2,1)S(1)}, bf16[4,2,48,128]{3,2,1,0:T(8,128)(2,1)S(1)}, u32[]{:S(2)}, u32[]{:S(2)}) collective-permute-start(bf16[4,2,48,128]{3,2,1,0:T(8,128)(2,1)S(1)} %pad_maximum_fusion), channel_id=1, source_target_pairs={{0,32},{16,48},{32,0},{48,16},{1,33},{17,49},{33,1},{49,17},{2,34}... | collective-permute-start | bytes 294920 | tf_op jit(solution)/shard_map/ppermute | solution.py:223
  85.6 5.8 %collective-permute-start.12 = (bf16[4,2,48,128]{3,2,1,0:T(8,128)(2,1)S(1)}, bf16[4,2,48,128]{3,2,1,0:T(8,128)(2,1)S(1)}, u32[]{:S(2)}, u32[]{:S(2)}) collective-permute-start(bf16[4,2,48,128]{3,2,1,0:T(8,128)(2,1)S(1)} %pad_maximum_fusion), channel_id=1, source_target_pairs={{0,48},{16,32},{32,16},{48,0},{1,49},{17,33},{33,17},{49,1},{2,50}... | collective-permute-start | bytes 294920 | tf_op jit(solution)/shard_map/ppermute | solution.py:223
  91.5 1.8 %collective-permute-start.13 = (bf16[16,2,48,128]{3,2,1,0:T(8,128)(2,1)S(1)}, bf16[16,2,48,128]{3,2,1,0:T(8,128)(2,1)S(1)}, u32[]{:S(2)}, u32[]{:S(2)}) collective-permute-start(bf16[16,2,48,128]{3,2,1,0:T(8,128)(2,1)S(1)} %constant_dynamic-update-slice_fusion.a_ref.refs_5_), channel_id=1, source_target_pairs={{0,8},{8,0},{1,9},{9,1},{2,10},{10,2},{3,11},{11,3},{4,12},{12,4},... | collective-permute-start | bytes 1179656 | tf_op jit(solution)/shard_map/ppermute | solution.py:223
  93.5 3.7 %collective-permute-start.14 = (f32[8,128]{1,0:T(8,128)S(1)}, f32[8,128]{1,0:T(8,128)S(1)}, u32[]{:S(2)}, u32[]{:S(2)}) collective-permute-start(f32[8,128]{1,0:T(8,128)S(1)} %delta_squares.1), channel_id=1, source_target_pairs={{0,1},{1,0},{2,3},{3,2},{4,5},{5,4},{6,7},{7,6},{8,9},{9,8},{10,11... | collective-permute-start | bytes 12296 | tf_op jit(solution)/shard_map/ppermute | solution.py:223
  97.2 5.0 %collective-permute-start.15 = (f32[8,128]{1,0:T(8,128)S(1)}, f32[8,128]{1,0:T(8,128)S(1)}, u32[]{:S(2)}, u32[]{:S(2)}) collective-permute-start(f32[8,128]{1,0:T(8,128)S(1)} %add.23.refs_1_), channel_id=1, source_target_pairs={{0,2},{2,0},{4,6},{6,4},{1,3},{3,1},{5,7},{7,5},{8,10},{10,8},{12,... | collective-permute-start | bytes 12296 | tf_op jit(solution)/shard_map/ppermute | solution.py:223
  99.1 5.1 %collective-permute-start.16 = (f32[8,128]{1,0:T(8,128)S(1)}, f32[8,128]{1,0:T(8,128)S(1)}, u32[]{:S(2)}, u32[]{:S(2)}) collective-permute-start(f32[8,128]{1,0:T(8,128)S(1)} %add.23.refs_1_), channel_id=1, source_target_pairs={{0,4},{2,6},{4,0},{6,2},{1,5},{3,7},{5,1},{7,3},{8,12},{10,14},{12... | collective-permute-start | bytes 12296 | tf_op jit(solution)/shard_map/ppermute | solution.py:223
  101.8 4.8 %collective-permute-start.17 = (f32[8,128]{1,0:T(8,128)S(1)}, f32[8,128]{1,0:T(8,128)S(1)}, u32[]{:S(2)}, u32[]{:S(2)}) collective-permute-start(f32[8,128]{1,0:T(8,128)S(1)} %add.23.refs_1_), channel_id=1, source_target_pairs={{0,6},{2,4},{4,2},{6,0},{1,7},{3,5},{5,3},{7,1},{8,14},{10,12},{12... | collective-permute-start | bytes 12296 | tf_op jit(solution)/shard_map/ppermute | solution.py:223

commit v2 on v1

v2 whole, which is shorter than its diff:
```python
import jax
import jax.numpy as jnp
from jax import lax
from jax.experimental import pallas as pl
from jax.experimental.pallas import tpu as pltpu
from jax.sharding import Mesh
from jax.sharding import PartitionSpec as P

f32 = jnp.float32
bf16 = jnp.bfloat16

outer_momentum = 0.9
outer_rate = 0.7
merge_weight = 0.5
clip_epsilon = 1e-06

EXPERTS = 8
REP = ("zh", "y", "c")
SHARD = ("x", "zl")
VMEM_LIMIT = 16 * 1024 * 1024


def params(**more):
    return pltpu.CompilerParams(vmem_limit_bytes=VMEM_LIMIT, **more)


def whole(count):
    return [pl.BlockSpec(memory_space=pltpu.VMEM)] * count


def slots(routes, tokens, capacity):
    ids = lax.broadcasted_iota(jnp.int32, (EXPERTS, tokens), 0)
    named = jnp.logical_or(routes[0:1, :] == ids, routes[1:2, :] == ids)
    before = lax.broadcasted_iota(jnp.int32, (tokens, tokens), 0) < lax.broadcasted_iota(
        jnp.int32, (tokens, tokens), 1
    )
    place = jnp.dot(
        named.astype(f32).astype(bf16), before.astype(f32).astype(bf16), preferred_element_type=f32
    )
    return jnp.where(named, place.astype(jnp.int32), capacity)


def dispatch_kernel(routes_ref, tokens_ref, out_ref):
    tokens = tokens_ref.shape[0]
    capacity = out_ref.shape[1]
    place = slots(routes_ref[...], tokens, capacity)
    row = lax.broadcasted_iota(jnp.int32, (capacity, tokens), 0)
    table = jnp.concatenate(
        [(row == place[e : e + 1, :]).astype(f32) for e in range(EXPERTS)], axis=0
    ).astype(bf16)
    width = 512
    for j in range(tokens_ref.shape[1] // width):
        cols = pl.ds(j * width, width)
        part = jnp.dot(table, tokens_ref[:, cols], preferred_element_type=f32).astype(bf16)
        out_ref[:, :, cols] = part.reshape(EXPERTS, capacity, width)


def combine_table_kernel(routes_ref, weight_ref, high_ref, low_ref):
    tokens = routes_ref.shape[1]
    capacity = high_ref.shape[1] // EXPERTS
    routes = routes_ref[...]
    place = slots(routes, tokens, capacity)
    row = lax.broadcasted_iota(jnp.int32, (capacity, tokens), 0)
    parts = []
    for e in range(EXPERTS):
        weight = jnp.where(routes[0:1, :] == e, weight_ref[0:1, :], weight_ref[1:2, :])
        parts.append(jnp.where(row == place[e : e + 1, :], weight, 0.0))
    table = jnp.concatenate(parts, axis=0).T
    high = table.astype(bf16)
    high_ref[...] = high
    low_ref[...] = (table - high.astype(f32)).astype(bf16)


def combine_kernel(high_ref, low_ref, rows_ref, out_ref):
    width = 512
    for j in range(out_ref.shape[1] // width):
        cols = pl.ds(j * width, width)
        rows = rows_ref[:, cols]
        out_ref[:, cols] = (
            jnp.dot(high_ref[...], rows, preferred_element_type=f32)
            + jnp.dot(low_ref[...], rows, preferred_element_type=f32)
        ).astype(bf16)


def ffn_kernel(
    x_hbm, gate_hbm, up_hbm, down_hbm, out_hbm, x_ref, gate_ref, up_ref, down_ref, hidden_ref, out_ref, sems
):
    block, wide = 256, 512
    count, last = hidden_ref.shape[1] // block, out_ref.shape[1] // wide
    copies = [pltpu.make_async_copy(x_hbm, x_ref, sems.at[0])]
    for i in range(count):
        cols = pl.ds(i * block, block)
        for hbm, ref in ((gate_hbm, gate_ref), (up_hbm, up_ref)):
            copies.append(
                pltpu.make_async_copy(hbm.at[0, :, cols], ref.at[:, cols], sems.at[len(copies)])
            )
    for i in range(last):
        cols = pl.ds(i * wide, wide)
        copies.append(
            pltpu.make_async_copy(down_hbm.at[0, :, cols], down_ref.at[:, cols], sems.at[len(copies)])
        )
    for copy in copies:
        copy.start()
    copies[0].wait()
    for i in range(count):
        cols = pl.ds(i * block, block)
        copies[2 * i + 1].wait()
        gate = jnp.dot(x_ref[...], gate_ref[:, cols], preferred_element_type=f32)
        copies[2 * i + 2].wait()
        up = jnp.dot(x_ref[...], up_ref[:, cols], preferred_element_type=f32)
        hidden_ref[:, cols] = (gate / (1.0 + jnp.exp(-gate)) * up).astype(bf16)
    results = []
    for i in range(last):
        cols = pl.ds(i * wide, wide)
        copies[2 * count + 1 + i].wait()
        out_ref[:, cols] = jnp.dot(
            hidden_ref[...], down_ref[:, cols], preferred_element_type=f32
        ).astype(bf16)
        results.append(
            pltpu.make_async_copy(out_ref.at[:, cols], out_hbm.at[:, cols], sems.at[len(copies) + i])
        )
        results[-1].start()
    for copy in results:
        copy.wait()


def ffn(x, w_gate, w_up, w_down):
    rows, width = x.shape
    hidden = w_gate.shape[2]
    anywhere = pl.BlockSpec(memory_space=pl.ANY)
    return pl.pallas_call(
        ffn_kernel,
        in_specs=[anywhere] * 4,
        out_specs=anywhere,
        out_shape=jax.ShapeDtypeStruct((rows, width), bf16),
        scratch_shapes=[
            pltpu.VMEM((rows, width), bf16),
            pltpu.VMEM((width, hidden), bf16),
            pltpu.VMEM((width, hidden), bf16),
            pltpu.VMEM((hidden, width), bf16),
            pltpu.VMEM((rows, hidden), bf16),
            pltpu.VMEM((rows, width), bf16),
            pltpu.SemaphoreType.DMA((1 + hidden // 128 + width // 256,)),
        ],
        compiler_params=pltpu.CompilerParams(vmem_limit_bytes=58 * 1024 * 1024),
        cost_estimate=pl.CostEstimate(
            flops=6 * rows * width * hidden,
            bytes_accessed=6 * width * hidden + 4 * rows * width,
            transcendentals=rows * hidden,
        ),
        name="expert_ffn",
    )(x, w_gate, w_up, w_down)


def halve_first_kernel(at_ref, own_ref, got_ref, keep_ref, send_ref):
    core, bit = at_ref[0], at_ref[1]
    half, width = got_ref.shape[1], keep_ref.shape[1]
    for ref, which in ((send_ref, 1 - bit), (keep_ref, bit)):
        mine = own_ref[0, :, pl.ds(pl.multiple_of(core * half + which * width, width), width)]
        other = got_ref[:, pl.ds(pl.multiple_of(which * width, width), width)]
        ref[...] = (mine + other).astype(ref.dtype)


def halve_kernel(at_ref, own_ref, got_ref, keep_ref, send_ref):
    bit, width = at_ref[2], keep_ref.shape[1]
    for ref, which in ((send_ref, 1 - bit), (keep_ref, bit)):
        cols = pl.ds(pl.multiple_of(which * width, width), width)
        ref[...] = (own_ref[:, cols] + got_ref[:, cols].astype(f32)).astype(ref.dtype)


def add_z_first_kernel(own_ref, got_ref, mom_ref, keep_ref, send_ref):
    rows = send_ref.shape[1]
    total = own_ref[...] + got_ref[...].astype(f32)
    for p in range(4):
        keep_ref[p] = total[(p & 1) * rows : (p & 1) * rows + rows, (p >> 1) * 128 : (p >> 1) * 128 + 128]
    send_ref[0:4] = keep_ref[...].astype(bf16)
    send_ref[4] = mom_ref[...].astype(bf16)


def add_z_kernel(own_ref, sent_ref, got_ref, keep_ref, send_ref):
    total = own_ref[...] + got_ref[0:4].astype(f32)
    keep_ref[...] = total
    send_ref[0:4] = total.astype(bf16)
    send_ref[4] = sent_ref[4]
    send_ref[5] = got_ref[4]


def mean_kernel(replicas, own_ref, sent_ref, got_ref, out_ref):
    total = own_ref[...] + got_ref[0:4].astype(f32)
    out_ref[0, 0:4] = (total * (1.0 / replicas)).astype(bf16)
    out_ref[0, 4:6] = sent_ref[4:6]
    out_ref[0, 6:8] = got_ref[4:6]


def square_kernel(a_ref, b_ref, out_ref):
    total = jnp.zeros(out_ref.shape, f32)
    step = out_ref.shape[0]
    for ref in (a_ref, b_ref):
        for j in range(4):
            for k in range(4):
                block = ref[j, k].astype(f32)
                block = block * block
                for i in range(block.shape[0] // step):
                    total += block[i * step : i * step + step]
    out_ref[...] = total


def quarter_of(y):
    return ((y & 1) ^ (y >> 1)) * 2 + (y >> 1)


def outer_kernel(entries, at_ref, near_s, far_s, near_ref, far_ref, params_ref, local_ref, mom_ref, next_ref, mom_out, scratch):
    core, quarter, zh, rep = at_ref[0], at_ref[3], at_ref[4], at_ref[5]
    squares = near_s[...] + far_s[...]
    squares = jnp.sum(jnp.sum(squares, axis=1, keepdims=True), axis=0, keepdims=True)
    clip = jnp.minimum(1.0, lax.rsqrt(squares * (1.0 / entries) + clip_epsilon))

    def delta(side, piece, slot):
        j = jnp.bitwise_xor(piece, quarter)
        return jnp.where(
            core == side, near_ref[j, slot].astype(f32), far_ref[j, slot].astype(f32)
        )

    for cb in range(16):
        j = jnp.bitwise_xor(quarter_of(cb & 3), quarter)
        apart = jnp.bitwise_xor(zh, cb >> 2)
        high = jnp.right_shift(apart, 1)
        slot = 4 + high * 2 + jnp.bitwise_xor(jnp.bitwise_and(apart, 1), high)
        near, far = near_ref[j, slot].astype(f32), far_ref[j, slot].astype(f32)
        m0, m1 = jnp.where(core == 0, near, far), jnp.where(core == 0, far, near)
        for h in range(2):
            rows, cols = pl.ds(h * 48, 48), pl.ds(cb * 128, 128)
            mom = jnp.concatenate([m0[:, h * 64 : h * 64 + 64], m1[:, h * 64 : h * 64 + 64]], axis=1)
            clipped = clip * delta(cb >> 3, (cb >> 1) & 3, (cb & 1) * 2 + h)
            after = outer_momentum * mom + clipped
            outer = params_ref[rows, cols] - outer_rate * (outer_momentum * after + clipped)
            local = local_ref[0, rows, cols].astype(f32)
            next_ref[0, rows, cols] = (merge_weight * local + (1.0 - merge_weight) * outer).astype(bf16)
    cb = jnp.right_shift(rep, 1)
    side, piece = jnp.right_shift(cb, 3), jnp.bitwise_and(jnp.right_shift(cb, 1), 3)
    scratch[...] = jnp.zeros_like(scratch)
    for h in range(2):
        scratch[h * 48 : h * 48 + 48, :] = delta(side, piece, jnp.bitwise_and(cb, 1) * 2 + h)
    scratch[...] = scratch[...].T
    start = pl.multiple_of(core * 64, 64)
    mom_out[...] = outer_momentum * mom_ref[...] + clip * scratch[pl.ds(start, 64), 0:96]


def smem():
    return pl.BlockSpec(memory_space=pltpu.SMEM)


def swap(value, axis, bits):
    size = lax.axis_size(axis)
    return lax.ppermute(value, axis, [(i, i ^ bits) for i in range(size)])


def outer_sum(pseudo_grad, momentum):
    rows, width = pseudo_grad.shape[1:]
    core, y, zh = lax.axis_index("c"), lax.axis_index("y"), lax.axis_index("zh")
    rep = (zh * 4 + y) * 2 + core
    first, second = (y & 1) ^ (y >> 1), y >> 1
    at = jnp.stack([core, first, second, first * 2 + second, zh, rep]).astype(jnp.int32)
    half = width // 2
    got = swap(lax.dynamic_slice_in_dim(pseudo_grad[0], (1 - core) * half, half, 1), "c", 1)
    keep, send = pl.pallas_call(
        halve_first_kernel,
        in_specs=[smem()] + whole(2),
        out_specs=whole(2),
        out_shape=[jax.ShapeDtypeStruct((rows, half // 2), t) for t in (f32, bf16)],
        compiler_params=params(),
        name="delta_halve_first",
    )(at, pseudo_grad, got)
    got = swap(send, "y", 1)
    keep, send = pl.pallas_call(
        halve_kernel,
        in_specs=[smem()] + whole(2),
        out_specs=whole(2),
        out_shape=[jax.ShapeDtypeStruct((rows, half // 4), t) for t in (f32, bf16)],
        compiler_params=params(),
        name="delta_halve",
    )(at, keep, got)
    got = swap(send, "y", 3)
    part = (rows // 2, half // 8)
    mom_block = jnp.concatenate([momentum[: rows // 2], momentum[rows // 2 :]], axis=1)
    keep, send = pl.pallas_call(
        add_z_first_kernel,
        in_specs=whole(3),
        out_specs=whole(2),
        out_shape=[jax.ShapeDtypeStruct((4,) + part, f32), jax.ShapeDtypeStruct((5,) + part, bf16)],
        compiler_params=params(),
        name="delta_add_z_first",
    )(keep, got, mom_block)
    got = swap(send, "zh", 1)
    keep, send = pl.pallas_call(
        add_z_kernel,
        in_specs=whole(3),
        out_specs=whole(2),
        out_shape=[jax.ShapeDtypeStruct((4,) + part, f32), jax.ShapeDtypeStruct((6,) + part, bf16)],
        compiler_params=params(),
        name="delta_add_z",
    )(keep, send, got)
    got = swap(send, "zh", 3)
    block = pl.pallas_call(
        lambda *refs: mean_kernel(32, *refs),
        in_specs=whole(3),
        out_specs=whole(1)[0],
        out_shape=jax.ShapeDtypeStruct((1, 8) + part, bf16),
        compiler_params=params(),
        name="delta_mean",
    )(keep, send, got)
    return at, block


def outer_finish(at, block, global_params, momentum, local_params):
    rows, width = global_params.shape
    block = jnp.concatenate([block, swap(block, "y", 3)], axis=0)
    block = jnp.concatenate([block, swap(block, "y", 1)], axis=0)
    far = swap(block, "c", 1)
    squares = pl.pallas_call(
        square_kernel,
        in_specs=whole(2),
        out_specs=whole(1)[0],
        out_shape=jax.ShapeDtypeStruct((8, 128), f32),
        compiler_params=params(),
        name="delta_squares",
    )(block, far)
    squares = squares + swap(squares, "zl", 1)
    squares = squares + swap(squares, "x", 1)
    entries = float(rows * 8 * width)
    local_next, momentum_next = pl.pallas_call(
        lambda *refs: outer_kernel(entries, *refs),
        in_specs=[smem()] + whole(7),
        out_specs=whole(2),
        out_shape=[
            jax.ShapeDtypeStruct((1, rows, width), bf16),
            jax.ShapeDtypeStruct((momentum.shape[1], rows), f32),
        ],
        scratch_shapes=[pltpu.VMEM((128, 128), f32)],
        compiler_params=params(),
        name="outer_update",
    )(at, squares, swap(squares, "x", 3), block, far, global_params, local_params, momentum.T)
    return momentum_next.T, local_next


def local(
    tokens, routes, route_weight, w_gate, w_up, w_down, pseudo_grad, global_params, momentum, local_params
):
    tok_rows, feat_width = tokens.shape
    capacity = tok_rows * 3 // 8
    routes_t, weight_t = routes.T, route_weight.T
    outgoing = pl.pallas_call(
        dispatch_kernel,
        in_specs=whole(2),
        out_specs=whole(1)[0],
        out_shape=jax.ShapeDtypeStruct((EXPERTS, capacity, feat_width), bf16),
        compiler_params=params(),
        name="dispatch",
    )(routes_t, tokens)
    high, low = pl.pallas_call(
        combine_table_kernel,
        in_specs=whole(2),
        out_specs=whole(2),
        out_shape=[jax.ShapeDtypeStruct((tok_rows, EXPERTS * capacity), bf16)] * 2,
        compiler_params=params(),
        name="combine_table",
    )(routes_t, weight_t)
    at, block = outer_sum(pseudo_grad, momentum)
    received = lax.all_to_all(outgoing, SHARD, split_axis=0, concat_axis=0, tiled=True)
    received, block = lax.optimization_barrier((received, block))
    result = ffn(received.reshape(EXPERTS * capacity, feat_width), w_gate, w_up, w_down)
    result = result.reshape(EXPERTS, capacity, feat_width)
    returned = lax.all_to_all(result, SHARD, split_axis=0, concat_axis=0, tiled=True)
    moe_out = pl.pallas_call(
        combine_kernel,
        in_specs=whole(3),
        out_specs=whole(1)[0],
        out_shape=jax.ShapeDtypeStruct((tok_rows, feat_width), bf16),
        compiler_params=params(),
        name="combine",
    )(high, low, returned.reshape(EXPERTS * capacity, feat_width))
    momentum_next, local_next = outer_finish(at, block, global_params, momentum, local_params)
    return (moe_out, momentum_next, local_next)


def solution(mesh):
    fine = Mesh(mesh.devices.reshape(4, 4, 2, 4, 2), REP + SHARD)
    in_specs = (
        P(REP + SHARD, None),
        P(REP + SHARD, None),
        P(REP + SHARD, None),
        P(SHARD, None, None),
        P(SHARD, None, None),
        P(SHARD, None, None),
        P(REP, SHARD, None),
        P(SHARD, None),
        P(SHARD, REP),
        P(REP, SHARD, None),
    )
    out_specs = (P(REP + SHARD, None), P(SHARD, REP), P(REP, SHARD, None))
    return jax.shard_map(local, mesh=fine, in_specs=in_specs, out_specs=out_specs, check_vma=False)
```

time: 110 us -> 86.1 us (0.78)
  blocking collectives: 27 us -> 0 us
  waiting for transfers between devices: 25.2 us -> 33.7 us
  local copies, waits for them, and re-layouts: 7.43 us -> 3.32 us
  starting transfers between devices: 34.5 us -> 30.4 us
  Pallas kernels: 14.9 us -> 17.2 us
    all_to_all x1 -> x0, blocking collectives: 27 us -> none  [local(): lax.all_to_all(outgoing, SHARD, split_axis=0, concat_axis=0, tiled=True)]
    ppermute x18 -> x11, starting transfers between devices: 30.8 us -> 18.6 us  [swap(): return lax.ppermute(value, axis, [(i, i ^ bits) for i in range(size)])]
    ppermute x18 -> x11, waiting for transfers between devices: 25.2 us -> 33.7 us  [swap(): return lax.ppermute(value, axis, [(i, i ^ bits) for i in range(size)])]
    all_to_all x0 -> x1, starting transfers between devices: none -> 5.79 us  [local(): lax.all_to_all(outgoing, SHARD, split_axis=0, concat_axis=0, tiled=True)]
    unnamed x34 -> x22, local copies, waits for them, and re-layouts: 6.39 us -> 3.11 us
    all_to_all x1, starting transfers between devices: 3.71 us -> 6.04 us  [local(): lax.all_to_all(result, SHARD, split_axis=0, concat_axis=0, tiled=True)]
    pallas_call x1, Pallas kernels: 0.68 us -> 1.88 us  [local(): pl.pallas_call(dispatch_kernel, in_specs=whole(2), out_specs=whole(1)[0],...]
    pallas_call x6 -> x8, Pallas kernels: 12.5 us -> 13.5 us  [the longest x1 10.3 us: ffn(): pl.pallas_call(ffn_kernel, in_specs=[anywhere] * 4, out_specs=anywhere, o...]
  transfers between devices with their start and end apart: 19 -> 13, of which waited for: 13 -> 11; matrix products, arithmetic and copies ran while one was open for 1% -> 1% of each run, Pallas kernels for 4% -> 4%
where the time goes in v2:
time: 86.1 us; the launch traced here: 85.7 us
  waiting for transfers between devices  33.7 us (39%)
  starting transfers between devices  30.4 us (35%)
  Pallas kernels  17.2 us (20%)
  local copies, waits for them, and re-layouts  3.32 us (4%)
    ppermute x11, waiting for transfers between devices, swap(): return lax.ppermute(value, axis, [(i, i ^ bits) for i in range(size)])  33.7 us
    ppermute x11, starting transfers between devices, swap(): return lax.ppermute(value, axis, [(i, i ^ bits) for i in range(size)])  18.6 us
    pallas_call x1, Pallas kernels, ffn(): pl.pallas_call(ffn_kernel, in_specs=[anywhere] * 4, out_specs=anywhere, o...  10.3 us
    all_to_all x1, starting transfers between devices, local(): lax.all_to_all(result, SHARD, split_axis=0, concat_axis=0, tiled=True)  6.04 us
    all_to_all x1, starting transfers between devices, local(): lax.all_to_all(outgoing, SHARD, split_axis=0, concat_axis=0, tiled=True)  5.79 us
    unnamed x22, local copies, waits for them, and re-layouts  3.11 us
    pallas_call x1, Pallas kernels, local(): pl.pallas_call(dispatch_kernel, in_specs=whole(2), out_specs=whole(1)[0],...  1.88 us
    pallas_call x1, Pallas kernels, outer_finish(): pl.pallas_call(lambda *refs: outer_kernel(entries, *refs), in_specs=[smem...  1.85 us
  transfers between devices with their start and end apart: 13, of which 11 were waited for; matrix products, arithmetic and copies ran while one was open for 1% of the time, Pallas kernels for 4%

profile of v2, /device:TPU:24, one launch (start us, length us, event | category | flops | bytes accessed | tf_op | source)
XLA Modules:
  0.0 85.7 jit_solution(15094149037004374979)
XLA Ops:
  0.6 0.0 copy-start.2
  0.6 1.0 %copy-done.2 = bf16[128,2048]{1,0:T(8,128)(2,1)S(1)} copy-done((bf16[128,2048]{1,0:T(8,128)(2,1)S(1)}, bf16[128,2048]{1,0:T(8,128)(2,1)}, u32[]{:S(2)}) %copy-start.2) | copy-done | bytes 524312
  1.7 0.0 copy-start.5
  1.7 0.7 copy-done.5
  2.4 1.9 %dispatch.1 = bf16[8,48,2048]{2,1,0:T(8,128)(2,1)} custom-call(s32[2,128]{1,0:T(2,128)S(1)} %bitcast.17, bf16[128,2048]{1,0:T(8,128)(2,1)S(1)} %copy-done.2), custom_call_target="tpu_custom_call" | custom-call | tf_op jit(solution)/shard_map/dispatch/pallas_call | solution.py:352
  4.2 0.0 copy-start
  4.2 5.8 %all-to-all-start = ((bf16[8,48,2048]{2,1,0:T(8,128)(2,1)}), bf16[8,48,2048]{2,1,0:T(8,128)(2,1)S(1)}, u32[]{:S(2)}, u32[]{:S(2)}) async-start(bf16[8,48,2048]{2,1,0:T(8,128)(2,1)} %dispatch.1), calls=%async_computation | async-start | bytes 3145728 | tf_op jit(solution)/shard_map/all_to_all | solution.py:369
  10.0 0.0 copy-start.4
  10.0 0.0 copy-done
  10.1 0.1 collective-permute-start
  10.2 0.1 stack.27.at_ref.refs_0_
  10.3 1.6 %collective-permute-done.got_ref = f32[96,1024]{1,0:T(8,128)S(1)} collective-permute-done((f32[96,1024]{1,0:T(8,128)S(1)}, f32[96,1024]{1,0:T(8,128)S(1)}, u32[]{:S(2)}, u32[]{:S(2)}) %collective-permute-start) | collective-permute-done | bytes 393248 | tf_op jit(solution)/shard_map/ppermute | solution.py:255
  11.9 0.6 delta_halve_first.1
  12.5 0.8 collective-permute-start.1
  13.3 0.0 copy-done.4
  13.3 0.1 fusion
  13.4 0.1 copy.15
  13.5 0.1 copy.16
  13.5 3.9 %collective-permute-done.1.got_ref = bf16[96,512]{1,0:T(8,128)(2,1)S(1)} collective-permute-done((bf16[96,512]{1,0:T(8,128)(2,1)S(1)}, bf16[96,512]{1,0:T(8,128)(2,1)S(1)}, u32[]{:S(2)}, u32[]{:S(2)}) %collective-permute-start.1) | collective-permute-done | bytes 98336 | tf_op jit(solution)/shard_map/ppermute | solution.py:255
  17.4 0.6 delta_halve.1
  18.0 0.3 collective-permute-start.2
  18.3 0.1 pad_maximum_fusion.1.mom_ref
  18.4 5.0 %collective-permute-done.2.got_ref = bf16[96,256]{1,0:T(8,128)(2,1)S(1)} collective-permute-done((bf16[96,256]{1,0:T(8,128)(2,1)S(1)}, bf16[96,256]{1,0:T(8,128)(2,1)S(1)}, u32[]{:S(2)}, u32[]{:S(2)}) %collective-permute-start.2) | collective-permute-done | bytes 49184 | tf_op jit(solution)/shard_map/ppermute | solution.py:255
  23.4 3.4 %collective-permute-start.3 = (bf16[5,48,128]{2,1,0:T(8,128)(2,1)S(1)}, bf16[5,48,128]{2,1,0:T(8,128)(2,1)S(1)}, u32[]{:S(2)}, u32[]{:S(2)}) collective-permute-start(bf16[5,48,128]{2,1,0:T(8,128)(2,1)S(1)} %get-tuple-element.24.sent_ref), channel_id=1, source_target_pairs={{0,64},{64,0},{128,192},{192,128},{1,65},{65,1},{129,193},{193,129... | collective-permute-start | bytes 184328 | tf_op jit(solution)/shard_map/ppermute | solution.py:255
  26.8 2.3 %collective-permute-done.3.got_ref = bf16[5,48,128]{2,1,0:T(8,128)(2,1)S(1)} collective-permute-done((bf16[5,48,128]{2,1,0:T(8,128)(2,1)S(1)}, bf16[5,48,128]{2,1,0:T(8,128)(2,1)S(1)}, u32[]{:S(2)}, u32[]{:S(2)}) %collective-permute-start.3) | collective-permute-done | bytes 61472 | tf_op jit(solution)/shard_map/ppermute | solution.py:255
  29.1 6.8 %collective-permute-start.4 = (bf16[6,48,128]{2,1,0:T(8,128)(2,1)S(1)}, bf16[6,48,128]{2,1,0:T(8,128)(2,1)S(1)}, u32[]{:S(2)}, u32[]{:S(2)}) collective-permute-start(bf16[6,48,128]{2,1,0:T(8,128)(2,1)S(1)} %get-tuple-element.26.refs_1_), channel_id=1, source_target_pairs={{0,192},{64,128},{128,64},{192,0},{1,193},{65,129},{129,65},{193,1... | collective-permute-start | bytes 221192 | tf_op jit(solution)/shard_map/ppermute | solution.py:255
  35.8 2.7 %collective-permute-done.4.refs_2_ = bf16[6,48,128]{2,1,0:T(8,128)(2,1)S(1)} collective-permute-done((bf16[6,48,128]{2,1,0:T(8,128)(2,1)S(1)}, bf16[6,48,128]{2,1,0:T(8,128)(2,1)S(1)}, u32[]{:S(2)}, u32[]{:S(2)}) %collective-permute-start.4) | collective-permute-done | bytes 73760 | tf_op jit(solution)/shard_map/ppermute | solution.py:255
  38.6 0.0 all-to-all-done
  38.6 0.0 copy-start.8
  38.6 1.2 %copy-done.8 = bf16[8,48,2048]{2,1,0:T(8,128)(2,1)} copy-done((bf16[8,48,2048]{2,1,0:T(8,128)(2,1)}, bf16[8,48,2048]{2,1,0:T(8,128)(2,1)S(1)}, u32[]{:S(2)}) %copy-start.8) | copy-done | bytes 1572888
  39.8 10.3 %expert_ffn.1 = bf16[384,2048]{1,0:T(8,128)(2,1)} custom-call(bf16[384,2048]{1,0:T(8,128)(2,1)} %bitcast.20, bf16[1,2048,768]{2,1,0:T(8,128)(2,1)} %gate_hbm.1, bf16[1,2048,768]{2,1,0:T(8,128)(2,1)} %up_hbm.1, bf16[1,768,2048]{2,1,0:T(8,128)(2,1)} %down_hbm.1), custom_call_target="tpu_custom_call" | custom-call | flops 3623878656 | bytes 12582912 | tf_op jit(solution)/shard_map/expert_ffn/pallas_call | solution.py:131
  50.1 6.0 %all-to-all-start.1 = ((bf16[8,48,2048]{2,1,0:T(8,128)(2,1)}), bf16[8,48,2048]{2,1,0:T(8,128)(2,1)S(1)}, u32[]{:S(2)}, u32[]{:S(2)}) async-start(bf16[8,48,2048]{2,1,0:T(8,128)(2,1)} %bitcast.21), calls=%async_computation.1 | async-start | bytes 3145728 | tf_op jit(solution)/shard_map/all_to_all | solution.py:373
  56.1 0.0 copy-start.6
  56.1 0.0 copy-start.7
  56.1 0.0 copy-start.1
  56.1 0.0 copy-start.3
  56.1 0.3 collective-permute-start.5
  56.4 5.6 %collective-permute-done.5 = bf16[1,8,48,128]{3,2,1,0:T(8,128)(2,1)S(1)} collective-permute-done((bf16[1,8,48,128]{3,2,1,0:T(8,128)(2,1)S(1)}, bf16[1,8,48,128]{3,2,1,0:T(8,128)(2,1)S(1)}, u32[]{:S(2)}, u32[]{:S(2)}) %collective-permute-start.5) | collective-permute-done | bytes 98336 | tf_op jit(solution)/shard_map/ppermute | solution.py:255
  62.1 0.1 collective-permute-start.6
  62.2 5.6 %collective-permute-done.6 = bf16[2,8,48,128]{3,2,1,0:T(8,128)(2,1)S(1)} collective-permute-done((bf16[2,8,48,128]{3,2,1,0:T(8,128)(2,1)S(1)}, bf16[2,8,48,128]{3,2,1,0:T(8,128)(2,1)S(1)}, u32[]{:S(2)}, u32[]{:S(2)}) %collective-permute-start.6) | collective-permute-done | bytes 196640 | tf_op jit(solution)/shard_map/ppermute | solution.py:255
  67.9 0.1 collective-permute-start.7
  68.0 1.7 %collective-permute-done.7.b_ref.refs_4_ = bf16[4,8,48,128]{3,2,1,0:T(8,128)(2,1)S(1)} collective-permute-done((bf16[4,8,48,128]{3,2,1,0:T(8,128)(2,1)S(1)}, bf16[4,8,48,128]{3,2,1,0:T(8,128)(2,1)S(1)}, u32[]{:S(2)}, u32[]{:S(2)}) %collective-permute-start.7) | collective-permute-done | bytes 393248 | tf_op jit(solution)/shard_map/ppermute | solution.py:255
  69.7 0.2 delta_squares.1
  69.9 2.1 %collective-permute-start.8 = (f32[8,128]{1,0:T(8,128)S(1)}, f32[8,128]{1,0:T(8,128)S(1)}, u32[]{:S(2)}, u32[]{:S(2)}) collective-permute-start(f32[8,128]{1,0:T(8,128)S(1)} %delta_squares.1), channel_id=1, source_target_pairs={{0,1},{1,0},{2,3},{3,2},{4,5},{5,4},{6,7},{7,6},{8,9},{9,8},{10,11... | collective-permute-start | bytes 12296 | tf_op jit(solution)/shard_map/ppermute | solution.py:255
  72.0 1.9 %collective-permute-done.8 = f32[8,128]{1,0:T(8,128)S(1)} collective-permute-done((f32[8,128]{1,0:T(8,128)S(1)}, f32[8,128]{1,0:T(8,128)S(1)}, u32[]{:S(2)}, u32[]{:S(2)}) %collective-permute-start.8) | collective-permute-done | bytes 4128 | tf_op jit(solution)/shard_map/ppermute | solution.py:255
  73.8 1.7 %collective-permute-start.9 = (f32[8,128]{1,0:T(8,128)S(1)}, f32[8,128]{1,0:T(8,128)S(1)}, u32[]{:S(2)}, u32[]{:S(2)}) collective-permute-start(f32[8,128]{1,0:T(8,128)S(1)} %add.22), channel_id=1, source_target_pairs={{0,2},{2,0},{4,6},{6,4},{1,3},{3,1},{5,7},{7,5},{8,10},{10,8},{12,... | collective-permute-start | bytes 12296 | tf_op jit(solution)/shard_map/ppermute | solution.py:255
  75.6 1.9 %collective-permute-done.9 = f32[8,128]{1,0:T(8,128)S(1)} collective-permute-done((f32[8,128]{1,0:T(8,128)S(1)}, f32[8,128]{1,0:T(8,128)S(1)}, u32[]{:S(2)}, u32[]{:S(2)}) %collective-permute-start.9) | collective-permute-done | bytes 4128 | tf_op jit(solution)/shard_map/ppermute | solution.py:255
  77.4 3.0 %collective-permute-start.10 = (f32[8,128]{1,0:T(8,128)S(1)}, f32[8,128]{1,0:T(8,128)S(1)}, u32[]{:S(2)}, u32[]{:S(2)}) collective-permute-start(f32[8,128]{1,0:T(8,128)S(1)} %add.23.refs_1_), channel_id=1, source_target_pairs={{0,6},{2,4},{4,2},{6,0},{1,7},{3,5},{5,3},{7,1},{8,14},{10,12},{12... | collective-permute-start | bytes 12296 | tf_op jit(solution)/shard_map/ppermute | solution.py:255
  80.4 0.0 copy-done.6
  80.4 0.0 copy-done.7
  80.4 0.3 combine_table.1
  80.7 1.6 %collective-permute-done.10.refs_2_ = f32[8,128]{1,0:T(8,128)S(1)} collective-permute-done((f32[8,128]{1,0:T(8,128)S(1)}, f32[8,128]{1,0:T(8,128)S(1)}, u32[]{:S(2)}, u32[]{:S(2)}) %collective-permute-start.10) | collective-permute-done | bytes 4128 | tf_op jit(solution)/shard_map/ppermute | solution.py:255
  82.3 0.0 copy-done.1
  82.3 0.0 copy-done.3
  82.3 1.8 %outer_update.1 = (bf16[1,96,2048]{2,1,0:T(8,128)(2,1)}, f32[64,96]{1,0:T(8,128)}) custom-call(s32[6]{0:T(128)S(1)} %stack.27.at_ref.refs_0_, f32[8,128]{1,0:T(8,128)S(1)} %add.23.refs_1_, f32[8,128]{1,0:T(8,128)S(1)} %collective-permute-done.10.refs_2_, bf16[4,8,48,128]{3,2,1,0:T(8,128)(2,1)S(1)} %constant_dynamic-update-slice_fusion.a_ref.refs_3_, ...), custom_call_target="tpu_custom_call" | custom-call | tf_op jit(solution)/shard_map/outer_update/pallas_call | solution.py:331
  84.1 0.0 all-to-all-done.1
  84.1 1.5 %combine.1 = bf16[128,2048]{1,0:T(8,128)(2,1)} custom-call(bf16[128,384]{1,0:T(8,128)(2,1)S(1)} %get-tuple-element.17.high_ref, bf16[128,384]{1,0:T(8,128)(2,1)S(1)} %get-tuple-element.18.low_ref, bf16[384,2048]{1,0:T(8,128)(2,1)S(1)} %bitcast.15), custom_call_target="tpu_custom_call" | custom-call | tf_op jit(solution)/shard_map/combine/pallas_call | solution.py:374
  (10 shorter events, 0.2 us)
Async XLA Ops:
  0.6 1.0 %copy-start.2 = (bf16[128,2048]{1,0:T(8,128)(2,1)S(1)}, bf16[128,2048]{1,0:T(8,128)(2,1)}, u32[]{:S(2)}) copy-start(bf16[128,2048]{1,0:T(8,128)(2,1)} %tokens_ref.1) | copy-start | bytes 1572868
  1.7 0.7 copy-start.5
  4.2 5.8 %copy-start = (f32[1,96,2048]{2,1,0:T(8,128)S(1)}, f32[1,96,2048]{2,1,0:T(8,128)}, u32[]{:S(2)}) copy-start(f32[1,96,2048]{2,1,0:T(8,128)} %own_ref.1) | copy-start | bytes 2359300
  4.2 34.3 %all-to-all-start = ((bf16[8,48,2048]{2,1,0:T(8,128)(2,1)}), bf16[8,48,2048]{2,1,0:T(8,128)(2,1)S(1)}, u32[]{:S(2)}, u32[]{:S(2)}) async-start(bf16[8,48,2048]{2,1,0:T(8,128)(2,1)} %dispatch.1), calls=%async_computation | async-start | bytes 3145728 | tf_op jit(solution)/shard_map/all_to_all | solution.py:369
  10.0 3.3 %copy-start.4 = (f32[96,64]{0,1:T(8,128)S(1)}, f32[96,64]{0,1:T(8,128)}, u32[]{:S(2)}) copy-start(f32[96,64]{0,1:T(8,128)} %param.18) | copy-start | bytes 73732
  10.1 1.8 %collective-permute-start = (f32[96,1024]{1,0:T(8,128)S(1)}, f32[96,1024]{1,0:T(8,128)S(1)}, u32[]{:S(2)}, u32[]{:S(2)}) collective-permute-start(f32[96,1024]{1,0:T(8,128)S(1)} %dynamic-slice_bitcast_fusion), channel_id=1, source_target_pairs={{0,8},{8,0},{1,9},{9,1},{2,10},{10,2},{3,11},{11,3},{4,12},{12,4},... | collective-permute-start | bytes 1179656 | tf_op jit(solution)/shard_map/ppermute | solution.py:255
  12.5 4.9 %collective-permute-start.1 = (bf16[96,512]{1,0:T(8,128)(2,1)S(1)}, bf16[96,512]{1,0:T(8,128)(2,1)S(1)}, u32[]{:S(2)}, u32[]{:S(2)}) collective-permute-start(bf16[96,512]{1,0:T(8,128)(2,1)S(1)} %get-tuple-element.20), channel_id=1, source_target_pairs={{0,16},{16,0},{32,48},{48,32},{1,17},{17,1},{33,49},{49,33},{2,18}... | collective-permute-start | bytes 294920 | tf_op jit(solution)/shard_map/ppermute | solution.py:255
  18.0 5.4 %collective-permute-start.2 = (bf16[96,256]{1,0:T(8,128)(2,1)S(1)}, bf16[96,256]{1,0:T(8,128)(2,1)S(1)}, u32[]{:S(2)}, u32[]{:S(2)}) collective-permute-start(bf16[96,256]{1,0:T(8,128)(2,1)S(1)} %get-tuple-element.22), channel_id=1, source_target_pairs={{0,48},{16,32},{32,16},{48,0},{1,49},{17,33},{33,17},{49,1},{2,50}... | collective-permute-start | bytes 147464 | tf_op jit(solution)/shard_map/ppermute | solution.py:255
  23.4 5.7 %collective-permute-start.3 = (bf16[5,48,128]{2,1,0:T(8,128)(2,1)S(1)}, bf16[5,48,128]{2,1,0:T(8,128)(2,1)S(1)}, u32[]{:S(2)}, u32[]{:S(2)}) collective-permute-start(bf16[5,48,128]{2,1,0:T(8,128)(2,1)S(1)} %get-tuple-element.24.sent_ref), channel_id=1, source_target_pairs={{0,64},{64,0},{128,192},{192,128},{1,65},{65,1},{129,193},{193,129... | collective-permute-start | bytes 184328 | tf_op jit(solution)/shard_map/ppermute | solution.py:255
  29.1 9.5 %collective-permute-start.4 = (bf16[6,48,128]{2,1,0:T(8,128)(2,1)S(1)}, bf16[6,48,128]{2,1,0:T(8,128)(2,1)S(1)}, u32[]{:S(2)}, u32[]{:S(2)}) collective-permute-start(bf16[6,48,128]{2,1,0:T(8,128)(2,1)S(1)} %get-tuple-element.26.refs_1_), channel_id=1, source_target_pairs={{0,192},{64,128},{128,64},{192,0},{1,193},{65,129},{129,65},{193,1... | collective-permute-start | bytes 221192 | tf_op jit(solution)/shard_map/ppermute | solution.py:255
  38.6 1.2 %copy-start.8 = (bf16[8,48,2048]{2,1,0:T(8,128)(2,1)}, bf16[8,48,2048]{2,1,0:T(8,128)(2,1)S(1)}, u32[]{:S(2)}) copy-start(bf16[8,48,2048]{2,1,0:T(8,128)(2,1)S(1)} %all-to-all-done) | copy-start | bytes 4718596
  50.1 34.1 %all-to-all-start.1 = ((bf16[8,48,2048]{2,1,0:T(8,128)(2,1)}), bf16[8,48,2048]{2,1,0:T(8,128)(2,1)S(1)}, u32[]{:S(2)}, u32[]{:S(2)}) async-start(bf16[8,48,2048]{2,1,0:T(8,128)(2,1)} %bitcast.21), calls=%async_computation.1 | async-start | bytes 3145728 | tf_op jit(solution)/shard_map/all_to_all | solution.py:373
  56.1 24.3 %copy-start.6 = (s32[128,2]{0,1:T(2,128)S(1)}, s32[128,2]{0,1:T(2,128)}, u32[]{:S(2)}) copy-start(s32[128,2]{0,1:T(2,128)} %param.11) | copy-start | bytes 3076
  56.1 24.3 %copy-start.7 = (f32[128,2]{0,1:T(2,128)S(1)}, f32[128,2]{0,1:T(2,128)}, u32[]{:S(2)}) copy-start(f32[128,2]{0,1:T(2,128)} %param.12) | copy-start | bytes 3076
  56.1 26.2 %copy-start.1 = (f32[96,2048]{1,0:T(8,128)S(1)}, f32[96,2048]{1,0:T(8,128)}, u32[]{:S(2)}) copy-start(f32[96,2048]{1,0:T(8,128)} %refs_5_.1) | copy-start | bytes 2359300
  56.1 26.1 %copy-start.3 = (bf16[1,96,2048]{2,1,0:T(8,128)(2,1)S(1)}, bf16[1,96,2048]{2,1,0:T(8,128)(2,1)}, u32[]{:S(2)}) copy-start(bf16[1,96,2048]{2,1,0:T(8,128)(2,1)} %refs_6_.1) | copy-start | bytes 1179652
  56.1 5.9 %collective-permute-start.5 = (bf16[1,8,48,128]{3,2,1,0:T(8,128)(2,1)S(1)}, bf16[1,8,48,128]{3,2,1,0:T(8,128)(2,1)S(1)}, u32[]{:S(2)}, u32[]{:S(2)}) collective-permute-start(bf16[1,8,48,128]{3,2,1,0:T(8,128)(2,1)S(1)} %delta_mean.1), channel_id=1, source_target_pairs={{0,48},{16,32},{32,16},{48,0},{1,49},{17,33},{33,17},{49,1},{2,50}... | collective-permute-start | bytes 294920 | tf_op jit(solution)/shard_map/ppermute | solution.py:255
  62.1 5.8 %collective-permute-start.6 = (bf16[2,8,48,128]{3,2,1,0:T(8,128)(2,1)S(1)}, bf16[2,8,48,128]{3,2,1,0:T(8,128)(2,1)S(1)}, u32[]{:S(2)}, u32[]{:S(2)}) collective-permute-start(bf16[2,8,48,128]{3,2,1,0:T(8,128)(2,1)S(1)} %pad_maximum_fusion), channel_id=1, source_target_pairs={{0,16},{16,0},{32,48},{48,32},{1,17},{17,1},{33,49},{49,33},{2,18}... | collective-permute-start | bytes 589832 | tf_op jit(solution)/shard_map/ppermute | solution.py:255
  67.9 1.8 %collective-permute-start.7 = (bf16[4,8,48,128]{3,2,1,0:T(8,128)(2,1)S(1)}, bf16[4,8,48,128]{3,2,1,0:T(8,128)(2,1)S(1)}, u32[]{:S(2)}, u32[]{:S(2)}) collective-permute-start(bf16[4,8,48,128]{3,2,1,0:T(8,128)(2,1)S(1)} %constant_dynamic-update-slice_fusion.a_ref.refs_3_), channel_id=1, source_target_pairs={{0,8},{8,0},{1,9},{9,1},{2,10},{10,2},{3,11},{11,3},{4,12},{12,4},... | collective-permute-start | bytes 1179656 | tf_op jit(solution)/shard_map/ppermute | solution.py:255
  69.9 4.0 %collective-permute-start.8 = (f32[8,128]{1,0:T(8,128)S(1)}, f32[8,128]{1,0:T(8,128)S(1)}, u32[]{:S(2)}, u32[]{:S(2)}) collective-permute-start(f32[8,128]{1,0:T(8,128)S(1)} %delta_squares.1), channel_id=1, source_target_pairs={{0,1},{1,0},{2,3},{3,2},{4,5},{5,4},{6,7},{7,6},{8,9},{9,8},{10,11... | collective-permute-start | bytes 12296 | tf_op jit(solution)/shard_map/ppermute | solution.py:255
  73.8 3.6 %collective-permute-start.9 = (f32[8,128]{1,0:T(8,128)S(1)}, f32[8,128]{1,0:T(8,128)S(1)}, u32[]{:S(2)}, u32[]{:S(2)}) collective-permute-start(f32[8,128]{1,0:T(8,128)S(1)} %add.22), channel_id=1, source_target_pairs={{0,2},{2,0},{4,6},{6,4},{1,3},{3,1},{5,7},{7,5},{8,10},{10,8},{12,... | collective-permute-start | bytes 12296 | tf_op jit(solution)/shard_map/ppermute | solution.py:255
  77.4 4.8 %collective-permute-start.10 = (f32[8,128]{1,0:T(8,128)S(1)}, f32[8,128]{1,0:T(8,128)S(1)}, u32[]{:S(2)}, u32[]{:S(2)}) collective-permute-start(f32[8,128]{1,0:T(8,128)S(1)} %add.23.refs_1_), channel_id=1, source_target_pairs={{0,6},{2,4},{4,2},{6,0},{1,7},{3,5},{5,3},{7,1},{8,14},{10,12},{12... | collective-permute-start | bytes 12296 | tf_op jit(solution)/shard_map/ppermute | solution.py:255

commit v3 on v2

--- a/solution.py
+++ b/solution.py
@@ -17,7 +17,9 @@
 EXPERTS = 8
 REP = ("zh", "y", "c")
 SHARD = ("x", "zl")
-VMEM_LIMIT = 16 * 1024 * 1024
+VMEM_LIMIT = 8 * 1024 * 1024
+FFN_LIMIT = 52 * 1000000
+DISPATCH_LIMIT = 58 * 1024 * 1024
 
 
 def params(**more):
@@ -40,24 +42,41 @@
     return jnp.where(named, place.astype(jnp.int32), capacity)
 
 
-def dispatch_kernel(routes_ref, tokens_ref, out_ref):
+def dispatch_kernel(routes_hbm, tokens_hbm, out_hbm, routes_ref, tokens_ref, out_ref, sems):
     tokens = tokens_ref.shape[0]
     capacity = out_ref.shape[1]
+    width = 512
+    parts = [pl.ds(j * width, width) for j in range(tokens_ref.shape[1] // width)]
+    first = pltpu.make_async_copy(routes_hbm, routes_ref, sems.at[0])
+    first.start()
+    reads = [
+        pltpu.make_async_copy(tokens_hbm.at[:, cols], tokens_ref.at[:, cols], sems.at[1 + j])
+        for j, cols in enumerate(parts)
+    ]
+    for copy in reads:
+        copy.start()
+    first.wait()
     place = slots(routes_ref[...], tokens, capacity)
     row = lax.broadcasted_iota(jnp.int32, (capacity, tokens), 0)
     table = jnp.concatenate(
         [(row == place[e : e + 1, :]).astype(f32) for e in range(EXPERTS)], axis=0
     ).astype(bf16)
-    width = 512
-    for j in range(tokens_ref.shape[1] // width):
-        cols = pl.ds(j * width, width)
+    writes = []
+    for j, cols in enumerate(parts):
+        reads[j].wait()
         part = jnp.dot(table, tokens_ref[:, cols], preferred_element_type=f32).astype(bf16)
         out_ref[:, :, cols] = part.reshape(EXPERTS, capacity, width)
-
-
-def combine_table_kernel(routes_ref, weight_ref, high_ref, low_ref):
+        writes.append(
+            pltpu.make_async_copy(out_ref.at[:, :, cols], out_hbm.at[:, :, cols], sems.at[1 + len(parts) + j])
+        )
+        writes[-1].start()
+    for copy in writes:
+        copy.wait()
+
+
+def combine_kernel(routes_ref, weight_ref, rows_ref, out_ref):
     tokens = routes_ref.shape[1]
-    capacity = high_ref.shape[1] // EXPERTS
+    capacity = rows_ref.shape[0] // EXPERTS
     routes = routes_ref[...]
     place = slots(routes, tokens, capacity)
     row = lax.broadcasted_iota(jnp.int32, (capacity, tokens), 0)
@@ -67,58 +86,53 @@
         parts.append(jnp.where(row == place[e : e + 1, :], weight, 0.0))
     table = jnp.concatenate(parts, axis=0).T
     high = table.astype(bf16)
-    high_ref[...] = high
-    low_ref[...] = (table - high.astype(f32)).astype(bf16)
-
-
-def combine_kernel(high_ref, low_ref, rows_ref, out_ref):
+    low = (table - high.astype(f32)).astype(bf16)
     width = 512
     for j in range(out_ref.shape[1] // width):
         cols = pl.ds(j * width, width)
         rows = rows_ref[:, cols]
         out_ref[:, cols] = (
-            jnp.dot(high_ref[...], rows, preferred_element_type=f32)
-            + jnp.dot(low_ref[...], rows, preferred_element_type=f32)
+            jnp.dot(high, rows, preferred_element_type=f32)
+            + jnp.dot(low, rows, preferred_element_type=f32)
         ).astype(bf16)
 
 
 def ffn_kernel(
-    x_hbm, gate_hbm, up_hbm, down_hbm, out_hbm, x_ref, gate_ref, up_ref, down_ref, hidden_ref, out_ref, sems
+    x_ref, gate_hbm, up_hbm, down_hbm, out_hbm, gate_ref, up_ref, down_ref, gated_ref, hidden_ref, out_ref, sems
 ):
     block, wide = 256, 512
-    count, last = hidden_ref.shape[1] // block, out_ref.shape[1] // wide
-    copies = [pltpu.make_async_copy(x_hbm, x_ref, sems.at[0])]
-    for i in range(count):
-        cols = pl.ds(i * block, block)
-        for hbm, ref in ((gate_hbm, gate_ref), (up_hbm, up_ref)):
-            copies.append(
-                pltpu.make_async_copy(hbm.at[0, :, cols], ref.at[:, cols], sems.at[len(copies)])
-            )
-    for i in range(last):
-        cols = pl.ds(i * wide, wide)
-        copies.append(
-            pltpu.make_async_copy(down_hbm.at[0, :, cols], down_ref.at[:, cols], sems.at[len(copies)])
-        )
+    width, hidden = gate_ref.shape
+    half, count = width // 2, hidden // block
+    copies = []
+    for hbm, ref in ((gate_hbm, gate_ref), (up_hbm, up_ref)):
+        for i in range(2):
+            rows = pl.ds(i * half, half)
+            copies.append(pltpu.make_async_copy(hbm.at[0, rows], ref.at[rows], sems.at[len(copies)]))
+    copies.append(pltpu.make_async_copy(down_hbm.at[0], down_ref, sems.at[4]))
     for copy in copies:
         copy.start()
-    copies[0].wait()
-    for i in range(count):
-        cols = pl.ds(i * block, block)
-        copies[2 * i + 1].wait()
-        gate = jnp.dot(x_ref[...], gate_ref[:, cols], preferred_element_type=f32)
-        copies[2 * i + 2].wait()
+    for i in range(2):
+        rows = pl.ds(i * half, half)
+        copies[i].wait()
+        for n in range(count):
+            cols = pl.ds(n * block, block)
+            part = jnp.dot(x_ref[:, rows], gate_ref[rows, cols], preferred_element_type=f32)
+            gated_ref[:, cols] = part if i == 0 else gated_ref[:, cols] + part
+    copies[2].wait()
+    copies[3].wait()
+    for n in range(count):
+        cols = pl.ds(n * block, block)
         up = jnp.dot(x_ref[...], up_ref[:, cols], preferred_element_type=f32)
+        gate = gated_ref[:, cols]
         hidden_ref[:, cols] = (gate / (1.0 + jnp.exp(-gate)) * up).astype(bf16)
+    copies[4].wait()
     results = []
-    for i in range(last):
-        cols = pl.ds(i * wide, wide)
-        copies[2 * count + 1 + i].wait()
+    for n in range(width // wide):
+        cols = pl.ds(n * wide, wide)
         out_ref[:, cols] = jnp.dot(
             hidden_ref[...], down_ref[:, cols], preferred_element_type=f32
         ).astype(bf16)
-        results.append(
-            pltpu.make_async_copy(out_ref.at[:, cols], out_hbm.at[:, cols], sems.at[len(copies) + i])
-        )
+        results.append(pltpu.make_async_copy(out_ref.at[:, cols], out_hbm.at[:, cols], sems.at[5 + n]))
         results[-1].start()
     for copy in results:
         copy.wait()
@@ -130,19 +144,19 @@
     anywhere = pl.BlockSpec(memory_space=pl.ANY)
     return pl.pallas_call(
         ffn_kernel,
-        in_specs=[anywhere] * 4,
+        in_specs=whole(1) + [anywhere] * 3,
         out_specs=anywhere,
         out_shape=jax.ShapeDtypeStruct((rows, width), bf16),
         scratch_shapes=[
-            pltpu.VMEM((rows, width), bf16),
             pltpu.VMEM((width, hidden), bf16),
             pltpu.VMEM((width, hidden), bf16),
             pltpu.VMEM((hidden, width), bf16),
+            pltpu.VMEM((rows, hidden), f32),
             pltpu.VMEM((rows, hidden), bf16),
             pltpu.VMEM((rows, width), bf16),
-            pltpu.SemaphoreType.DMA((1 + hidden // 128 + width // 256,)),
+            pltpu.SemaphoreType.DMA((5 + width // 512,)),
         ],
-        compiler_params=pltpu.CompilerParams(vmem_limit_bytes=58 * 1024 * 1024),
+        compiler_params=pltpu.CompilerParams(vmem_limit_bytes=FFN_LIMIT),
         cost_estimate=pl.CostEstimate(
             flops=6 * rows * width * hidden,
             bytes_accessed=6 * width * hidden + 4 * rows * width,
@@ -255,7 +269,7 @@
     return lax.ppermute(value, axis, [(i, i ^ bits) for i in range(size)])
 
 
-def outer_sum(pseudo_grad, momentum):
+def outer_sum(pseudo_grad, momentum, outgoing):
     rows, width = pseudo_grad.shape[1:]
     core, y, zh = lax.axis_index("c"), lax.axis_index("y"), lax.axis_index("zh")
     rep = (zh * 4 + y) * 2 + core
@@ -271,6 +285,7 @@
         compiler_params=params(),
         name="delta_halve_first",
     )(at, pseudo_grad, got)
+    outgoing, keep, send = lax.optimization_barrier((outgoing, keep, send))
     got = swap(send, "y", 1)
     keep, send = pl.pallas_call(
         halve_kernel,
@@ -300,8 +315,12 @@
         compiler_params=params(),
         name="delta_add_z",
     )(keep, send, got)
-    got = swap(send, "zh", 3)
-    block = pl.pallas_call(
+    return at, outgoing, keep, send
+
+
+def outer_mean(keep, send, got):
+    part = keep.shape[1:]
+    return pl.pallas_call(
         lambda *refs: mean_kernel(32, *refs),
         in_specs=whole(3),
         out_specs=whole(1)[0],
@@ -309,10 +328,9 @@
         compiler_params=params(),
         name="delta_mean",
     )(keep, send, got)
-    return at, block
-
-
-def outer_finish(at, block, global_params, momentum, local_params):
+
+
+def outer_finish(moe_out, at, block, global_params, momentum, local_params):
     rows, width = global_params.shape
     block = jnp.concatenate([block, swap(block, "y", 3)], axis=0)
     block = jnp.concatenate([block, swap(block, "y", 1)], axis=0)
@@ -328,6 +346,8 @@
     squares = squares + swap(squares, "zl", 1)
     squares = squares + swap(squares, "x", 1)
     entries = float(rows * 8 * width)
+    apart = swap(squares, "x", 3)
+    apart, moe_out = lax.optimization_barrier((apart, moe_out))
     local_next, momentum_next = pl.pallas_call(
         lambda *refs: outer_kernel(entries, *refs),
         in_specs=[smem()] + whole(7),
@@ -339,8 +359,8 @@
         scratch_shapes=[pltpu.VMEM((128, 128), f32)],
         compiler_params=params(),
         name="outer_update",
-    )(at, squares, swap(squares, "x", 3), block, far, global_params, local_params, momentum.T)
-    return momentum_next.T, local_next
+    )(at, squares, apart, block, far, global_params, local_params, momentum.T)
+    return momentum_next.T, local_next, moe_out
 
 
 def local(
@@ -351,24 +371,23 @@
     routes_t, weight_t = routes.T, route_weight.T
     outgoing = pl.pallas_call(
         dispatch_kernel,
-        in_specs=whole(2),
-        out_specs=whole(1)[0],
+        in_specs=[pl.BlockSpec(memory_space=pl.ANY)] * 2,
+        out_specs=pl.BlockSpec(memory_space=pl.ANY),
         out_shape=jax.ShapeDtypeStruct((EXPERTS, capacity, feat_width), bf16),
-        compiler_params=params(),
+        scratch_shapes=[
+            pltpu.VMEM(routes_t.shape, jnp.int32),
+            pltpu.VMEM(tokens.shape, bf16),
+            pltpu.VMEM((EXPERTS, capacity, feat_width), bf16),
+            pltpu.SemaphoreType.DMA((1 + 2 * (feat_width // 512),)),
+        ],
+        compiler_params=pltpu.CompilerParams(vmem_limit_bytes=DISPATCH_LIMIT),
         name="dispatch",
     )(routes_t, tokens)
-    high, low = pl.pallas_call(
-        combine_table_kernel,
-        in_specs=whole(2),
-        out_specs=whole(2),
-        out_shape=[jax.ShapeDtypeStruct((tok_rows, EXPERTS * capacity), bf16)] * 2,
-        compiler_params=params(),
-        name="combine_table",
-    )(routes_t, weight_t)
-    at, block = outer_sum(pseudo_grad, momentum)
+    at, outgoing, keep, send = outer_sum(pseudo_grad, momentum, outgoing)
     received = lax.all_to_all(outgoing, SHARD, split_axis=0, concat_axis=0, tiled=True)
-    received, block = lax.optimization_barrier((received, block))
+    received, keep, send = lax.optimization_barrier((received, keep, send))
     result = ffn(received.reshape(EXPERTS * capacity, feat_width), w_gate, w_up, w_down)
+    result, got = lax.optimization_barrier((result, swap(send, "zh", 3)))
     result = result.reshape(EXPERTS, capacity, feat_width)
     returned = lax.all_to_all(result, SHARD, split_axis=0, concat_axis=0, tiled=True)
     moe_out = pl.pallas_call(
@@ -378,8 +397,9 @@
         out_shape=jax.ShapeDtypeStruct((tok_rows, feat_width), bf16),
         compiler_params=params(),
         name="combine",
-    )(high, low, returned.reshape(EXPERTS * capacity, feat_width))
-    momentum_next, local_next = outer_finish(at, block, global_params, momentum, local_params)
+    )(routes_t, weight_t, returned.reshape(EXPERTS * capacity, feat_width))
+    block = outer_mean(keep, send, got)
+    momentum_next, local_next, moe_out = outer_finish(moe_out, at, block, global_params, momentum, local_params)
     return (moe_out, momentum_next, local_next)
 
 

time: 86.1 us -> 79.1 us (0.919)
  starting transfers between devices: 30.4 us -> 25.2 us
  Pallas kernels: 17.2 us -> 15.1 us
  waiting for transfers between devices: 33.7 us -> 35.4 us
  local copies, waits for them, and re-layouts: 3.32 us -> 2.12 us
    all_to_all x1, waiting for transfers between devices: 0.01 us -> 4.05 us  [local(): lax.all_to_all(outgoing, SHARD, split_axis=0, concat_axis=0, tiled=True)]
    ppermute x11, starting transfers between devices: 18.6 us -> 15.9 us  [swap(): return lax.ppermute(value, axis, [(i, i ^ bits) for i in range(size)])]
    all_to_all x1, starting transfers between devices: 6.04 us -> 3.59 us  [local(): lax.all_to_all(result, SHARD, split_axis=0, concat_axis=0, tiled=True)]
    ppermute x11, waiting for transfers between devices: 33.7 us -> 31.3 us  [swap(): return lax.ppermute(value, axis, [(i, i ^ bits) for i in range(size)])]
    pallas_call x4 -> x3, Pallas kernels: 12.4 us -> 10.1 us  [the longest x1 7.32 us: ffn(): pl.pallas_call(ffn_kernel, in_specs=whole(1) + [anywhere] * 3, out_specs=...]
    unnamed x22 -> x16, local copies, waits for them, and re-layouts: 3.11 us -> 0.86 us
    dynamic_slice x1, local copies, waits for them, and re-layouts: 0.03 us -> 1.1 us  [outer_sum(): lax.dynamic_slice_in_dim(pseudo_grad[0], (1 - core) * half, half, 1)]
  transfers between devices with their start and end apart: 13 -> 13, of which waited for: 11 -> 9; matrix products, arithmetic and copies ran while one was open for 1% -> 1% of each run, Pallas kernels for 4% -> 16%
where the time goes in v3:
time: 79.1 us; the launch traced here: 78.7 us
  waiting for transfers between devices  35.4 us (45%)
  starting transfers between devices  25.2 us (32%)
  Pallas kernels  15.1 us (19%)
  local copies, waits for them, and re-layouts  2.12 us (3%)
  between operations  0.82 us (1%)
    ppermute x11, waiting for transfers between devices, swap(): return lax.ppermute(value, axis, [(i, i ^ bits) for i in range(size)])  31.3 us
    ppermute x11, starting transfers between devices, swap(): return lax.ppermute(value, axis, [(i, i ^ bits) for i in range(size)])  15.9 us
    pallas_call x1, Pallas kernels, ffn(): pl.pallas_call(ffn_kernel, in_specs=whole(1) + [anywhere] * 3, out_specs=...  7.32 us
    all_to_all x1, starting transfers between devices, local(): lax.all_to_all(outgoing, SHARD, split_axis=0, concat_axis=0, tiled=True)  5.69 us
    all_to_all x1, waiting for transfers between devices, local(): lax.all_to_all(outgoing, SHARD, split_axis=0, concat_axis=0, tiled=True)  4.05 us
    all_to_all x1, starting transfers between devices, local(): lax.all_to_all(result, SHARD, split_axis=0, concat_axis=0, tiled=True)  3.59 us
    pallas_call x1, Pallas kernels, local(): pl.pallas_call(dispatch_kernel, in_specs=[pl.BlockSpec(memory_space=pl.AN...  2.78 us
    pallas_call x1, Pallas kernels, outer_finish(): pl.pallas_call(lambda *refs: outer_kernel(entries, *refs), in_specs=[smem...  1.85 us
  transfers between devices with their start and end apart: 13, of which 9 were waited for; matrix products, arithmetic and copies ran while one was open for 1% of the time, Pallas kernels for 16%

profile of v3, /device:TPU:24, one launch (start us, length us, event | category | flops | bytes accessed | tf_op | source)
XLA Modules:
  0.0 78.7 jit_solution(18404555736157317868)
XLA Ops:
  0.6 0.0 copy-start
  0.6 1.1 %dynamic-slice_bitcast_fusion = f32[96,1024]{1,0:T(8,128)S(1)} fusion(f32[1,96,2048]{2,1,0:T(8,128)} %own_ref.1, s32[]{:T(128)S(6)} %select_n.3), kind=kLoop, calls=%fused_computation.1 | loop fusion | bytes 786436 | tf_op jit(solution)/shard_map/dynamic_slice | solution.py:279
  1.7 0.1 collective-permute-start
  1.9 2.8 %dispatch.1 = bf16[8,48,2048]{2,1,0:T(8,128)(2,1)} custom-call(s32[2,128]{1,0:T(2,128)} %bitcast.18, bf16[128,2048]{1,0:T(8,128)(2,1)} %tokens_hbm.1), custom_call_target="tpu_custom_call" | custom-call | tf_op jit(solution)/shard_map/dispatch/pallas_call | solution.py:372
  4.7 0.1 stack.27.at_ref.refs_0_
  4.7 0.0 collective-permute-done.got_ref
  4.7 0.0 copy-done
  4.7 0.6 delta_halve_first.1
  5.3 0.0 copy-start.3
  5.4 5.7 %all-to-all-start = ((bf16[8,48,2048]{2,1,0:T(8,128)(2,1)}), bf16[8,48,2048]{2,1,0:T(8,128)(2,1)S(1)}, u32[]{:S(2)}, u32[]{:S(2)}) async-start(bf16[8,48,2048]{2,1,0:T(8,128)(2,1)} %dispatch.1), calls=%async_computation | async-start | bytes 3145728 | tf_op jit(solution)/shard_map/all_to_all | solution.py:387
  11.0 0.7 collective-permute-start.1
  11.8 0.0 copy-done.3
  11.8 0.1 fusion
  11.9 0.1 copy.15
  11.9 0.1 copy.16
  12.0 3.9 %collective-permute-done.1.got_ref = bf16[96,512]{1,0:T(8,128)(2,1)S(1)} collective-permute-done((bf16[96,512]{1,0:T(8,128)(2,1)S(1)}, bf16[96,512]{1,0:T(8,128)(2,1)S(1)}, u32[]{:S(2)}, u32[]{:S(2)}) %collective-permute-start.1) | collective-permute-done | bytes 98336 | tf_op jit(solution)/shard_map/ppermute | solution.py:269
  15.9 0.6 delta_halve.1
  16.5 0.4 collective-permute-start.2
  16.9 0.1 pad_maximum_fusion.2.mom_ref
  17.0 4.9 %collective-permute-done.2.got_ref = bf16[96,256]{1,0:T(8,128)(2,1)S(1)} collective-permute-done((bf16[96,256]{1,0:T(8,128)(2,1)S(1)}, bf16[96,256]{1,0:T(8,128)(2,1)S(1)}, u32[]{:S(2)}, u32[]{:S(2)}) %collective-permute-start.2) | collective-permute-done | bytes 49184 | tf_op jit(solution)/shard_map/ppermute | solution.py:269
  21.9 3.4 %collective-permute-start.3 = (bf16[5,48,128]{2,1,0:T(8,128)(2,1)S(1)}, bf16[5,48,128]{2,1,0:T(8,128)(2,1)S(1)}, u32[]{:S(2)}, u32[]{:S(2)}) collective-permute-start(bf16[5,48,128]{2,1,0:T(8,128)(2,1)S(1)} %get-tuple-element.31.sent_ref), channel_id=1, source_target_pairs={{0,64},{64,0},{128,192},{192,128},{1,65},{65,1},{129,193},{193,129... | collective-permute-start | bytes 184328 | tf_op jit(solution)/shard_map/ppermute | solution.py:269
  25.3 5.0 %collective-permute-done.3.got_ref = bf16[5,48,128]{2,1,0:T(8,128)(2,1)S(1)} collective-permute-done((bf16[5,48,128]{2,1,0:T(8,128)(2,1)S(1)}, bf16[5,48,128]{2,1,0:T(8,128)(2,1)S(1)}, u32[]{:S(2)}, u32[]{:S(2)}) %collective-permute-start.3) | collective-permute-done | bytes 61472 | tf_op jit(solution)/shard_map/ppermute | solution.py:269
  30.3 4.0 %all-to-all-done = bf16[8,48,2048]{2,1,0:T(8,128)(2,1)S(1)} async-done(((bf16[8,48,2048]{2,1,0:T(8,128)(2,1)}), bf16[8,48,2048]{2,1,0:T(8,128)(2,1)S(1)}, u32[]{:S(2)}, u32[]{:S(2)}) %all-to-all-start) | async-done | bytes 1572896 | tf_op jit(solution)/shard_map/all_to_all | solution.py:387
  34.4 4.7 %collective-permute-start.4 = (bf16[6,48,128]{2,1,0:T(8,128)(2,1)S(1)}, bf16[6,48,128]{2,1,0:T(8,128)(2,1)S(1)}, u32[]{:S(2)}, u32[]{:S(2)}) collective-permute-start(bf16[6,48,128]{2,1,0:T(8,128)(2,1)S(1)} %get-tuple-element.35.refs_1_), channel_id=1, source_target_pairs={{0,192},{64,128},{128,64},{192,0},{1,193},{65,129},{129,65},{193,1... | collective-permute-start | bytes 221192 | tf_op jit(solution)/shard_map/ppermute | solution.py:269
  39.1 7.3 %expert_ffn.1 = bf16[384,2048]{1,0:T(8,128)(2,1)} custom-call(bf16[384,2048]{1,0:T(8,128)(2,1)S(1)} %bitcast.16, bf16[1,2048,768]{2,1,0:T(8,128)(2,1)} %gate_hbm.1, bf16[1,2048,768]{2,1,0:T(8,128)(2,1)} %up_hbm.1, bf16[1,768,2048]{2,1,0:T(8,128)(2,1)} %down_hbm.1), custom_call_target="tpu_custom_call" | custom-call | flops 3623878656 | bytes 12582912 | tf_op jit(solution)/shard_map/expert_ffn/pallas_call | solution.py:145
  46.4 0.0 collective-permute-done.4.refs_2_
  46.4 3.6 %all-to-all-start.1 = ((bf16[8,48,2048]{2,1,0:T(8,128)(2,1)}), bf16[8,48,2048]{2,1,0:T(8,128)(2,1)S(1)}, u32[]{:S(2)}, u32[]{:S(2)}) async-start(bf16[8,48,2048]{2,1,0:T(8,128)(2,1)} %bitcast.10), calls=%async_computation.1 | async-start | bytes 3145728 | tf_op jit(solution)/shard_map/all_to_all | solution.py:392
  50.0 0.0 copy-start.5
  50.1 0.3 collective-permute-start.5
  50.4 5.6 %collective-permute-done.5 = bf16[1,8,48,128]{3,2,1,0:T(8,128)(2,1)S(1)} collective-permute-done((bf16[1,8,48,128]{3,2,1,0:T(8,128)(2,1)S(1)}, bf16[1,8,48,128]{3,2,1,0:T(8,128)(2,1)S(1)}, u32[]{:S(2)}, u32[]{:S(2)}) %collective-permute-start.5) | collective-permute-done | bytes 98336 | tf_op jit(solution)/shard_map/ppermute | solution.py:269
  56.0 0.1 collective-permute-start.6
  56.1 5.7 %collective-permute-done.6 = bf16[2,8,48,128]{3,2,1,0:T(8,128)(2,1)S(1)} collective-permute-done((bf16[2,8,48,128]{3,2,1,0:T(8,128)(2,1)S(1)}, bf16[2,8,48,128]{3,2,1,0:T(8,128)(2,1)S(1)}, u32[]{:S(2)}, u32[]{:S(2)}) %collective-permute-start.6) | collective-permute-done | bytes 196640 | tf_op jit(solution)/shard_map/ppermute | solution.py:269
  61.8 0.0 copy-start.1
  61.8 0.0 copy-start.2
  61.8 0.1 collective-permute-start.7
  61.9 1.7 %collective-permute-done.7.b_ref.refs_4_ = bf16[4,8,48,128]{3,2,1,0:T(8,128)(2,1)S(1)} collective-permute-done((bf16[4,8,48,128]{3,2,1,0:T(8,128)(2,1)S(1)}, bf16[4,8,48,128]{3,2,1,0:T(8,128)(2,1)S(1)}, u32[]{:S(2)}, u32[]{:S(2)}) %collective-permute-start.7) | collective-permute-done | bytes 393248 | tf_op jit(solution)/shard_map/ppermute | solution.py:269
  63.6 0.2 delta_squares.1
  63.8 2.0 %collective-permute-start.8 = (f32[8,128]{1,0:T(8,128)S(1)}, f32[8,128]{1,0:T(8,128)S(1)}, u32[]{:S(2)}, u32[]{:S(2)}) collective-permute-start(f32[8,128]{1,0:T(8,128)S(1)} %delta_squares.1), channel_id=1, source_target_pairs={{0,1},{1,0},{2,3},{3,2},{4,5},{5,4},{6,7},{7,6},{8,9},{9,8},{10,11... | collective-permute-start | bytes 12296 | tf_op jit(solution)/shard_map/ppermute | solution.py:269
  65.8 2.3 %collective-permute-done.8 = f32[8,128]{1,0:T(8,128)S(1)} collective-permute-done((f32[8,128]{1,0:T(8,128)S(1)}, f32[8,128]{1,0:T(8,128)S(1)}, u32[]{:S(2)}, u32[]{:S(2)}) %collective-permute-start.8) | collective-permute-done | bytes 4128 | tf_op jit(solution)/shard_map/ppermute | solution.py:269
  68.1 1.4 %collective-permute-start.9 = (f32[8,128]{1,0:T(8,128)S(1)}, f32[8,128]{1,0:T(8,128)S(1)}, u32[]{:S(2)}, u32[]{:S(2)}) collective-permute-start(f32[8,128]{1,0:T(8,128)S(1)} %add.22), channel_id=1, source_target_pairs={{0,2},{2,0},{4,6},{6,4},{1,3},{3,1},{5,7},{7,5},{8,10},{10,8},{12,... | collective-permute-start | bytes 12296 | tf_op jit(solution)/shard_map/ppermute | solution.py:269
  69.6 2.2 %collective-permute-done.9 = f32[8,128]{1,0:T(8,128)S(1)} collective-permute-done((f32[8,128]{1,0:T(8,128)S(1)}, f32[8,128]{1,0:T(8,128)S(1)}, u32[]{:S(2)}, u32[]{:S(2)}) %collective-permute-start.9) | collective-permute-done | bytes 4128 | tf_op jit(solution)/shard_map/ppermute | solution.py:269
  71.7 2.7 %collective-permute-start.10 = (f32[8,128]{1,0:T(8,128)S(1)}, f32[8,128]{1,0:T(8,128)S(1)}, u32[]{:S(2)}, u32[]{:S(2)}) collective-permute-start(f32[8,128]{1,0:T(8,128)S(1)} %add.23.refs_1_), channel_id=1, source_target_pairs={{0,6},{2,4},{4,2},{6,0},{1,7},{3,5},{5,3},{7,1},{8,14},{10,12},{12... | collective-permute-start | bytes 12296 | tf_op jit(solution)/shard_map/ppermute | solution.py:269
  74.4 0.0 all-to-all-done.1
  74.4 0.0 copy-start.4
  74.4 0.0 copy-done.5
  74.4 0.0 copy-start.6
  74.4 0.7 copy-done.6
  75.1 1.7 %combine.1 = bf16[128,2048]{1,0:T(8,128)(2,1)} custom-call(s32[2,128]{1,0:T(2,128)S(1)} %bitcast.19, f32[2,128]{1,0:T(2,128)S(1)} %bitcast.20, bf16[384,2048]{1,0:T(8,128)(2,1)S(1)} %bitcast.15), custom_call_target="tpu_custom_call" | custom-call | tf_op jit(solution)/shard_map/combine/pallas_call | solution.py:393
  76.8 0.0 collective-permute-done.10.refs_2_
  76.8 0.0 copy-done.1
  76.8 0.0 copy-done.2
  76.8 0.0 copy-done.4
  76.8 1.9 %outer_update.1 = (bf16[1,96,2048]{2,1,0:T(8,128)(2,1)}, f32[64,96]{1,0:T(8,128)}) custom-call(s32[6]{0:T(128)S(1)} %stack.27.at_ref.refs_0_, f32[8,128]{1,0:T(8,128)S(1)} %add.23.refs_1_, f32[8,128]{1,0:T(8,128)S(1)} %collective-permute-done.10.refs_2_, bf16[4,8,48,128]{3,2,1,0:T(8,128)(2,1)S(1)} %pad_maximum_fusion.a_ref.refs_3_, ...), custom_call_target="tpu_custom_call" | custom-call | tf_op jit(solution)/shard_map/outer_update/pallas_call | solution.py:351
  (7 shorter events, 0.1 us)
Async XLA Ops:
  0.6 4.1 %copy-start = (f32[1,96,2048]{2,1,0:T(8,128)S(1)}, f32[1,96,2048]{2,1,0:T(8,128)}, u32[]{:S(2)}) copy-start(f32[1,96,2048]{2,1,0:T(8,128)} %own_ref.1) | copy-start | bytes 2359300
  1.7 3.0 %collective-permute-start = (f32[96,1024]{1,0:T(8,128)S(1)}, f32[96,1024]{1,0:T(8,128)S(1)}, u32[]{:S(2)}, u32[]{:S(2)}) collective-permute-start(f32[96,1024]{1,0:T(8,128)S(1)} %dynamic-slice_bitcast_fusion), channel_id=1, source_target_pairs={{0,8},{8,0},{1,9},{9,1},{2,10},{10,2},{3,11},{11,3},{4,12},{12,4},... | collective-permute-start | bytes 1179656 | tf_op jit(solution)/shard_map/ppermute | solution.py:269
  5.3 6.4 %copy-start.3 = (f32[96,64]{0,1:T(8,128)S(1)}, f32[96,64]{0,1:T(8,128)}, u32[]{:S(2)}) copy-start(f32[96,64]{0,1:T(8,128)} %param.18) | copy-start | bytes 73732
  5.4 29.0 %all-to-all-start = ((bf16[8,48,2048]{2,1,0:T(8,128)(2,1)}), bf16[8,48,2048]{2,1,0:T(8,128)(2,1)S(1)}, u32[]{:S(2)}, u32[]{:S(2)}) async-start(bf16[8,48,2048]{2,1,0:T(8,128)(2,1)} %dispatch.1), calls=%async_computation | async-start | bytes 3145728 | tf_op jit(solution)/shard_map/all_to_all | solution.py:387
  11.0 4.9 %collective-permute-start.1 = (bf16[96,512]{1,0:T(8,128)(2,1)S(1)}, bf16[96,512]{1,0:T(8,128)(2,1)S(1)}, u32[]{:S(2)}, u32[]{:S(2)}) collective-permute-start(bf16[96,512]{1,0:T(8,128)(2,1)S(1)} %get-tuple-element.27), channel_id=1, source_target_pairs={{0,16},{16,0},{32,48},{48,32},{1,17},{17,1},{33,49},{49,33},{2,18}... | collective-permute-start | bytes 294920 | tf_op jit(solution)/shard_map/ppermute | solution.py:269
  16.5 5.4 %collective-permute-start.2 = (bf16[96,256]{1,0:T(8,128)(2,1)S(1)}, bf16[96,256]{1,0:T(8,128)(2,1)S(1)}, u32[]{:S(2)}, u32[]{:S(2)}) collective-permute-start(bf16[96,256]{1,0:T(8,128)(2,1)S(1)} %get-tuple-element.29), channel_id=1, source_target_pairs={{0,48},{16,32},{32,16},{48,0},{1,49},{17,33},{33,17},{49,1},{2,50}... | collective-permute-start | bytes 147464 | tf_op jit(solution)/shard_map/ppermute | solution.py:269
  21.9 8.4 %collective-permute-start.3 = (bf16[5,48,128]{2,1,0:T(8,128)(2,1)S(1)}, bf16[5,48,128]{2,1,0:T(8,128)(2,1)S(1)}, u32[]{:S(2)}, u32[]{:S(2)}) collective-permute-start(bf16[5,48,128]{2,1,0:T(8,128)(2,1)S(1)} %get-tuple-element.31.sent_ref), channel_id=1, source_target_pairs={{0,64},{64,0},{128,192},{192,128},{1,65},{65,1},{129,193},{193,129... | collective-permute-start | bytes 184328 | tf_op jit(solution)/shard_map/ppermute | solution.py:269
  34.4 12.0 %collective-permute-start.4 = (bf16[6,48,128]{2,1,0:T(8,128)(2,1)S(1)}, bf16[6,48,128]{2,1,0:T(8,128)(2,1)S(1)}, u32[]{:S(2)}, u32[]{:S(2)}) collective-permute-start(bf16[6,48,128]{2,1,0:T(8,128)(2,1)S(1)} %get-tuple-element.35.refs_1_), channel_id=1, source_target_pairs={{0,192},{64,128},{128,64},{192,0},{1,193},{65,129},{129,65},{193,1... | collective-permute-start | bytes 221192 | tf_op jit(solution)/shard_map/ppermute | solution.py:269
  46.4 28.0 %all-to-all-start.1 = ((bf16[8,48,2048]{2,1,0:T(8,128)(2,1)}), bf16[8,48,2048]{2,1,0:T(8,128)(2,1)S(1)}, u32[]{:S(2)}, u32[]{:S(2)}) async-start(bf16[8,48,2048]{2,1,0:T(8,128)(2,1)} %bitcast.10), calls=%async_computation.1 | async-start | bytes 3145728 | tf_op jit(solution)/shard_map/all_to_all | solution.py:392
  50.0 24.4 %copy-start.5 = (s32[128,2]{0,1:T(2,128)S(1)}, s32[128,2]{0,1:T(2,128)}, u32[]{:S(2)}) copy-start(s32[128,2]{0,1:T(2,128)} %param.11) | copy-start | bytes 3076
  50.1 5.9 %collective-permute-start.5 = (bf16[1,8,48,128]{3,2,1,0:T(8,128)(2,1)S(1)}, bf16[1,8,48,128]{3,2,1,0:T(8,128)(2,1)S(1)}, u32[]{:S(2)}, u32[]{:S(2)}) collective-permute-start(bf16[1,8,48,128]{3,2,1,0:T(8,128)(2,1)S(1)} %delta_mean.1), channel_id=1, source_target_pairs={{0,48},{16,32},{32,16},{48,0},{1,49},{17,33},{33,17},{49,1},{2,50}... | collective-permute-start | bytes 294920 | tf_op jit(solution)/shard_map/ppermute | solution.py:269
  56.0 5.8 %collective-permute-start.6 = (bf16[2,8,48,128]{3,2,1,0:T(8,128)(2,1)S(1)}, bf16[2,8,48,128]{3,2,1,0:T(8,128)(2,1)S(1)}, u32[]{:S(2)}, u32[]{:S(2)}) collective-permute-start(bf16[2,8,48,128]{3,2,1,0:T(8,128)(2,1)S(1)} %pad_maximum_fusion.1), channel_id=1, source_target_pairs={{0,16},{16,0},{32,48},{48,32},{1,17},{17,1},{33,49},{49,33},{2,18}... | collective-permute-start | bytes 589832 | tf_op jit(solution)/shard_map/ppermute | solution.py:269
  61.8 15.0 %copy-start.1 = (f32[96,2048]{1,0:T(8,128)S(1)}, f32[96,2048]{1,0:T(8,128)}, u32[]{:S(2)}) copy-start(f32[96,2048]{1,0:T(8,128)} %refs_5_.1) | copy-start | bytes 2359300
  61.8 15.0 %copy-start.2 = (bf16[1,96,2048]{2,1,0:T(8,128)(2,1)S(1)}, bf16[1,96,2048]{2,1,0:T(8,128)(2,1)}, u32[]{:S(2)}) copy-start(bf16[1,96,2048]{2,1,0:T(8,128)(2,1)} %refs_6_.1) | copy-start | bytes 1179652
  61.8 1.8 %collective-permute-start.7 = (bf16[4,8,48,128]{3,2,1,0:T(8,128)(2,1)S(1)}, bf16[4,8,48,128]{3,2,1,0:T(8,128)(2,1)S(1)}, u32[]{:S(2)}, u32[]{:S(2)}) collective-permute-start(bf16[4,8,48,128]{3,2,1,0:T(8,128)(2,1)S(1)} %pad_maximum_fusion.a_ref.refs_3_), channel_id=1, source_target_pairs={{0,8},{8,0},{1,9},{9,1},{2,10},{10,2},{3,11},{11,3},{4,12},{12,4},... | collective-permute-start | bytes 1179656 | tf_op jit(solution)/shard_map/ppermute | solution.py:269
  63.8 4.3 %collective-permute-start.8 = (f32[8,128]{1,0:T(8,128)S(1)}, f32[8,128]{1,0:T(8,128)S(1)}, u32[]{:S(2)}, u32[]{:S(2)}) collective-permute-start(f32[8,128]{1,0:T(8,128)S(1)} %delta_squares.1), channel_id=1, source_target_pairs={{0,1},{1,0},{2,3},{3,2},{4,5},{5,4},{6,7},{7,6},{8,9},{9,8},{10,11... | collective-permute-start | bytes 12296 | tf_op jit(solution)/shard_map/ppermute | solution.py:269
  68.1 3.6 %collective-permute-start.9 = (f32[8,128]{1,0:T(8,128)S(1)}, f32[8,128]{1,0:T(8,128)S(1)}, u32[]{:S(2)}, u32[]{:S(2)}) collective-permute-start(f32[8,128]{1,0:T(8,128)S(1)} %add.22), channel_id=1, source_target_pairs={{0,2},{2,0},{4,6},{6,4},{1,3},{3,1},{5,7},{7,5},{8,10},{10,8},{12,... | collective-permute-start | bytes 12296 | tf_op jit(solution)/shard_map/ppermute | solution.py:269
  71.7 5.1 %collective-permute-start.10 = (f32[8,128]{1,0:T(8,128)S(1)}, f32[8,128]{1,0:T(8,128)S(1)}, u32[]{:S(2)}, u32[]{:S(2)}) collective-permute-start(f32[8,128]{1,0:T(8,128)S(1)} %add.23.refs_1_), channel_id=1, source_target_pairs={{0,6},{2,4},{4,2},{6,0},{1,7},{3,5},{5,3},{7,1},{8,14},{10,12},{12... | collective-permute-start | bytes 12296 | tf_op jit(solution)/shard_map/ppermute | solution.py:269
  74.4 2.4 %copy-start.4 = (f32[96,64]{0,1:T(8,128)S(1)}, f32[96,64]{0,1:T(8,128)}, u32[]{:S(2)}) copy-start(f32[96,64]{0,1:T(8,128)} %param.18) | copy-start | bytes 73732
  74.4 0.7 copy-start.6

commit v4 on v0

v4 whole, which is shorter than its diff:
```python
import jax
import jax.numpy as jnp
from jax import lax
from jax.experimental import pallas as pl
from jax.experimental.pallas import tpu as pltpu
from jax.sharding import Mesh
from jax.sharding import PartitionSpec as P

f32 = jnp.float32
bf16 = jnp.bfloat16

outer_momentum = 0.9
outer_rate = 0.7
merge_weight = 0.5
clip_epsilon = 1e-06

EXPERTS = 8
REP = ("zh", "y", "c")
SHARD = ("x", "zl")
VMEM_LIMIT = 8 * 1024 * 1024
FFN_LIMIT = 52 * 1000000


def params(**more):
    return pltpu.CompilerParams(vmem_limit_bytes=VMEM_LIMIT, **more)


def whole(count):
    return [pl.BlockSpec(memory_space=pltpu.VMEM)] * count


def slots(routes, ids, capacity):
    tokens = routes.shape[1]
    named = jnp.logical_or(routes[0:1, :] == ids, routes[1:2, :] == ids)
    before = lax.broadcasted_iota(jnp.int32, (tokens, tokens), 0) < lax.broadcasted_iota(
        jnp.int32, (tokens, tokens), 1
    )
    place = jnp.dot(
        named.astype(f32).astype(bf16), before.astype(f32).astype(bf16), preferred_element_type=f32
    )
    return jnp.where(named, place.astype(jnp.int32), capacity)


def column_experts(at_ref, tokens):
    step = lax.broadcasted_iota(jnp.int32, (8, tokens), 0)
    column = jnp.bitwise_and(at_ref[4] + step, 3)
    return jnp.where(step < 4, column * 2 + at_ref[0], -1)


def one_hot(place, capacity):
    row = lax.broadcasted_iota(jnp.int32, (capacity, place.shape[1]), 0)
    return [(row == place[k : k + 1, :]).astype(f32) for k in range(4)]


def dispatch_kernel(at_ref, own_routes, far_routes, own_ref, far_ref, *out_refs):
    tokens, width = own_ref.shape[0], 512
    capacity = out_refs[0].shape[1]
    ids = column_experts(at_ref, tokens)
    for side, (routes_ref, tokens_ref) in enumerate(((own_routes, own_ref), (far_routes, far_ref))):
        place = slots(routes_ref[0:2].astype(jnp.int32), ids, capacity)
        table = jnp.concatenate(one_hot(place, capacity), axis=0).astype(bf16)
        for j in range(tokens_ref.shape[1] // width):
            cols = pl.ds(j * width, width)
            part = jnp.dot(table, tokens_ref[:, cols], preferred_element_type=f32).astype(bf16)
            for k in range(4):
                out_refs[k][side, :, cols] = part[k * capacity : (k + 1) * capacity]


def combine_kernel(at_ref, own_routes, far_routes, r0, r1, r2, r3, own_ref, far_ref, rows_ref, sems):
    refs = (r0, r1, r2, r3)
    capacity = r0.shape[1]
    tokens, width = own_ref.shape[0], 512
    copies = []
    for side in (1, 0):
        for k, ref in enumerate(refs):
            copies.append(
                pltpu.make_async_copy(
                    ref.at[side], rows_ref.at[side, pl.ds(k * capacity, capacity)], sems.at[len(copies)]
                )
            )
            copies[-1].start()
    ids = column_experts(at_ref, tokens)
    for n, (side, routes_ref, out_ref) in enumerate(((1, far_routes, far_ref), (0, own_routes, own_ref))):
        routes = routes_ref[0:2].astype(jnp.int32)
        hot = one_hot(slots(routes, ids, capacity), capacity)
        parts = []
        for k in range(4):
            weight = jnp.where(
                routes[0:1, :] == ids[k : k + 1, :], routes_ref[2:3, :], routes_ref[3:4, :]
            )
            parts.append(hot[k] * weight)
        table = jnp.concatenate(parts + [jnp.zeros((256 - 4 * capacity, tokens), f32)], axis=0).T
        table = table[:, : 4 * capacity]
        high = table.astype(bf16)
        low = (table - high.astype(f32)).astype(bf16)
        for copy in copies[4 * n : 4 * n + 4]:
            copy.wait()
        for j in range(out_ref.shape[1] // width):
            cols = pl.ds(j * width, width)
            rows = rows_ref[side, :, cols]
            out_ref[:, cols] = (
                jnp.dot(high, rows, preferred_element_type=f32)
                + jnp.dot(low, rows, preferred_element_type=f32)
            ).astype(out_ref.dtype)


def join_kernel(own_ref, got_ref, out_ref):
    out_ref[...] = (own_ref[...] + got_ref[...].astype(f32)).astype(bf16)


def ffn_kernel(*refs):
    x_hbm, (gate_hbm, up_hbm, down_hbm), out_hbm = refs[0:4], refs[4:7], refs[7:11]
    x_ref, gate_ref, up_ref, down_ref, gated_ref, hidden_ref, out_ref, sems = refs[11:]
    block, wide = 256, 512
    width, hidden = gate_ref.shape
    half, count = width // 2, hidden // block
    part_rows = x_hbm[0].shape[0]
    copies = []

    def copy(source, target):
        copies.append(pltpu.make_async_copy(source, target, sems.at[len(copies)]))
        copies[-1].start()

    for k in range(4):
        copy(x_hbm[k], x_ref.at[pl.ds(k * part_rows, part_rows)])
    for hbm, ref in ((gate_hbm, gate_ref), (up_hbm, up_ref)):
        for i in range(2):
            rows = pl.ds(i * half, half)
            copy(hbm.at[0, rows], ref.at[rows])
    copy(down_hbm.at[0], down_ref)
    for k in range(4):
        copies[k].wait()
    for i in range(2):
        rows = pl.ds(i * half, half)
        copies[4 + i].wait()
        for n in range(count):
            cols = pl.ds(n * block, block)
            part = jnp.dot(x_ref[:, rows], gate_ref[rows, cols], preferred_element_type=f32)
            gated_ref[:, cols] = part if i == 0 else gated_ref[:, cols] + part
    copies[6].wait()
    copies[7].wait()
    for n in range(count):
        cols = pl.ds(n * block, block)
        up = jnp.dot(x_ref[...], up_ref[:, cols], preferred_element_type=f32)
        gate = gated_ref[:, cols]
        hidden_ref[:, cols] = (gate / (1.0 + jnp.exp(-gate)) * up).astype(bf16)
    copies[8].wait()
    for n in range(width // wide):
        cols = pl.ds(n * wide, wide)
        out_ref[:, cols] = jnp.dot(
            hidden_ref[...], down_ref[:, cols], preferred_element_type=f32
        ).astype(bf16)
        for k in range(4):
            copy(out_ref.at[pl.ds(k * part_rows, part_rows), cols], out_hbm[k].at[:, cols])
    for out in copies[9:]:
        out.wait()


def ffn(parts, w_gate, w_up, w_down):
    part_rows, width = parts[0].shape
    rows = 4 * part_rows
    hidden = w_gate.shape[2]
    anywhere = pl.BlockSpec(memory_space=pl.ANY)
    return pl.pallas_call(
        ffn_kernel,
        in_specs=[anywhere] * 7,
        out_specs=[anywhere] * 4,
        out_shape=[jax.ShapeDtypeStruct((part_rows, width), bf16)] * 4,
        scratch_shapes=[
            pltpu.VMEM((rows, width), bf16),
            pltpu.VMEM((width, hidden), bf16),
            pltpu.VMEM((width, hidden), bf16),
            pltpu.VMEM((hidden, width), bf16),
            pltpu.VMEM((rows, hidden), f32),
            pltpu.VMEM((rows, hidden), bf16),
            pltpu.VMEM((rows, width), bf16),
            pltpu.SemaphoreType.DMA((9 + 4 * (width // 512),)),
        ],
        compiler_params=pltpu.CompilerParams(vmem_limit_bytes=FFN_LIMIT),
        cost_estimate=pl.CostEstimate(
            flops=6 * rows * width * hidden,
            bytes_accessed=6 * width * hidden + 4 * rows * width,
            transcendentals=rows * hidden,
        ),
        name="expert_ffn",
    )(*parts, w_gate, w_up, w_down)


def pieces_kernel(at_ref, own_ref, got_ref, send_ref):
    half = got_ref.shape[1]
    rows, width = send_ref.shape[1:]
    for p in range(send_ref.shape[0]):
        at_rows, first = pl.ds((p & 1) * rows, rows), (p >> 1) * width
        mine = own_ref[0, at_rows, pl.ds(pl.multiple_of(at_ref[0] * half + first, width), width)]
        send_ref[p] = (mine + got_ref[at_rows, first : first + width]).astype(bf16)


def mean_kernel(replicas, got_ref, mom_ref, out_ref):
    total = got_ref[0].astype(f32)
    for p in range(1, got_ref.shape[0]):
        total += got_ref[p].astype(f32)
    mean = (total * (1.0 / replicas)).astype(bf16)
    mom = mom_ref[...].astype(bf16)
    for p in range(out_ref.shape[0]):
        out_ref[p, 0] = mean
        out_ref[p, 1] = mom


def square_kernel(a_ref, b_ref, out_ref):
    total = jnp.zeros(out_ref.shape, f32)
    step = out_ref.shape[0]
    for ref in (a_ref, b_ref):
        for p in range(ref.shape[0]):
            block = ref[p, 0].astype(f32)
            block = block * block
            for i in range(block.shape[0] // step):
                total += block[i * step : i * step + step]
    out_ref[...] = total


def outer_kernel(entries, at_ref, near_s, far_s, near_ref, far_ref, params_ref, local_ref, mom_ref, next_ref, mom_out, scratch):
    core, rep = at_ref[0], at_ref[5]
    squares = near_s[...] + far_s[...]
    squares = jnp.sum(jnp.sum(squares, axis=1, keepdims=True), axis=0, keepdims=True)
    clip = jnp.minimum(1.0, lax.rsqrt(squares * (1.0 / entries) + clip_epsilon))

    def delta(side, piece):
        return jnp.where(core == side, near_ref[piece, 0].astype(f32), far_ref[piece, 0].astype(f32))

    for cb in range(16):
        near, far = near_ref[cb, 1].astype(f32), far_ref[cb, 1].astype(f32)
        m0, m1 = jnp.where(core == 0, near, far), jnp.where(core == 0, far, near)
        for h in range(2):
            rows, cols = pl.ds(h * 48, 48), pl.ds(cb * 128, 128)
            mom = jnp.concatenate([m0[:, h * 64 : h * 64 + 64], m1[:, h * 64 : h * 64 + 64]], axis=1)
            clipped = clip * delta(cb >> 3, (cb & 7) * 2 + h)
            after = outer_momentum * mom + clipped
            outer = params_ref[rows, cols] - outer_rate * (outer_momentum * after + clipped)
            local = local_ref[0, rows, cols].astype(f32)
            next_ref[0, rows, cols] = (merge_weight * local + (1.0 - merge_weight) * outer).astype(bf16)
    cb = jnp.right_shift(rep, 1)
    side, piece = jnp.right_shift(cb, 3), jnp.bitwise_and(cb, 7) * 2
    scratch[...] = jnp.zeros_like(scratch)
    for h in range(2):
        scratch[h * 48 : h * 48 + 48, :] = delta(side, piece + h)
    scratch[...] = scratch[...].T
    start = pl.multiple_of(core * 64, 64)
    mom_out[...] = outer_momentum * mom_ref[...] + clip * scratch[pl.ds(start, 64), 0:96]


def smem():
    return pl.BlockSpec(memory_space=pltpu.SMEM)


def swap(value, axis, bits):
    size = lax.axis_size(axis)
    return lax.ppermute(value, axis, [(i, i ^ bits) for i in range(size)])


def expert_route(step, back):
    pairs = []
    for zh in range(4):
        for y in range(4):
            for c in range(2):
                for x in range(4):
                    for zl in range(2):
                        z = 2 * zh + zl
                        to = z
                        if zl != c:
                            to = z ^ 1 if step < 2 else (z + (1 if zl else -1)) % 8
                        here = (((zh * 4 + y) * 2 + c) * 4 + x) * 2 + zl
                        there = ((((to >> 1) * 4 + y) * 2 + zl) * 4 + (x + step) % 4) * 2 + (to & 1)
                        pairs.append((there, here) if back else (here, there))
    return pairs


def expert_send(value, step, back=False):
    return lax.ppermute(value, REP + SHARD, expert_route(step, back))


def local(
    tokens, routes, route_weight, w_gate, w_up, w_down, pseudo_grad, global_params, momentum, local_params
):
    tok_rows, feat_width = tokens.shape
    capacity = tok_rows * 3 // 8
    core, y, zh = lax.axis_index("c"), lax.axis_index("y"), lax.axis_index("zh")
    x, zl = lax.axis_index("x"), lax.axis_index("zl")
    rep = (zh * 4 + y) * 2 + core
    at = jnp.stack([core, y, zh, zl, x, rep]).astype(jnp.int32)
    rows, width = pseudo_grad.shape[1:]
    half = width // 2
    part = (rows // 2, 128)

    table = jnp.concatenate([routes.T.astype(f32), route_weight.T], axis=0)
    far_tokens, far_table = swap(tokens, "c", 1), swap(table, "c", 1)
    got = swap(lax.dynamic_slice_in_dim(pseudo_grad[0], (1 - core) * half, half, 1), "c", 1)
    outgoing = pl.pallas_call(
        dispatch_kernel,
        in_specs=[smem()] + whole(4),
        out_specs=whole(4),
        out_shape=[jax.ShapeDtypeStruct((2, capacity, feat_width), bf16)] * 4,
        compiler_params=params(),
        name="dispatch",
    )(at, table, far_table, tokens, far_tokens)
    pieces = pl.pallas_call(
        pieces_kernel,
        in_specs=[smem()] + whole(2),
        out_specs=whole(1)[0],
        out_shape=jax.ShapeDtypeStruct((16,) + part, bf16),
        compiler_params=params(),
        name="delta_pieces",
    )(at, pseudo_grad, got)
    summands = lax.all_to_all(pieces, ("zh", "y"), split_axis=0, concat_axis=0, tiled=True)
    mom_block = jnp.concatenate([momentum[: rows // 2], momentum[rows // 2 :]], axis=1)
    block = pl.pallas_call(
        lambda *refs: mean_kernel(32, *refs),
        in_specs=whole(2),
        out_specs=whole(1)[0],
        out_shape=jax.ShapeDtypeStruct((16, 2) + part, bf16),
        compiler_params=params(),
        name="delta_mean",
    )(summands, mom_block)
    received = [expert_send(outgoing[k], k).reshape(2 * capacity, feat_width) for k in range(4)]
    received, block = lax.optimization_barrier((received, block))
    near = lax.all_to_all(block, ("zh", "y"), split_axis=0, concat_axis=0, tiled=True)
    result = ffn(received, w_gate, w_up, w_down)
    returned = [
        expert_send(result[k].reshape(2, capacity, feat_width), k, back=True) for k in range(4)
    ]
    far = swap(near, "c", 1)
    squares = pl.pallas_call(
        square_kernel,
        in_specs=whole(2),
        out_specs=whole(1)[0],
        out_shape=jax.ShapeDtypeStruct((8, 128), f32),
        compiler_params=params(),
        name="delta_squares",
    )(near, far)
    squares = squares + swap(squares, "zl", 1)
    squares = squares + swap(squares, "x", 1)
    returned, squares = lax.optimization_barrier((returned, squares))
    own_sum, far_sum = pl.pallas_call(
        combine_kernel,
        in_specs=[smem()] + whole(2) + [pl.BlockSpec(memory_space=pl.ANY)] * 4,
        out_specs=whole(2),
        out_shape=[jax.ShapeDtypeStruct((tok_rows, feat_width), t) for t in (f32, bf16)],
        scratch_shapes=[
            pltpu.VMEM((2, 4 * capacity, feat_width), bf16),
            pltpu.SemaphoreType.DMA((8,)),
        ],
        compiler_params=params(),
        name="combine",
    )(at, table, far_table, *returned)
    moe_out = pl.pallas_call(
        join_kernel,
        in_specs=whole(2),
        out_specs=whole(1)[0],
        out_shape=jax.ShapeDtypeStruct((tok_rows, feat_width), bf16),
        compiler_params=params(),
        name="combine_join",
    )(own_sum, swap(far_sum, "c", 1))
    entries = float(rows * 8 * width)
    local_next, momentum_next = pl.pallas_call(
        lambda *refs: outer_kernel(entries, *refs),
        in_specs=[smem()] + whole(7),
        out_specs=whole(2),
        out_shape=[
            jax.ShapeDtypeStruct((1, rows, width), bf16),
            jax.ShapeDtypeStruct((momentum.shape[1], rows), f32),
        ],
        scratch_shapes=[pltpu.VMEM((128, 128), f32)],
        compiler_params=params(),
        name="outer_update",
    )(at, squares, swap(squares, "x", 3), near, far, global_params, local_params, momentum.T)
    return (moe_out, momentum_next.T, local_next)


def solution(mesh):
    fine = Mesh(mesh.devices.reshape(4, 4, 2, 4, 2), REP + SHARD)
    in_specs = (
        P(REP + SHARD, None),
        P(REP + SHARD, None),
        P(REP + SHARD, None),
        P(SHARD, None, None),
        P(SHARD, None, None),
        P(SHARD, None, None),
        P(REP, SHARD, None),
        P(SHARD, None),
        P(SHARD, REP),
        P(REP, SHARD, None),
    )
    out_specs = (P(REP + SHARD, None), P(SHARD, REP), P(REP, SHARD, None))
    return jax.shard_map(local, mesh=fine, in_specs=in_specs, out_specs=out_specs, check_vma=False)
```

time: 398 us -> 104 us (0.26)
  the two profiles are of different devices: /device:TPU:0 before, /device:TPU:24 now
where the time goes in v4:
time: 104 us
  starting transfers between devices  31.9 us (31%)
  waiting for transfers between devices  30.1 us (29%)
  Pallas kernels  18.4 us (18%)
  blocking collectives  16.6 us (16%)
  local copies, waits for them, and re-layouts  4.26 us (4%)
  other arithmetic  1.46 us (1%)
    ppermute x8, waiting for transfers between devices, swap(): return lax.ppermute(value, axis, [(i, i ^ bits) for i in range(size)])  18.4 us
    all_to_all x1, blocking collectives, local(): lax.all_to_all(block, ('zh', 'y'), split_axis=0, concat_axis=0, tiled=True)  16.6 us
    ppermute x8, starting transfers between devices, expert_send(): return lax.ppermute(value, REP + SHARD, expert_route(step, back))  12 us
    all_to_all x1, starting transfers between devices, local(): lax.all_to_all(pieces, ('zh', 'y'), split_axis=0, concat_axis=0, tiled=True)  11.3 us
    all_to_all x1, waiting for transfers between devices, local(): lax.all_to_all(pieces, ('zh', 'y'), split_axis=0, concat_axis=0, tiled=True)  8.72 us
    ppermute x8, starting transfers between devices, swap(): return lax.ppermute(value, axis, [(i, i ^ bits) for i in range(size)])  8.62 us
    pallas_call x1, Pallas kernels, ffn(): pl.pallas_call(ffn_kernel, in_specs=[anywhere] * 7, out_specs=[anywhere]...  8.12 us
    pallas_call x1, Pallas kernels, local(): pl.pallas_call(combine_kernel, in_specs=[smem()] + whole(2) + [pl.BlockSp...  3.87 us
  transfers between devices with their start and end apart: 17, of which 6 were waited for; matrix products, arithmetic and copies ran while one was open for 3% of the time, Pallas kernels for 13%

profile of v4, /device:TPU:24, one launch (start us, length us, event | category | flops | bytes accessed | tf_op | source)
XLA Modules:
  0.0 103.5 jit_solution(9675305319228443706)
XLA Ops:
  0.6 0.0 copy-start.4
  0.6 0.1 collective-permute-start.1
  0.7 1.8 %dynamic-slice_bitcast_fusion = f32[96,1024]{1,0:T(8,128)} fusion(f32[1,96,2048]{2,1,0:T(8,128)} %own_ref.3, s32[]{:T(128)S(6)} %select_n.3), kind=kLoop, calls=%fused_computation | loop fusion | bytes 786436 | tf_op jit(solution)/shard_map/dynamic_slice | solution.py:296
  2.5 0.5 collective-permute-start.6
  3.0 0.7 convert_bitcast_fusion
  3.7 0.7 pad_maximum_fusion.1.own_routes
  4.4 0.0 collective-permute-start
  4.4 0.1 stack.27.at_ref.refs_0_
  4.5 1.0 %collective-permute-done.far_routes = f32[4,128]{1,0:T(4,128)S(1)} collective-permute-done((f32[4,128]{1,0:T(4,128)S(1)}, f32[4,128]{1,0:T(4,128)S(1)}, u32[]{:S(2)}, u32[]{:S(2)}) %collective-permute-start) | collective-permute-done | bytes 2080 | tf_op jit(solution)/shard_map/ppermute | solution.py:257
  5.5 0.0 collective-permute-done.1.far_ref
  5.5 0.0 copy-start.2
  5.5 1.0 %copy-done.2 = bf16[128,2048]{1,0:T(8,128)(2,1)S(1)} copy-done((bf16[128,2048]{1,0:T(8,128)(2,1)S(1)}, bf16[128,2048]{1,0:T(8,128)(2,1)}, u32[]{:S(2)}) %copy-start.2) | copy-done | bytes 524312
  6.6 2.2 %dispatch.1 = (bf16[2,48,2048]{2,1,0:T(8,128)(2,1)}, bf16[2,48,2048]{2,1,0:T(8,128)(2,1)}, bf16[2,48,2048]{2,1,0:T(8,128)(2,1)S(1)}, bf16[2,48,2048]{2,1,0:T(8,128)(2,1)S(1)}) custom-call(s32[6]{0:T(128)S(1)} %stack.27.at_ref.refs_0_, f32[4,128]{1,0:T(4,128)S(1)} %pad_maximum_fusion.1.own_routes, f32[4,128]{1,0:T(4,128)S(1)} %collective-permute-done.far_routes, ...), custom_call_target="tpu_custom_call" | custom-call | tf_op jit(solution)/shard_map/dispatch/pallas_call | solution.py:297
  8.8 1.6 %collective-permute-start.2 = (bf16[2,48,2048]{2,1,0:T(8,128)(2,1)}, bf16[2,48,2048]{2,1,0:T(8,128)(2,1)S(1)}, u32[]{:S(2)}, u32[]{:S(2)}) collective-permute-start(bf16[2,48,2048]{2,1,0:T(8,128)(2,1)} %get-tuple-element.25), channel_id=1, source_target_pairs={{0,0},{1,8},{2,2},{3,10},{4,4},{5,12},{6,6},{7,14},{8,1},{9,9},{10... | collective-permute-start | bytes 1179656 | tf_op jit(solution)/shard_map/ppermute | solution.py:278
  10.4 1.5 %collective-permute-start.3 = (bf16[2,48,2048]{2,1,0:T(8,128)(2,1)}, bf16[2,48,2048]{2,1,0:T(8,128)(2,1)S(1)}, u32[]{:S(2)}, u32[]{:S(2)}) collective-permute-start(bf16[2,48,2048]{2,1,0:T(8,128)(2,1)} %get-tuple-element.26), channel_id=1, source_target_pairs={{0,2},{1,10},{2,4},{3,12},{4,6},{5,14},{6,0},{7,8},{8,3},{9,11},{1... | collective-permute-start | bytes 1179656 | tf_op jit(solution)/shard_map/ppermute | solution.py:278
  11.9 2.7 %collective-permute-start.4 = (bf16[2,48,2048]{2,1,0:T(8,128)(2,1)S(1)}, bf16[2,48,2048]{2,1,0:T(8,128)(2,1)S(1)}, u32[]{:S(2)}, u32[]{:S(2)}) collective-permute-start(bf16[2,48,2048]{2,1,0:T(8,128)(2,1)S(1)} %get-tuple-element.27), channel_id=1, source_target_pairs={{0,4},{1,76},{2,6},{3,78},{4,0},{5,72},{6,2},{7,74},{8,197},{9,13}... | collective-permute-start | bytes 1179656 | tf_op jit(solution)/shard_map/ppermute | solution.py:278
  14.6 1.4 %collective-permute-start.5 = (bf16[2,48,2048]{2,1,0:T(8,128)(2,1)S(1)}, bf16[2,48,2048]{2,1,0:T(8,128)(2,1)S(1)}, u32[]{:S(2)}, u32[]{:S(2)}) collective-permute-start(bf16[2,48,2048]{2,1,0:T(8,128)(2,1)S(1)} %get-tuple-element.28), channel_id=1, source_target_pairs={{0,6},{1,78},{2,0},{3,72},{4,2},{5,74},{6,4},{7,76},{8,199},{9,15}... | collective-permute-start | bytes 1179656 | tf_op jit(solution)/shard_map/ppermute | solution.py:278
  16.1 0.0 collective-permute-done.6.got_ref
  16.1 0.0 copy-start
  16.1 1.1 %copy-done = f32[1,96,2048]{2,1,0:T(8,128)S(1)} copy-done((f32[1,96,2048]{2,1,0:T(8,128)S(1)}, f32[1,96,2048]{2,1,0:T(8,128)}, u32[]{:S(2)}) %copy-start) | copy-done | bytes 786456
  17.2 1.3 %delta_pieces.1 = bf16[16,48,128]{2,1,0:T(8,128)(2,1)} custom-call(s32[6]{0:T(128)S(1)} %stack.27.at_ref.refs_0_, f32[1,96,2048]{2,1,0:T(8,128)S(1)} %copy-done, f32[96,1024]{1,0:T(8,128)S(1)} %collective-permute-done.6.got_ref), custom_call_target="tpu_custom_call" | custom-call | tf_op jit(solution)/shard_map/delta_pieces/pallas_call | solution.py:305
  18.5 11.3 %all-to-all-start = ((bf16[16,48,128]{2,1,0:T(8,128)(2,1)}), bf16[16,48,128]{2,1,0:T(8,128)(2,1)S(1)}, u32[]{:S(2)}, u32[]{:S(2)}) async-start(bf16[16,48,128]{2,1,0:T(8,128)(2,1)} %delta_pieces.1), calls=%async_computation | async-start | bytes 393216 | tf_op jit(solution)/shard_map/all_to_all | solution.py:313
  29.8 0.0 copy-done.4
  29.8 0.1 fusion
  29.9 0.1 copy.15
  30.0 0.1 copy.16
  30.1 0.1 pad_maximum_fusion.refs_1_
  30.1 8.7 %all-to-all-done.refs_0_ = bf16[16,48,128]{2,1,0:T(8,128)(2,1)S(1)} async-done(((bf16[16,48,128]{2,1,0:T(8,128)(2,1)}), bf16[16,48,128]{2,1,0:T(8,128)(2,1)S(1)}, u32[]{:S(2)}, u32[]{:S(2)}) %all-to-all-start) | async-done | bytes 196640 | tf_op jit(solution)/shard_map/all_to_all | solution.py:313
  38.9 0.0 collective-permute-done.2
  38.9 0.0 collective-permute-done.3
  38.9 0.0 collective-permute-done.4
  38.9 0.0 collective-permute-done.5
  39.0 16.6 %all_to_all.10.a_ref.refs_3_ = bf16[16,2,48,128]{3,2,1,0:T(8,128)(2,1)S(1)} all-to-all(bf16[16,2,48,128]{3,2,1,0:T(8,128)(2,1)S(1)} %delta_mean.1), channel_id=1, replica_groups=mesh['zh'=4,'y'=4,'c'=2,'x'=4,'zl'=2] {'zh','y'}, dimensions={0} | all-to-all | bytes 786432 | tf_op jit(solution)/shard_map/all_to_all | solution.py:325
  55.6 0.0 copy-start.1
  55.6 0.0 copy-start.3
  55.6 2.5 %collective-permute-start.11 = (bf16[16,2,48,128]{3,2,1,0:T(8,128)(2,1)S(1)}, bf16[16,2,48,128]{3,2,1,0:T(8,128)(2,1)S(1)}, u32[]{:S(2)}, u32[]{:S(2)}) collective-permute-start(bf16[16,2,48,128]{3,2,1,0:T(8,128)(2,1)S(1)} %all_to_all.10.a_ref.refs_3_), channel_id=1, source_target_pairs={{0,8},{8,0},{1,9},{9,1},{2,10},{10,2},{3,11},{11,3},{4,12},{12,4},... | collective-permute-start | bytes 1179656 | tf_op jit(solution)/shard_map/ppermute | solution.py:257
  58.1 8.1 %expert_ffn.1 = (bf16[96,2048]{1,0:T(8,128)(2,1)S(1)}, bf16[96,2048]{1,0:T(8,128)(2,1)S(1)}, bf16[96,2048]{1,0:T(8,128)(2,1)S(1)}, bf16[96,2048]{1,0:T(8,128)(2,1)S(1)}) custom-call(bf16[96,2048]{1,0:T(8,128)(2,1)S(1)} %bitcast.22, bf16[96,2048]{1,0:T(8,128)(2,1)S(1)} %bitcast.23, bf16[96,2048]{1,0:T(8,128)(2,1)S(1)} %bitcast.24, ...), custom_call_target="tpu_custom_call" | custom-call | flops 3623878656 | bytes 12582912 | tf_op jit(solution)/shard_map/expert_ffn/pallas_call | solution.py:164
  66.2 3.0 %collective-permute-start.8 = (bf16[2,48,2048]{2,1,0:T(8,128)(2,1)S(1)}, bf16[2,48,2048]{2,1,0:T(8,128)(2,1)S(1)}, u32[]{:S(2)}, u32[]{:S(2)}) collective-permute-start(bf16[2,48,2048]{2,1,0:T(8,128)(2,1)S(1)} %bitcast.29), channel_id=1, source_target_pairs={{2,0},{10,1},{4,2},{12,3},{6,4},{14,5},{0,6},{8,7},{3,8},{11,9},{5... | collective-permute-start | bytes 1179656 | tf_op jit(solution)/shard_map/ppermute | solution.py:278
  69.2 0.7 collective-permute-start.7
  69.9 1.0 collective-permute-start.9
  70.9 0.0 collective-permute-start.10
  70.9 0.0 collective-permute-done.11.b_ref.refs_4_
  70.9 0.2 delta_squares.1
  71.1 3.7 %collective-permute-start.12 = (f32[8,128]{1,0:T(8,128)S(1)}, f32[8,128]{1,0:T(8,128)S(1)}, u32[]{:S(2)}, u32[]{:S(2)}) collective-permute-start(f32[8,128]{1,0:T(8,128)S(1)} %delta_squares.1), channel_id=1, source_target_pairs={{0,1},{1,0},{2,3},{3,2},{4,5},{5,4},{6,7},{7,6},{8,9},{9,8},{10,11... | collective-permute-start | bytes 12296 | tf_op jit(solution)/shard_map/ppermute | solution.py:257
  74.8 5.6 %collective-permute-done.12 = f32[8,128]{1,0:T(8,128)S(1)} collective-permute-done((f32[8,128]{1,0:T(8,128)S(1)}, f32[8,128]{1,0:T(8,128)S(1)}, u32[]{:S(2)}, u32[]{:S(2)}) %collective-permute-start.12) | collective-permute-done | bytes 4128 | tf_op jit(solution)/shard_map/ppermute | solution.py:257
  80.4 0.0 collective-permute-start.13
  80.4 8.5 %collective-permute-done.13 = f32[8,128]{1,0:T(8,128)S(1)} collective-permute-done((f32[8,128]{1,0:T(8,128)S(1)}, f32[8,128]{1,0:T(8,128)S(1)}, u32[]{:S(2)}, u32[]{:S(2)}) %collective-permute-start.13) | collective-permute-done | bytes 4128 | tf_op jit(solution)/shard_map/ppermute | solution.py:257
  88.9 0.0 collective-permute-done.8.r1
  88.9 0.0 collective-permute-done.7.r0
  89.0 0.0 collective-permute-done.9.r2
  89.0 3.0 %collective-permute-done.10.r3 = bf16[2,48,2048]{2,1,0:T(8,128)(2,1)S(1)} collective-permute-done((bf16[2,48,2048]{2,1,0:T(8,128)(2,1)S(1)}, bf16[2,48,2048]{2,1,0:T(8,128)(2,1)S(1)}, u32[]{:S(2)}, u32[]{:S(2)}) %collective-permute-start.10) | collective-permute-done | bytes 393248 | tf_op jit(solution)/shard_map/ppermute | solution.py:278
  91.9 3.9 %combine.1 = (f32[128,2048]{1,0:T(8,128)S(1)}, bf16[128,2048]{1,0:T(8,128)(2,1)S(1)}) custom-call(s32[6]{0:T(128)S(1)} %stack.27.at_ref.refs_0_, f32[4,128]{1,0:T(4,128)S(1)} %pad_maximum_fusion.1.own_routes, f32[4,128]{1,0:T(4,128)S(1)} %collective-permute-done.far_routes, bf16[2,48,2048]{2,1,0:T(8,128)(2,1)S(1)} %collective-permute-done.7.r0, ...), custom_call_target="tpu_custom_call" | custom-call | tf_op jit(solution)/shard_map/combine/pallas_call | solution.py:342
  95.8 0.1 collective-permute-start.14
  95.9 1.7 %collective-permute-start.15 = (f32[8,128]{1,0:T(8,128)S(1)}, f32[8,128]{1,0:T(8,128)S(1)}, u32[]{:S(2)}, u32[]{:S(2)}) collective-permute-start(f32[8,128]{1,0:T(8,128)S(1)} %add.19.refs_1_), channel_id=1, source_target_pairs={{0,6},{2,4},{4,2},{6,0},{1,7},{3,5},{5,3},{7,1},{8,14},{10,12},{12... | collective-permute-start | bytes 12296 | tf_op jit(solution)/shard_map/ppermute | solution.py:257
  97.6 3.2 %collective-permute-done.15.refs_2_ = f32[8,128]{1,0:T(8,128)S(1)} collective-permute-done((f32[8,128]{1,0:T(8,128)S(1)}, f32[8,128]{1,0:T(8,128)S(1)}, u32[]{:S(2)}, u32[]{:S(2)}) %collective-permute-start.15) | collective-permute-done | bytes 4128 | tf_op jit(solution)/shard_map/ppermute | solution.py:257
  100.8 0.0 copy-done.1
  100.8 0.0 copy-done.3
  100.8 1.8 %outer_update.1 = (bf16[1,96,2048]{2,1,0:T(8,128)(2,1)}, f32[64,96]{1,0:T(8,128)}) custom-call(s32[6]{0:T(128)S(1)} %stack.27.at_ref.refs_0_, f32[8,128]{1,0:T(8,128)S(1)} %add.19.refs_1_, f32[8,128]{1,0:T(8,128)S(1)} %collective-permute-done.15.refs_2_, bf16[16,2,48,128]{3,2,1,0:T(8,128)(2,1)S(1)} %all_to_all.10.a_ref.refs_3_, ...), custom_call_target="tpu_custom_call" | custom-call | tf_op jit(solution)/shard_map/outer_update/pallas_call | solution.py:363
  102.6 0.0 collective-permute-done.14.got_ref
  102.6 0.9 combine_join.1
  (3 shorter events, 0.1 us)
Async XLA Ops:
  0.6 29.2 %copy-start.4 = (f32[96,64]{0,1:T(8,128)S(1)}, f32[96,64]{0,1:T(8,128)}, u32[]{:S(2)}) copy-start(f32[96,64]{0,1:T(8,128)} %param.18) | copy-start | bytes 73732
  0.6 4.9 %collective-permute-start.1 = (bf16[128,2048]{1,0:T(8,128)(2,1)}, bf16[128,2048]{1,0:T(8,128)(2,1)S(1)}, u32[]{:S(2)}, u32[]{:S(2)}) collective-permute-start(bf16[128,2048]{1,0:T(8,128)(2,1)} %own_ref.2), channel_id=1, source_target_pairs={{0,8},{8,0},{1,9},{9,1},{2,10},{10,2},{3,11},{11,3},{4,12},{12,4},... | collective-permute-start | bytes 1572872 | tf_op jit(solution)/shard_map/ppermute | solution.py:257
  2.5 13.6 %collective-permute-start.6 = (f32[96,1024]{1,0:T(8,128)}, f32[96,1024]{1,0:T(8,128)S(1)}, u32[]{:S(2)}, u32[]{:S(2)}) collective-permute-start(f32[96,1024]{1,0:T(8,128)} %dynamic-slice_bitcast_fusion), channel_id=1, source_target_pairs={{0,8},{8,0},{1,9},{9,1},{2,10},{10,2},{3,11},{11,3},{4,12},{12,4},... | collective-permute-start | bytes 1179656 | tf_op jit(solution)/shard_map/ppermute | solution.py:257
  4.4 1.2 %collective-permute-start = (f32[4,128]{1,0:T(4,128)S(1)}, f32[4,128]{1,0:T(4,128)S(1)}, u32[]{:S(2)}, u32[]{:S(2)}) collective-permute-start(f32[4,128]{1,0:T(4,128)S(1)} %pad_maximum_fusion.1.own_routes), channel_id=1, source_target_pairs={{0,8},{8,0},{1,9},{9,1},{2,10},{10,2},{3,11},{11,3},{4,12},{12,4},... | collective-permute-start | bytes 6152 | tf_op jit(solution)/shard_map/ppermute | solution.py:257
  5.5 1.0 %copy-start.2 = (bf16[128,2048]{1,0:T(8,128)(2,1)S(1)}, bf16[128,2048]{1,0:T(8,128)(2,1)}, u32[]{:S(2)}) copy-start(bf16[128,2048]{1,0:T(8,128)(2,1)} %own_ref.2) | copy-start | bytes 1572868
  8.8 30.2 %collective-permute-start.2 = (bf16[2,48,2048]{2,1,0:T(8,128)(2,1)}, bf16[2,48,2048]{2,1,0:T(8,128)(2,1)S(1)}, u32[]{:S(2)}, u32[]{:S(2)}) collective-permute-start(bf16[2,48,2048]{2,1,0:T(8,128)(2,1)} %get-tuple-element.25), channel_id=1, source_target_pairs={{0,0},{1,8},{2,2},{3,10},{4,4},{5,12},{6,6},{7,14},{8,1},{9,9},{10... | collective-permute-start | bytes 1179656 | tf_op jit(solution)/shard_map/ppermute | solution.py:278
  10.4 28.5 %collective-permute-start.3 = (bf16[2,48,2048]{2,1,0:T(8,128)(2,1)}, bf16[2,48,2048]{2,1,0:T(8,128)(2,1)S(1)}, u32[]{:S(2)}, u32[]{:S(2)}) collective-permute-start(bf16[2,48,2048]{2,1,0:T(8,128)(2,1)} %get-tuple-element.26), channel_id=1, source_target_pairs={{0,2},{1,10},{2,4},{3,12},{4,6},{5,14},{6,0},{7,8},{8,3},{9,11},{1... | collective-permute-start | bytes 1179656 | tf_op jit(solution)/shard_map/ppermute | solution.py:278
  11.9 27.0 %collective-permute-start.4 = (bf16[2,48,2048]{2,1,0:T(8,128)(2,1)S(1)}, bf16[2,48,2048]{2,1,0:T(8,128)(2,1)S(1)}, u32[]{:S(2)}, u32[]{:S(2)}) collective-permute-start(bf16[2,48,2048]{2,1,0:T(8,128)(2,1)S(1)} %get-tuple-element.27), channel_id=1, source_target_pairs={{0,4},{1,76},{2,6},{3,78},{4,0},{5,72},{6,2},{7,74},{8,197},{9,13}... | collective-permute-start | bytes 1179656 | tf_op jit(solution)/shard_map/ppermute | solution.py:278
  14.6 24.3 %collective-permute-start.5 = (bf16[2,48,2048]{2,1,0:T(8,128)(2,1)S(1)}, bf16[2,48,2048]{2,1,0:T(8,128)(2,1)S(1)}, u32[]{:S(2)}, u32[]{:S(2)}) collective-permute-start(bf16[2,48,2048]{2,1,0:T(8,128)(2,1)S(1)} %get-tuple-element.28), channel_id=1, source_target_pairs={{0,6},{1,78},{2,0},{3,72},{4,2},{5,74},{6,4},{7,76},{8,199},{9,15}... | collective-permute-start | bytes 1179656 | tf_op jit(solution)/shard_map/ppermute | solution.py:278
  16.1 1.1 %copy-start = (f32[1,96,2048]{2,1,0:T(8,128)S(1)}, f32[1,96,2048]{2,1,0:T(8,128)}, u32[]{:S(2)}) copy-start(f32[1,96,2048]{2,1,0:T(8,128)} %own_ref.3) | copy-start | bytes 2359300
  18.5 20.4 %all-to-all-start = ((bf16[16,48,128]{2,1,0:T(8,128)(2,1)}), bf16[16,48,128]{2,1,0:T(8,128)(2,1)S(1)}, u32[]{:S(2)}, u32[]{:S(2)}) async-start(bf16[16,48,128]{2,1,0:T(8,128)(2,1)} %delta_pieces.1), calls=%async_computation | async-start | bytes 393216 | tf_op jit(solution)/shard_map/all_to_all | solution.py:313
  55.6 45.2 %copy-start.1 = (f32[96,2048]{1,0:T(8,128)S(1)}, f32[96,2048]{1,0:T(8,128)}, u32[]{:S(2)}) copy-start(f32[96,2048]{1,0:T(8,128)} %refs_5_.3) | copy-start | bytes 2359300
  55.6 45.2 %copy-start.3 = (bf16[1,96,2048]{2,1,0:T(8,128)(2,1)S(1)}, bf16[1,96,2048]{2,1,0:T(8,128)(2,1)}, u32[]{:S(2)}) copy-start(bf16[1,96,2048]{2,1,0:T(8,128)(2,1)} %refs_6_.3) | copy-start | bytes 1179652
  55.6 15.3 %collective-permute-start.11 = (bf16[16,2,48,128]{3,2,1,0:T(8,128)(2,1)S(1)}, bf16[16,2,48,128]{3,2,1,0:T(8,128)(2,1)S(1)}, u32[]{:S(2)}, u32[]{:S(2)}) collective-permute-start(bf16[16,2,48,128]{3,2,1,0:T(8,128)(2,1)S(1)} %all_to_all.10.a_ref.refs_3_), channel_id=1, source_target_pairs={{0,8},{8,0},{1,9},{9,1},{2,10},{10,2},{3,11},{11,3},{4,12},{12,4},... | collective-permute-start | bytes 1179656 | tf_op jit(solution)/shard_map/ppermute | solution.py:257
  66.2 22.8 %collective-permute-start.8 = (bf16[2,48,2048]{2,1,0:T(8,128)(2,1)S(1)}, bf16[2,48,2048]{2,1,0:T(8,128)(2,1)S(1)}, u32[]{:S(2)}, u32[]{:S(2)}) collective-permute-start(bf16[2,48,2048]{2,1,0:T(8,128)(2,1)S(1)} %bitcast.29), channel_id=1, source_target_pairs={{2,0},{10,1},{4,2},{12,3},{6,4},{14,5},{0,6},{8,7},{3,8},{11,9},{5... | collective-permute-start | bytes 1179656 | tf_op jit(solution)/shard_map/ppermute | solution.py:278
  69.2 19.7 %collective-permute-start.7 = (bf16[2,48,2048]{2,1,0:T(8,128)(2,1)S(1)}, bf16[2,48,2048]{2,1,0:T(8,128)(2,1)S(1)}, u32[]{:S(2)}, u32[]{:S(2)}) collective-permute-start(bf16[2,48,2048]{2,1,0:T(8,128)(2,1)S(1)} %bitcast.28), channel_id=1, source_target_pairs={{0,0},{8,1},{2,2},{10,3},{4,4},{12,5},{6,6},{14,7},{1,8},{9,9},{3,... | collective-permute-start | bytes 1179656 | tf_op jit(solution)/shard_map/ppermute | solution.py:278
  69.9 19.0 %collective-permute-start.9 = (bf16[2,48,2048]{2,1,0:T(8,128)(2,1)S(1)}, bf16[2,48,2048]{2,1,0:T(8,128)(2,1)S(1)}, u32[]{:S(2)}, u32[]{:S(2)}) collective-permute-start(bf16[2,48,2048]{2,1,0:T(8,128)(2,1)S(1)} %bitcast.27), channel_id=1, source_target_pairs={{4,0},{76,1},{6,2},{78,3},{0,4},{72,5},{2,6},{74,7},{197,8},{13,9}... | collective-permute-start | bytes 1179656 | tf_op jit(solution)/shard_map/ppermute | solution.py:278
  70.9 21.0 %collective-permute-start.10 = (bf16[2,48,2048]{2,1,0:T(8,128)(2,1)S(1)}, bf16[2,48,2048]{2,1,0:T(8,128)(2,1)S(1)}, u32[]{:S(2)}, u32[]{:S(2)}) collective-permute-start(bf16[2,48,2048]{2,1,0:T(8,128)(2,1)S(1)} %bitcast.26), channel_id=1, source_target_pairs={{6,0},{78,1},{0,2},{72,3},{2,4},{74,5},{4,6},{76,7},{199,8},{15,9}... | collective-permute-start | bytes 1179656 | tf_op jit(solution)/shard_map/ppermute | solution.py:278
  71.1 9.3 %collective-permute-start.12 = (f32[8,128]{1,0:T(8,128)S(1)}, f32[8,128]{1,0:T(8,128)S(1)}, u32[]{:S(2)}, u32[]{:S(2)}) collective-permute-start(f32[8,128]{1,0:T(8,128)S(1)} %delta_squares.1), channel_id=1, source_target_pairs={{0,1},{1,0},{2,3},{3,2},{4,5},{5,4},{6,7},{7,6},{8,9},{9,8},{10,11... | collective-permute-start | bytes 12296 | tf_op jit(solution)/shard_map/ppermute | solution.py:257
  80.4 8.5 %collective-permute-start.13 = (f32[8,128]{1,0:T(8,128)S(1)}, f32[8,128]{1,0:T(8,128)S(1)}, u32[]{:S(2)}, u32[]{:S(2)}) collective-permute-start(f32[8,128]{1,0:T(8,128)S(1)} %add.18), channel_id=1, source_target_pairs={{0,2},{2,0},{4,6},{6,4},{1,3},{3,1},{5,7},{7,5},{8,10},{10,8},{12,... | collective-permute-start | bytes 12296 | tf_op jit(solution)/shard_map/ppermute | solution.py:257
  95.8 6.8 %collective-permute-start.14 = (bf16[128,2048]{1,0:T(8,128)(2,1)S(1)}, bf16[128,2048]{1,0:T(8,128)(2,1)S(1)}, u32[]{:S(2)}, u32[]{:S(2)}) collective-permute-start(bf16[128,2048]{1,0:T(8,128)(2,1)S(1)} %get-tuple-element.43), channel_id=1, source_target_pairs={{0,8},{8,0},{1,9},{9,1},{2,10},{10,2},{3,11},{11,3},{4,12},{12,4},... | collective-permute-start | bytes 1572872 | tf_op jit(solution)/shard_map/ppermute | solution.py:257
  95.9 4.9 %collective-permute-start.15 = (f32[8,128]{1,0:T(8,128)S(1)}, f32[8,128]{1,0:T(8,128)S(1)}, u32[]{:S(2)}, u32[]{:S(2)}) collective-permute-start(f32[8,128]{1,0:T(8,128)S(1)} %add.19.refs_1_), channel_id=1, source_target_pairs={{0,6},{2,4},{4,2},{6,0},{1,7},{3,5},{5,3},{7,1},{8,14},{10,12},{12... | collective-permute-start | bytes 12296 | tf_op jit(solution)/shard_map/ppermute | solution.py:257

commit v5 on v3

--- a/solution.py
+++ b/solution.py
@@ -42,13 +42,17 @@
     return jnp.where(named, place.astype(jnp.int32), capacity)
 
 
-def dispatch_kernel(routes_hbm, tokens_hbm, out_hbm, routes_ref, tokens_ref, out_ref, sems):
+def dispatch_kernel(
+    routes_hbm, tokens_hbm, weight_hbm, out_hbm, routes_ref, weight_ref, tokens_ref, out_ref, sems
+):
     tokens = tokens_ref.shape[0]
     capacity = out_ref.shape[1]
     width = 512
     parts = [pl.ds(j * width, width) for j in range(tokens_ref.shape[1] // width)]
     first = pltpu.make_async_copy(routes_hbm, routes_ref, sems.at[0])
     first.start()
+    last = pltpu.make_async_copy(weight_hbm, weight_ref, sems.at[1 + 2 * len(parts)])
+    last.start()
     reads = [
         pltpu.make_async_copy(tokens_hbm.at[:, cols], tokens_ref.at[:, cols], sems.at[1 + j])
         for j, cols in enumerate(parts)
@@ -70,7 +74,7 @@
             pltpu.make_async_copy(out_ref.at[:, :, cols], out_hbm.at[:, :, cols], sems.at[1 + len(parts) + j])
         )
         writes[-1].start()
-    for copy in writes:
+    for copy in writes + [last]:
         copy.wait()
 
 
@@ -166,44 +170,48 @@
     )(x, w_gate, w_up, w_down)
 
 
-def halve_first_kernel(at_ref, own_ref, got_ref, keep_ref, send_ref):
+def halve_first_kernel(at_ref, own_ref, got_ref, mom_ref, keep_ref, send_ref, scratch):
     core, bit = at_ref[0], at_ref[1]
-    half, width = got_ref.shape[1], keep_ref.shape[1]
+    half, (count, rows, width) = got_ref.shape[1], keep_ref.shape
     for ref, which in ((send_ref, 1 - bit), (keep_ref, bit)):
-        mine = own_ref[0, :, pl.ds(pl.multiple_of(core * half + which * width, width), width)]
-        other = got_ref[:, pl.ds(pl.multiple_of(which * width, width), width)]
-        ref[...] = (mine + other).astype(ref.dtype)
-
-
-def halve_kernel(at_ref, own_ref, got_ref, keep_ref, send_ref):
-    bit, width = at_ref[2], keep_ref.shape[1]
+        for b in range(count):
+            at_rows, first = pl.ds((b & 1) * rows, rows), which * (half // 2) + (b >> 1) * width
+            mine = own_ref[0, at_rows, pl.ds(pl.multiple_of(core * half + first, width), width)]
+            other = got_ref[at_rows, pl.ds(pl.multiple_of(first, width), width)]
+            ref[b] = (mine + other).astype(ref.dtype)
+    wide, tall = mom_ref.shape
+    scratch[...] = jnp.zeros_like(scratch)
+    scratch[0:wide, 0:tall] = mom_ref[...]
+    mom = scratch[...].T
+    mom = jnp.concatenate([mom[0:rows, 0:wide], mom[rows : 2 * rows, 0:wide]], axis=1)
+    send_ref[count] = mom.astype(bf16)
+
+
+def halve_kernel(at_ref, own_ref, sent_ref, got_ref, keep_ref, send_ref):
+    bit, count = at_ref[2], keep_ref.shape[0]
     for ref, which in ((send_ref, 1 - bit), (keep_ref, bit)):
-        cols = pl.ds(pl.multiple_of(which * width, width), width)
-        ref[...] = (own_ref[:, cols] + got_ref[:, cols].astype(f32)).astype(ref.dtype)
-
-
-def add_z_first_kernel(own_ref, got_ref, mom_ref, keep_ref, send_ref):
-    rows = send_ref.shape[1]
-    total = own_ref[...] + got_ref[...].astype(f32)
-    for p in range(4):
-        keep_ref[p] = total[(p & 1) * rows : (p & 1) * rows + rows, (p >> 1) * 128 : (p >> 1) * 128 + 128]
-    send_ref[0:4] = keep_ref[...].astype(bf16)
-    send_ref[4] = mom_ref[...].astype(bf16)
+        for b in range(count):
+            i = which * count + b
+            ref[b] = (own_ref[i] + got_ref[i].astype(f32)).astype(ref.dtype)
+    send_ref[count] = sent_ref[2 * count]
+    send_ref[count + 1] = got_ref[2 * count]
 
 
 def add_z_kernel(own_ref, sent_ref, got_ref, keep_ref, send_ref):
-    total = own_ref[...] + got_ref[0:4].astype(f32)
+    count, held = keep_ref.shape[0], sent_ref.shape[0] - keep_ref.shape[0]
+    total = own_ref[...] + got_ref[0:count].astype(f32)
     keep_ref[...] = total
-    send_ref[0:4] = total.astype(bf16)
-    send_ref[4] = sent_ref[4]
-    send_ref[5] = got_ref[4]
-
-
-def mean_kernel(replicas, own_ref, sent_ref, got_ref, out_ref):
-    total = own_ref[...] + got_ref[0:4].astype(f32)
-    out_ref[0, 0:4] = (total * (1.0 / replicas)).astype(bf16)
-    out_ref[0, 4:6] = sent_ref[4:6]
-    out_ref[0, 6:8] = got_ref[4:6]
+    send_ref[0:count] = total.astype(bf16)
+    send_ref[count : count + held] = sent_ref[count:]
+    send_ref[count + held :] = got_ref[count:]
+
+
+def mean_kernel(replicas, own_ref, sent_ref, got_ref, out_ref, mom_ref):
+    count, held = own_ref.shape[0], sent_ref.shape[0] - own_ref.shape[0]
+    total = own_ref[...] + got_ref[0:count].astype(f32)
+    out_ref[0] = (total * (1.0 / replicas)).astype(bf16)
+    mom_ref[0:held] = sent_ref[count:]
+    mom_ref[held:] = got_ref[count:]
 
 
 def square_kernel(a_ref, b_ref, out_ref):
@@ -223,8 +231,15 @@
     return ((y & 1) ^ (y >> 1)) * 2 + (y >> 1)
 
 
-def outer_kernel(entries, at_ref, near_s, far_s, near_ref, far_ref, params_ref, local_ref, mom_ref, next_ref, mom_out, scratch):
-    core, quarter, zh, rep = at_ref[0], at_ref[3], at_ref[4], at_ref[5]
+def flips(apart):
+    high = jnp.right_shift(apart, 1)
+    return high * 2 + jnp.bitwise_xor(jnp.bitwise_and(apart, 1), high)
+
+
+def outer_kernel(
+    entries, at_ref, near_s, far_s, near_ref, far_ref, near_m, far_m, params_ref, local_ref, mom_ref, next_ref, mom_out, scratch
+):
+    core, quarter, zh, rep, y = at_ref[0], at_ref[3], at_ref[4], at_ref[5], at_ref[6]
     squares = near_s[...] + far_s[...]
     squares = jnp.sum(jnp.sum(squares, axis=1, keepdims=True), axis=0, keepdims=True)
     clip = jnp.minimum(1.0, lax.rsqrt(squares * (1.0 / entries) + clip_epsilon))
@@ -236,11 +251,8 @@
         )
 
     for cb in range(16):
-        j = jnp.bitwise_xor(quarter_of(cb & 3), quarter)
-        apart = jnp.bitwise_xor(zh, cb >> 2)
-        high = jnp.right_shift(apart, 1)
-        slot = 4 + high * 2 + jnp.bitwise_xor(jnp.bitwise_and(apart, 1), high)
-        near, far = near_ref[j, slot].astype(f32), far_ref[j, slot].astype(f32)
+        slot = flips(jnp.bitwise_xor(zh, cb >> 2)) * 4 + flips(jnp.bitwise_xor(y, cb & 3))
+        near, far = near_m[slot].astype(f32), far_m[slot].astype(f32)
         m0, m1 = jnp.where(core == 0, near, far), jnp.where(core == 0, far, near)
         for h in range(2):
             rows, cols = pl.ds(h * 48, 48), pl.ds(cb * 128, 128)
@@ -274,47 +286,43 @@
     core, y, zh = lax.axis_index("c"), lax.axis_index("y"), lax.axis_index("zh")
     rep = (zh * 4 + y) * 2 + core
     first, second = (y & 1) ^ (y >> 1), y >> 1
-    at = jnp.stack([core, first, second, first * 2 + second, zh, rep]).astype(jnp.int32)
+    at = jnp.stack([core, first, second, first * 2 + second, zh, rep, y]).astype(jnp.int32)
     half = width // 2
+    part = (rows // 2, 128)
+
+    def pair(held, sent):
+        return [jax.ShapeDtypeStruct((held,) + part, f32), jax.ShapeDtypeStruct((sent,) + part, bf16)]
+
     got = swap(lax.dynamic_slice_in_dim(pseudo_grad[0], (1 - core) * half, half, 1), "c", 1)
     keep, send = pl.pallas_call(
         halve_first_kernel,
-        in_specs=[smem()] + whole(2),
+        in_specs=[smem()] + whole(3),
         out_specs=whole(2),
-        out_shape=[jax.ShapeDtypeStruct((rows, half // 2), t) for t in (f32, bf16)],
+        out_shape=pair(8, 9),
+        scratch_shapes=[pltpu.VMEM((128, 128), f32)],
         compiler_params=params(),
         name="delta_halve_first",
-    )(at, pseudo_grad, got)
+    )(at, pseudo_grad, got, momentum.T)
     outgoing, keep, send = lax.optimization_barrier((outgoing, keep, send))
     got = swap(send, "y", 1)
     keep, send = pl.pallas_call(
         halve_kernel,
-        in_specs=[smem()] + whole(2),
+        in_specs=[smem()] + whole(3),
         out_specs=whole(2),
-        out_shape=[jax.ShapeDtypeStruct((rows, half // 4), t) for t in (f32, bf16)],
+        out_shape=pair(4, 6),
         compiler_params=params(),
         name="delta_halve",
-    )(at, keep, got)
-    got = swap(send, "y", 3)
-    part = (rows // 2, half // 8)
-    mom_block = jnp.concatenate([momentum[: rows // 2], momentum[rows // 2 :]], axis=1)
-    keep, send = pl.pallas_call(
-        add_z_first_kernel,
-        in_specs=whole(3),
-        out_specs=whole(2),
-        out_shape=[jax.ShapeDtypeStruct((4,) + part, f32), jax.ShapeDtypeStruct((5,) + part, bf16)],
-        compiler_params=params(),
-        name="delta_add_z_first",
-    )(keep, got, mom_block)
-    got = swap(send, "zh", 1)
-    keep, send = pl.pallas_call(
-        add_z_kernel,
-        in_specs=whole(3),
-        out_specs=whole(2),
-        out_shape=[jax.ShapeDtypeStruct((4,) + part, f32), jax.ShapeDtypeStruct((6,) + part, bf16)],
-        compiler_params=params(),
-        name="delta_add_z",
-    )(keep, send, got)
+    )(at, keep, send, got)
+    for axis, bits, sent in (("y", 3, 8), ("zh", 1, 12)):
+        got = swap(send, axis, bits)
+        keep, send = pl.pallas_call(
+            add_z_kernel,
+            in_specs=whole(3),
+            out_specs=whole(2),
+            out_shape=pair(4, sent),
+            compiler_params=params(),
+            name="delta_add_" + axis,
+        )(keep, send, got)
     return at, outgoing, keep, send
 
 
@@ -323,15 +331,19 @@
     return pl.pallas_call(
         lambda *refs: mean_kernel(32, *refs),
         in_specs=whole(3),
-        out_specs=whole(1)[0],
-        out_shape=jax.ShapeDtypeStruct((1, 8) + part, bf16),
+        out_specs=whole(2),
+        out_shape=[
+            jax.ShapeDtypeStruct((1, 4) + part, bf16),
+            jax.ShapeDtypeStruct((16,) + part, bf16),
+        ],
         compiler_params=params(),
         name="delta_mean",
     )(keep, send, got)
 
 
-def outer_finish(moe_out, at, block, global_params, momentum, local_params):
+def outer_finish(moe_out, at, block, mom_near, global_params, momentum, local_params):
     rows, width = global_params.shape
+    mom_far = swap(mom_near, "c", 1)
     block = jnp.concatenate([block, swap(block, "y", 3)], axis=0)
     block = jnp.concatenate([block, swap(block, "y", 1)], axis=0)
     far = swap(block, "c", 1)
@@ -350,7 +362,7 @@
     apart, moe_out = lax.optimization_barrier((apart, moe_out))
     local_next, momentum_next = pl.pallas_call(
         lambda *refs: outer_kernel(entries, *refs),
-        in_specs=[smem()] + whole(7),
+        in_specs=[smem()] + whole(9),
         out_specs=whole(2),
         out_shape=[
             jax.ShapeDtypeStruct((1, rows, width), bf16),
@@ -359,7 +371,7 @@
         scratch_shapes=[pltpu.VMEM((128, 128), f32)],
         compiler_params=params(),
         name="outer_update",
-    )(at, squares, apart, block, far, global_params, local_params, momentum.T)
+    )(at, squares, apart, block, far, mom_near, mom_far, global_params, local_params, momentum.T)
     return momentum_next.T, local_next, moe_out
 
 
@@ -369,20 +381,23 @@
     tok_rows, feat_width = tokens.shape
     capacity = tok_rows * 3 // 8
     routes_t, weight_t = routes.T, route_weight.T
-    outgoing = pl.pallas_call(
+    outgoing, routes_t, weight_t = pl.pallas_call(
         dispatch_kernel,
-        in_specs=[pl.BlockSpec(memory_space=pl.ANY)] * 2,
-        out_specs=pl.BlockSpec(memory_space=pl.ANY),
-        out_shape=jax.ShapeDtypeStruct((EXPERTS, capacity, feat_width), bf16),
+        in_specs=[pl.BlockSpec(memory_space=pl.ANY)] * 3,
+        out_specs=[pl.BlockSpec(memory_space=pl.ANY)] + whole(2),
+        out_shape=[
+            jax.ShapeDtypeStruct((EXPERTS, capacity, feat_width), bf16),
+            jax.ShapeDtypeStruct(routes_t.shape, jnp.int32),
+            jax.ShapeDtypeStruct(weight_t.shape, f32),
+        ],
         scratch_shapes=[
-            pltpu.VMEM(routes_t.shape, jnp.int32),
             pltpu.VMEM(tokens.shape, bf16),
             pltpu.VMEM((EXPERTS, capacity, feat_width), bf16),
-            pltpu.SemaphoreType.DMA((1 + 2 * (feat_width // 512),)),
+            pltpu.SemaphoreType.DMA((2 + 2 * (feat_width // 512),)),
         ],
         compiler_params=pltpu.CompilerParams(vmem_limit_bytes=DISPATCH_LIMIT),
         name="dispatch",
-    )(routes_t, tokens)
+    )(routes_t, tokens, weight_t)
     at, outgoing, keep, send = outer_sum(pseudo_grad, momentum, outgoing)
     received = lax.all_to_all(outgoing, SHARD, split_axis=0, concat_axis=0, tiled=True)
     received, keep, send = lax.optimization_barrier((received, keep, send))
@@ -398,8 +413,8 @@
         compiler_params=params(),
         name="combine",
     )(routes_t, weight_t, returned.reshape(EXPERTS * capacity, feat_width))
-    block = outer_mean(keep, send, got)
-    momentum_next, local_next, moe_out = outer_finish(moe_out, at, block, global_params, momentum, local_params)
+    block, mom_near = outer_mean(keep, send, got)
+    momentum_next, local_next, moe_out = outer_finish(moe_out, at, block, mom_near, global_params, momentum, local_params)
     return (moe_out, momentum_next, local_next)
 
 

time: 79.1 us -> 83 us (1.049)
  waiting for transfers between devices: 35.4 us -> 39.8 us
  starting transfers between devices: 25.2 us -> 23.5 us
    ppermute x11 -> x12, waiting for transfers between devices: 31.3 us -> 35.8 us  [swap(): return lax.ppermute(value, axis, [(i, i ^ bits) for i in range(size)])]
    ppermute x11 -> x12, starting transfers between devices: 15.9 us -> 14 us  [swap(): return lax.ppermute(value, axis, [(i, i ^ bits) for i in range(size)])]
  transfers between devices with their start and end apart: 13 -> 14, of which waited for: 9 -> 10; matrix products, arithmetic and copies ran while one was open for 1% -> 0% of each run, Pallas kernels for 16% -> 16%
where the time goes in v5:
time: 83 us; the launch traced here: 82.6 us
  waiting for transfers between devices  39.8 us (48%)
  starting transfers between devices  23.5 us (28%)
  Pallas kernels  15.8 us (19%)
  local copies, waits for them, and re-layouts  2.68 us (3%)
    ppermute x12, waiting for transfers between devices, swap(): return lax.ppermute(value, axis, [(i, i ^ bits) for i in range(size)])  35.8 us
    ppermute x12, starting transfers between devices, swap(): return lax.ppermute(value, axis, [(i, i ^ bits) for i in range(size)])  14 us
    pallas_call x1, Pallas kernels, ffn(): pl.pallas_call(ffn_kernel, in_specs=whole(1) + [anywhere] * 3, out_specs=...  7.33 us
    all_to_all x1, starting transfers between devices, local(): lax.all_to_all(outgoing, SHARD, split_axis=0, concat_axis=0, tiled=True)  5.67 us
    all_to_all x1, waiting for transfers between devices, local(): lax.all_to_all(outgoing, SHARD, split_axis=0, concat_axis=0, tiled=True)  4 us
    all_to_all x1, starting transfers between devices, local(): lax.all_to_all(result, SHARD, split_axis=0, concat_axis=0, tiled=True)  3.88 us
    pallas_call x1, Pallas kernels, local(): pl.pallas_call(dispatch_kernel, in_specs=[pl.BlockSpec(memory_space=pl.AN...  3.39 us
    pallas_call x1, Pallas kernels, outer_finish(): pl.pallas_call(lambda *refs: outer_kernel(entries, *refs), in_specs=[smem...  1.86 us
  transfers between devices with their start and end apart: 14, of which 10 were waited for; matrix products, arithmetic and copies ran while one was open for 0% of the time, Pallas kernels for 16%

profile of v5, /device:TPU:24, one launch (start us, length us, event | category | flops | bytes accessed | tf_op | source)
XLA Modules:
  0.0 82.6 jit_solution(13263133692505071841)
XLA Ops:
  0.6 0.0 copy-start
  0.6 1.1 %dynamic-slice_bitcast_fusion = f32[96,1024]{1,0:T(8,128)S(1)} fusion(f32[1,96,2048]{2,1,0:T(8,128)} %own_ref.1, s32[]{:T(128)S(6)} %select_n.3), kind=kLoop, calls=%fused_computation | loop fusion | bytes 786436 | tf_op jit(solution)/shard_map/dynamic_slice | solution.py:296
  1.7 0.1 collective-permute-start
  1.9 3.4 %dispatch.1 = (bf16[8,48,2048]{2,1,0:T(8,128)(2,1)}, s32[2,128]{1,0:T(2,128)}, f32[2,128]{1,0:T(2,128)}) custom-call(s32[2,128]{1,0:T(2,128)} %bitcast.20, bf16[128,2048]{1,0:T(8,128)(2,1)} %tokens_hbm.1, f32[2,128]{1,0:T(2,128)} %bitcast.21), custom_call_target="tpu_custom_call" | custom-call | tf_op jit(solution)/shard_map/dispatch/pallas_call | solution.py:384
  5.3 0.1 stack.31.at_ref.refs_0_
  5.3 0.0 collective-permute-done.got_ref
  5.4 0.0 copy-done
  5.4 0.0 copy-start.3
  5.4 0.7 copy-done.3
  6.1 0.7 delta_halve_first.1
  6.8 5.7 %all-to-all-start = ((bf16[8,48,2048]{2,1,0:T(8,128)(2,1)}), bf16[8,48,2048]{2,1,0:T(8,128)(2,1)S(1)}, u32[]{:S(2)}, u32[]{:S(2)}) async-start(bf16[8,48,2048]{2,1,0:T(8,128)(2,1)} %get-tuple-element.31), calls=%async_computation | async-start | bytes 3145728 | tf_op jit(solution)/shard_map/all_to_all | solution.py:402
  12.5 0.7 collective-permute-start.1
  13.2 4.4 %collective-permute-done.1.got_ref = bf16[9,48,128]{2,1,0:T(8,128)(2,1)S(1)} collective-permute-done((bf16[9,48,128]{2,1,0:T(8,128)(2,1)S(1)}, bf16[9,48,128]{2,1,0:T(8,128)(2,1)S(1)}, u32[]{:S(2)}, u32[]{:S(2)}) %collective-permute-start.1) | collective-permute-done | bytes 110624 | tf_op jit(solution)/shard_map/ppermute | solution.py:281
  17.7 0.6 delta_halve.1
  18.3 0.3 collective-permute-start.2
  18.6 5.3 %collective-permute-done.2.got_ref = bf16[6,48,128]{2,1,0:T(8,128)(2,1)S(1)} collective-permute-done((bf16[6,48,128]{2,1,0:T(8,128)(2,1)S(1)}, bf16[6,48,128]{2,1,0:T(8,128)(2,1)S(1)}, u32[]{:S(2)}, u32[]{:S(2)}) %collective-permute-start.2) | collective-permute-done | bytes 73760 | tf_op jit(solution)/shard_map/ppermute | solution.py:281
  23.9 3.4 %collective-permute-start.3 = (bf16[8,48,128]{2,1,0:T(8,128)(2,1)S(1)}, bf16[8,48,128]{2,1,0:T(8,128)(2,1)S(1)}, u32[]{:S(2)}, u32[]{:S(2)}) collective-permute-start(bf16[8,48,128]{2,1,0:T(8,128)(2,1)S(1)} %get-tuple-element.37.sent_ref), channel_id=1, source_target_pairs={{0,64},{64,0},{128,192},{192,128},{1,65},{65,1},{129,193},{193,129... | collective-permute-start | bytes 294920 | tf_op jit(solution)/shard_map/ppermute | solution.py:281
  27.3 5.3 %collective-permute-done.3.got_ref = bf16[8,48,128]{2,1,0:T(8,128)(2,1)S(1)} collective-permute-done((bf16[8,48,128]{2,1,0:T(8,128)(2,1)S(1)}, bf16[8,48,128]{2,1,0:T(8,128)(2,1)S(1)}, u32[]{:S(2)}, u32[]{:S(2)}) %collective-permute-start.3) | collective-permute-done | bytes 98336 | tf_op jit(solution)/shard_map/ppermute | solution.py:281
  32.6 4.0 %all-to-all-done = bf16[8,48,2048]{2,1,0:T(8,128)(2,1)S(1)} async-done(((bf16[8,48,2048]{2,1,0:T(8,128)(2,1)}), bf16[8,48,2048]{2,1,0:T(8,128)(2,1)S(1)}, u32[]{:S(2)}, u32[]{:S(2)}) %all-to-all-start) | async-done | bytes 1572896 | tf_op jit(solution)/shard_map/all_to_all | solution.py:402
  36.6 4.0 %collective-permute-start.4 = (bf16[12,48,128]{2,1,0:T(8,128)(2,1)S(1)}, bf16[12,48,128]{2,1,0:T(8,128)(2,1)S(1)}, u32[]{:S(2)}, u32[]{:S(2)}) collective-permute-start(bf16[12,48,128]{2,1,0:T(8,128)(2,1)S(1)} %get-tuple-element.41.refs_1_), channel_id=1, source_target_pairs={{0,192},{64,128},{128,64},{192,0},{1,193},{65,129},{129,65},{193,1... | collective-permute-start | bytes 442376 | tf_op jit(solution)/shard_map/ppermute | solution.py:281
  40.7 7.3 %expert_ffn.1 = bf16[384,2048]{1,0:T(8,128)(2,1)} custom-call(bf16[384,2048]{1,0:T(8,128)(2,1)S(1)} %bitcast.17, bf16[1,2048,768]{2,1,0:T(8,128)(2,1)} %gate_hbm.1, bf16[1,2048,768]{2,1,0:T(8,128)(2,1)} %up_hbm.1, bf16[1,768,2048]{2,1,0:T(8,128)(2,1)} %down_hbm.1), custom_call_target="tpu_custom_call" | custom-call | flops 3623878656 | bytes 12582912 | tf_op jit(solution)/shard_map/expert_ffn/pallas_call | solution.py:149
  48.0 0.0 collective-permute-done.4.refs_2_
  48.0 0.0 copy-start.5
  48.0 3.9 %all-to-all-start.1 = ((bf16[8,48,2048]{2,1,0:T(8,128)(2,1)}), bf16[8,48,2048]{2,1,0:T(8,128)(2,1)S(1)}, u32[]{:S(2)}, u32[]{:S(2)}) async-start(bf16[8,48,2048]{2,1,0:T(8,128)(2,1)} %bitcast.12), calls=%async_computation.1 | async-start | bytes 3145728 | tf_op jit(solution)/shard_map/all_to_all | solution.py:407
  51.9 0.0 copy-start.1
  51.9 0.0 copy-start.2
  51.9 0.3 collective-permute-start.5
  52.2 5.1 %collective-permute-done.5 = bf16[1,4,48,128]{3,2,1,0:T(8,128)(2,1)S(1)} collective-permute-done((bf16[1,4,48,128]{3,2,1,0:T(8,128)(2,1)S(1)}, bf16[1,4,48,128]{3,2,1,0:T(8,128)(2,1)S(1)}, u32[]{:S(2)}, u32[]{:S(2)}) %collective-permute-start.5) | collective-permute-done | bytes 49184 | tf_op jit(solution)/shard_map/ppermute | solution.py:281
  57.4 0.1 collective-permute-start.6
  57.5 4.6 %collective-permute-done.6 = bf16[2,4,48,128]{3,2,1,0:T(8,128)(2,1)S(1)} collective-permute-done((bf16[2,4,48,128]{3,2,1,0:T(8,128)(2,1)S(1)}, bf16[2,4,48,128]{3,2,1,0:T(8,128)(2,1)S(1)}, u32[]{:S(2)}, u32[]{:S(2)}) %collective-permute-start.6) | collective-permute-done | bytes 98336 | tf_op jit(solution)/shard_map/ppermute | solution.py:281
  62.1 0.1 collective-permute-start.7
  62.2 0.5 collective-permute-start.11
  62.7 0.9 %collective-permute-done.7.b_ref.refs_4_ = bf16[4,4,48,128]{3,2,1,0:T(8,128)(2,1)S(1)} collective-permute-done((bf16[4,4,48,128]{3,2,1,0:T(8,128)(2,1)S(1)}, bf16[4,4,48,128]{3,2,1,0:T(8,128)(2,1)S(1)}, u32[]{:S(2)}, u32[]{:S(2)}) %collective-permute-start.7) | collective-permute-done | bytes 196640 | tf_op jit(solution)/shard_map/ppermute | solution.py:281
  63.6 0.2 delta_squares.1
  63.8 2.1 %collective-permute-start.8 = (f32[8,128]{1,0:T(8,128)S(1)}, f32[8,128]{1,0:T(8,128)S(1)}, u32[]{:S(2)}, u32[]{:S(2)}) collective-permute-start(f32[8,128]{1,0:T(8,128)S(1)} %delta_squares.1), channel_id=1, source_target_pairs={{0,1},{1,0},{2,3},{3,2},{4,5},{5,4},{6,7},{7,6},{8,9},{9,8},{10,11... | collective-permute-start | bytes 12296 | tf_op jit(solution)/shard_map/ppermute | solution.py:281
  65.9 6.4 %collective-permute-done.8 = f32[8,128]{1,0:T(8,128)S(1)} collective-permute-done((f32[8,128]{1,0:T(8,128)S(1)}, f32[8,128]{1,0:T(8,128)S(1)}, u32[]{:S(2)}, u32[]{:S(2)}) %collective-permute-start.8) | collective-permute-done | bytes 4128 | tf_op jit(solution)/shard_map/ppermute | solution.py:281
  72.3 0.6 collective-permute-start.9
  72.9 3.0 %collective-permute-done.9 = f32[8,128]{1,0:T(8,128)S(1)} collective-permute-done((f32[8,128]{1,0:T(8,128)S(1)}, f32[8,128]{1,0:T(8,128)S(1)}, u32[]{:S(2)}, u32[]{:S(2)}) %collective-permute-start.9) | collective-permute-done | bytes 4128 | tf_op jit(solution)/shard_map/ppermute | solution.py:281
  75.9 1.8 %collective-permute-start.10 = (f32[8,128]{1,0:T(8,128)S(1)}, f32[8,128]{1,0:T(8,128)S(1)}, u32[]{:S(2)}, u32[]{:S(2)}) collective-permute-start(f32[8,128]{1,0:T(8,128)S(1)} %add.23.refs_1_), channel_id=1, source_target_pairs={{0,6},{2,4},{4,2},{6,0},{1,7},{3,5},{5,3},{7,1},{8,14},{10,12},{12... | collective-permute-start | bytes 12296 | tf_op jit(solution)/shard_map/ppermute | solution.py:281
  77.7 0.0 all-to-all-done.1
  77.7 0.0 copy-start.4
  77.7 0.0 copy-done.5
  77.7 0.0 copy-start.6
  77.7 0.7 copy-done.6
  78.4 1.7 %combine.1 = bf16[128,2048]{1,0:T(8,128)(2,1)} custom-call(s32[2,128]{1,0:T(2,128)S(1)} %copy-done.5, f32[2,128]{1,0:T(2,128)S(1)} %copy-done.6, bf16[384,2048]{1,0:T(8,128)(2,1)S(1)} %bitcast.16), custom_call_target="tpu_custom_call" | custom-call | tf_op jit(solution)/shard_map/combine/pallas_call | solution.py:408
  80.1 0.6 collective-permute-done.10.refs_2_
  80.8 0.0 collective-permute-done.11.refs_6_
  80.8 0.0 copy-done.1
  80.8 0.0 copy-done.2
  80.8 0.0 copy-done.4
  80.8 1.9 %outer_update.1 = (bf16[1,96,2048]{2,1,0:T(8,128)(2,1)}, f32[64,96]{1,0:T(8,128)}) custom-call(s32[7]{0:T(128)S(1)} %stack.31.at_ref.refs_0_, f32[8,128]{1,0:T(8,128)S(1)} %add.23.refs_1_, f32[8,128]{1,0:T(8,128)S(1)} %collective-permute-done.10.refs_2_, bf16[4,4,48,128]{3,2,1,0:T(8,128)(2,1)S(1)} %constant_dynamic-update-slice_fusion.a_ref.refs_3_, ...), custom_call_target="tpu_custom_call" | custom-call | tf_op jit(solution)/shard_map/outer_update/pallas_call | solution.py:363
  (9 shorter events, 0.1 us)
Async XLA Ops:
  0.6 4.7 %copy-start = (f32[1,96,2048]{2,1,0:T(8,128)S(1)}, f32[1,96,2048]{2,1,0:T(8,128)}, u32[]{:S(2)}) copy-start(f32[1,96,2048]{2,1,0:T(8,128)} %own_ref.1) | copy-start | bytes 2359300
  1.7 3.6 %collective-permute-start = (f32[96,1024]{1,0:T(8,128)S(1)}, f32[96,1024]{1,0:T(8,128)S(1)}, u32[]{:S(2)}, u32[]{:S(2)}) collective-permute-start(f32[96,1024]{1,0:T(8,128)S(1)} %dynamic-slice_bitcast_fusion), channel_id=1, source_target_pairs={{0,8},{8,0},{1,9},{9,1},{2,10},{10,2},{3,11},{11,3},{4,12},{12,4},... | collective-permute-start | bytes 1179656 | tf_op jit(solution)/shard_map/ppermute | solution.py:281
  5.4 0.8 copy-start.3
  6.8 29.8 %all-to-all-start = ((bf16[8,48,2048]{2,1,0:T(8,128)(2,1)}), bf16[8,48,2048]{2,1,0:T(8,128)(2,1)S(1)}, u32[]{:S(2)}, u32[]{:S(2)}) async-start(bf16[8,48,2048]{2,1,0:T(8,128)(2,1)} %get-tuple-element.31), calls=%async_computation | async-start | bytes 3145728 | tf_op jit(solution)/shard_map/all_to_all | solution.py:402
  12.5 5.2 %collective-permute-start.1 = (bf16[9,48,128]{2,1,0:T(8,128)(2,1)S(1)}, bf16[9,48,128]{2,1,0:T(8,128)(2,1)S(1)}, u32[]{:S(2)}, u32[]{:S(2)}) collective-permute-start(bf16[9,48,128]{2,1,0:T(8,128)(2,1)S(1)} %get-tuple-element.33.sent_ref), channel_id=1, source_target_pairs={{0,16},{16,0},{32,48},{48,32},{1,17},{17,1},{33,49},{49,33},{2,18}... | collective-permute-start | bytes 331784 | tf_op jit(solution)/shard_map/ppermute | solution.py:281
  18.3 5.7 %collective-permute-start.2 = (bf16[6,48,128]{2,1,0:T(8,128)(2,1)S(1)}, bf16[6,48,128]{2,1,0:T(8,128)(2,1)S(1)}, u32[]{:S(2)}, u32[]{:S(2)}) collective-permute-start(bf16[6,48,128]{2,1,0:T(8,128)(2,1)S(1)} %get-tuple-element.35.sent_ref), channel_id=1, source_target_pairs={{0,48},{16,32},{32,16},{48,0},{1,49},{17,33},{33,17},{49,1},{2,50}... | collective-permute-start | bytes 221192 | tf_op jit(solution)/shard_map/ppermute | solution.py:281
  23.9 8.7 %collective-permute-start.3 = (bf16[8,48,128]{2,1,0:T(8,128)(2,1)S(1)}, bf16[8,48,128]{2,1,0:T(8,128)(2,1)S(1)}, u32[]{:S(2)}, u32[]{:S(2)}) collective-permute-start(bf16[8,48,128]{2,1,0:T(8,128)(2,1)S(1)} %get-tuple-element.37.sent_ref), channel_id=1, source_target_pairs={{0,64},{64,0},{128,192},{192,128},{1,65},{65,1},{129,193},{193,129... | collective-permute-start | bytes 294920 | tf_op jit(solution)/shard_map/ppermute | solution.py:281
  36.6 11.4 %collective-permute-start.4 = (bf16[12,48,128]{2,1,0:T(8,128)(2,1)S(1)}, bf16[12,48,128]{2,1,0:T(8,128)(2,1)S(1)}, u32[]{:S(2)}, u32[]{:S(2)}) collective-permute-start(bf16[12,48,128]{2,1,0:T(8,128)(2,1)S(1)} %get-tuple-element.41.refs_1_), channel_id=1, source_target_pairs={{0,192},{64,128},{128,64},{192,0},{1,193},{65,129},{129,65},{193,1... | collective-permute-start | bytes 442376 | tf_op jit(solution)/shard_map/ppermute | solution.py:281
  48.0 29.7 %copy-start.5 = (s32[2,128]{1,0:T(2,128)S(1)}, s32[2,128]{1,0:T(2,128)}, u32[]{:S(2)}) copy-start(s32[2,128]{1,0:T(2,128)} %get-tuple-element.45.routes_ref) | copy-start | bytes 3076
  48.0 29.7 %all-to-all-start.1 = ((bf16[8,48,2048]{2,1,0:T(8,128)(2,1)}), bf16[8,48,2048]{2,1,0:T(8,128)(2,1)S(1)}, u32[]{:S(2)}, u32[]{:S(2)}) async-start(bf16[8,48,2048]{2,1,0:T(8,128)(2,1)} %bitcast.12), calls=%async_computation.1 | async-start | bytes 3145728 | tf_op jit(solution)/shard_map/all_to_all | solution.py:407
  51.9 28.8 %copy-start.1 = (f32[96,2048]{1,0:T(8,128)S(1)}, f32[96,2048]{1,0:T(8,128)}, u32[]{:S(2)}) copy-start(f32[96,2048]{1,0:T(8,128)} %refs_7_.1) | copy-start | bytes 2359300
  51.9 28.8 %copy-start.2 = (bf16[1,96,2048]{2,1,0:T(8,128)(2,1)S(1)}, bf16[1,96,2048]{2,1,0:T(8,128)(2,1)}, u32[]{:S(2)}) copy-start(bf16[1,96,2048]{2,1,0:T(8,128)(2,1)} %refs_8_.1) | copy-start | bytes 1179652
  51.9 5.4 %collective-permute-start.5 = (bf16[1,4,48,128]{3,2,1,0:T(8,128)(2,1)S(1)}, bf16[1,4,48,128]{3,2,1,0:T(8,128)(2,1)S(1)}, u32[]{:S(2)}, u32[]{:S(2)}) collective-permute-start(bf16[1,4,48,128]{3,2,1,0:T(8,128)(2,1)S(1)} %get-tuple-element.44), channel_id=1, source_target_pairs={{0,48},{16,32},{32,16},{48,0},{1,49},{17,33},{33,17},{49,1},{2,50}... | collective-permute-start | bytes 147464 | tf_op jit(solution)/shard_map/ppermute | solution.py:281
  57.4 4.7 %collective-permute-start.6 = (bf16[2,4,48,128]{3,2,1,0:T(8,128)(2,1)S(1)}, bf16[2,4,48,128]{3,2,1,0:T(8,128)(2,1)S(1)}, u32[]{:S(2)}, u32[]{:S(2)}) collective-permute-start(bf16[2,4,48,128]{3,2,1,0:T(8,128)(2,1)S(1)} %pad_maximum_fusion), channel_id=1, source_target_pairs={{0,16},{16,0},{32,48},{48,32},{1,17},{17,1},{33,49},{49,33},{2,18}... | collective-permute-start | bytes 294920 | tf_op jit(solution)/shard_map/ppermute | solution.py:281
  62.1 1.5 %collective-permute-start.7 = (bf16[4,4,48,128]{3,2,1,0:T(8,128)(2,1)S(1)}, bf16[4,4,48,128]{3,2,1,0:T(8,128)(2,1)S(1)}, u32[]{:S(2)}, u32[]{:S(2)}) collective-permute-start(bf16[4,4,48,128]{3,2,1,0:T(8,128)(2,1)S(1)} %constant_dynamic-update-slice_fusion.a_ref.refs_3_), channel_id=1, source_target_pairs={{0,8},{8,0},{1,9},{9,1},{2,10},{10,2},{3,11},{11,3},{4,12},{12,4},... | collective-permute-start | bytes 589832 | tf_op jit(solution)/shard_map/ppermute | solution.py:281
  62.2 18.6 %collective-permute-start.11 = (bf16[16,48,128]{2,1,0:T(8,128)(2,1)S(1)}, bf16[16,48,128]{2,1,0:T(8,128)(2,1)S(1)}, u32[]{:S(2)}, u32[]{:S(2)}) collective-permute-start(bf16[16,48,128]{2,1,0:T(8,128)(2,1)S(1)} %get-tuple-element.50.refs_5_), channel_id=1, source_target_pairs={{0,8},{8,0},{1,9},{9,1},{2,10},{10,2},{3,11},{11,3},{4,12},{12,4},... | collective-permute-start | bytes 589832 | tf_op jit(solution)/shard_map/ppermute | solution.py:281
  63.8 8.5 %collective-permute-start.8 = (f32[8,128]{1,0:T(8,128)S(1)}, f32[8,128]{1,0:T(8,128)S(1)}, u32[]{:S(2)}, u32[]{:S(2)}) collective-permute-start(f32[8,128]{1,0:T(8,128)S(1)} %delta_squares.1), channel_id=1, source_target_pairs={{0,1},{1,0},{2,3},{3,2},{4,5},{5,4},{6,7},{7,6},{8,9},{9,8},{10,11... | collective-permute-start | bytes 12296 | tf_op jit(solution)/shard_map/ppermute | solution.py:281
  72.3 3.6 %collective-permute-start.9 = (f32[8,128]{1,0:T(8,128)S(1)}, f32[8,128]{1,0:T(8,128)S(1)}, u32[]{:S(2)}, u32[]{:S(2)}) collective-permute-start(f32[8,128]{1,0:T(8,128)S(1)} %add.22), channel_id=1, source_target_pairs={{0,2},{2,0},{4,6},{6,4},{1,3},{3,1},{5,7},{7,5},{8,10},{10,8},{12,... | collective-permute-start | bytes 12296 | tf_op jit(solution)/shard_map/ppermute | solution.py:281
  75.9 4.8 %collective-permute-start.10 = (f32[8,128]{1,0:T(8,128)S(1)}, f32[8,128]{1,0:T(8,128)S(1)}, u32[]{:S(2)}, u32[]{:S(2)}) collective-permute-start(f32[8,128]{1,0:T(8,128)S(1)} %add.23.refs_1_), channel_id=1, source_target_pairs={{0,6},{2,4},{4,2},{6,0},{1,7},{3,5},{5,3},{7,1},{8,14},{10,12},{12... | collective-permute-start | bytes 12296 | tf_op jit(solution)/shard_map/ppermute | solution.py:281
  77.7 3.1 %copy-start.4 = (f32[96,64]{0,1:T(8,128)S(1)}, f32[96,64]{0,1:T(8,128)}, u32[]{:S(2)}) copy-start(f32[96,64]{0,1:T(8,128)} %param.18) | copy-start | bytes 73732
  77.7 0.7 copy-start.6

commit v6 on v3

--- a/solution.py
+++ b/solution.py
@@ -269,7 +269,7 @@
     return lax.ppermute(value, axis, [(i, i ^ bits) for i in range(size)])
 
 
-def outer_sum(pseudo_grad, momentum, outgoing):
+def outer_sum(pseudo_grad, momentum):
     rows, width = pseudo_grad.shape[1:]
     core, y, zh = lax.axis_index("c"), lax.axis_index("y"), lax.axis_index("zh")
     rep = (zh * 4 + y) * 2 + core
@@ -285,7 +285,6 @@
         compiler_params=params(),
         name="delta_halve_first",
     )(at, pseudo_grad, got)
-    outgoing, keep, send = lax.optimization_barrier((outgoing, keep, send))
     got = swap(send, "y", 1)
     keep, send = pl.pallas_call(
         halve_kernel,
@@ -315,7 +314,7 @@
         compiler_params=params(),
         name="delta_add_z",
     )(keep, send, got)
-    return at, outgoing, keep, send
+    return at, keep, send
 
 
 def outer_mean(keep, send, got):
@@ -343,7 +342,9 @@
         compiler_params=params(),
         name="delta_squares",
     )(block, far)
-    squares = squares + swap(squares, "zl", 1)
+    squares = squares + lax.ppermute(
+        squares, ("zh", "zl"), [(z, (z + 1 if z % 2 else z - 1) % 8) for z in range(8)]
+    )
     squares = squares + swap(squares, "x", 1)
     entries = float(rows * 8 * width)
     apart = swap(squares, "x", 3)
@@ -383,7 +384,7 @@
         compiler_params=pltpu.CompilerParams(vmem_limit_bytes=DISPATCH_LIMIT),
         name="dispatch",
     )(routes_t, tokens)
-    at, outgoing, keep, send = outer_sum(pseudo_grad, momentum, outgoing)
+    at, keep, send = outer_sum(pseudo_grad, momentum)
     received = lax.all_to_all(outgoing, SHARD, split_axis=0, concat_axis=0, tiled=True)
     received, keep, send = lax.optimization_barrier((received, keep, send))
     result = ffn(received.reshape(EXPERTS * capacity, feat_width), w_gate, w_up, w_down)

time: 79.1 us -> 77.6 us (0.981)
  waiting for transfers between devices: 35.4 us -> 34.2 us
  local copies, waits for them, and re-layouts: 2.12 us -> 1.05 us
  starting transfers between devices: 25.2 us -> 26.1 us
    ppermute x11 -> x10, waiting for transfers between devices: 31.3 us -> 27.5 us  [swap(): return lax.ppermute(value, axis, [(i, i ^ bits) for i in range(size)])]
    ppermute x0 -> x1, waiting for transfers between devices: none -> 3.07 us  [outer_finish(): lax.ppermute(squares, ('zh', 'zl'), [(z, (z + 1 if z % 2 else z - 1) % 8)...]
    ppermute x0 -> x1, starting transfers between devices: none -> 1.83 us  [outer_finish(): lax.ppermute(squares, ('zh', 'zl'), [(z, (z + 1 if z % 2 else z - 1) % 8)...]
    dynamic_slice x1, local copies, waits for them, and re-layouts: 1.1 us -> 0.03 us  [outer_sum(): lax.dynamic_slice_in_dim(pseudo_grad[0], (1 - core) * half, half, 1)]
    ppermute x11 -> x10, starting transfers between devices: 15.9 us -> 14.9 us  [swap(): return lax.ppermute(value, axis, [(i, i ^ bits) for i in range(size)])]
  transfers between devices with their start and end apart: 13 -> 13, of which waited for: 9 -> 10; matrix products, arithmetic and copies ran while one was open for 1% -> 1% of each run, Pallas kernels for 16% -> 13%
where the time goes in v6:
time: 77.6 us; the launch traced here: 77.3 us
  waiting for transfers between devices  34.2 us (44%)
  starting transfers between devices  26.1 us (34%)
  Pallas kernels  15 us (19%)
  local copies, waits for them, and re-layouts  1.05 us (1%)
  between operations  0.82 us (1%)
    ppermute x10, waiting for transfers between devices, swap(): return lax.ppermute(value, axis, [(i, i ^ bits) for i in range(size)])  27.5 us
    ppermute x10, starting transfers between devices, swap(): return lax.ppermute(value, axis, [(i, i ^ bits) for i in range(size)])  14.9 us
    pallas_call x1, Pallas kernels, ffn(): pl.pallas_call(ffn_kernel, in_specs=whole(1) + [anywhere] * 3, out_specs=...  7.28 us
    all_to_all x1, starting transfers between devices, local(): lax.all_to_all(outgoing, SHARD, split_axis=0, concat_axis=0, tiled=True)  5.78 us
    all_to_all x1, waiting for transfers between devices, local(): lax.all_to_all(outgoing, SHARD, split_axis=0, concat_axis=0, tiled=True)  3.63 us
    all_to_all x1, starting transfers between devices, local(): lax.all_to_all(result, SHARD, split_axis=0, concat_axis=0, tiled=True)  3.59 us
    ppermute x1, waiting for transfers between devices, outer_finish(): lax.ppermute(squares, ('zh', 'zl'), [(z, (z + 1 if z % 2 else z - 1) % 8)...  3.07 us
    pallas_call x1, Pallas kernels, local(): pl.pallas_call(dispatch_kernel, in_specs=[pl.BlockSpec(memory_space=pl.AN...  2.8 us
  transfers between devices with their start and end apart: 13, of which 10 were waited for; matrix products, arithmetic and copies ran while one was open for 1% of the time, Pallas kernels for 13%

profile of v6, /device:TPU:24, one launch (start us, length us, event | category | flops | bytes accessed | tf_op | source)
XLA Modules:
  0.0 77.3 jit_solution(15650294917390545542)
XLA Ops:
  0.6 2.8 %dispatch.1 = bf16[8,48,2048]{2,1,0:T(8,128)(2,1)} custom-call(s32[2,128]{1,0:T(2,128)} %bitcast.18, bf16[128,2048]{1,0:T(8,128)(2,1)} %tokens_hbm.1), custom_call_target="tpu_custom_call" | custom-call | tf_op jit(solution)/shard_map/dispatch/pallas_call | solution.py:373
  3.4 0.0 copy-start
  3.4 5.8 %all-to-all-start = ((bf16[8,48,2048]{2,1,0:T(8,128)(2,1)}), bf16[8,48,2048]{2,1,0:T(8,128)(2,1)S(1)}, u32[]{:S(2)}, u32[]{:S(2)}) async-start(bf16[8,48,2048]{2,1,0:T(8,128)(2,1)} %dispatch.1), calls=%async_computation | async-start | bytes 3145728 | tf_op jit(solution)/shard_map/all_to_all | solution.py:388
  9.2 0.0 copy-start.3
  9.2 0.0 copy-done
  9.3 0.1 collective-permute-start
  9.4 0.1 stack.27.at_ref.refs_0_
  9.5 1.6 %collective-permute-done.got_ref = f32[96,1024]{1,0:T(8,128)S(1)} collective-permute-done((f32[96,1024]{1,0:T(8,128)S(1)}, f32[96,1024]{1,0:T(8,128)S(1)}, u32[]{:S(2)}, u32[]{:S(2)}) %collective-permute-start) | collective-permute-done | bytes 393248 | tf_op jit(solution)/shard_map/ppermute | solution.py:269
  11.1 0.6 delta_halve_first.1
  11.7 0.8 %collective-permute-start.1 = (bf16[96,512]{1,0:T(8,128)(2,1)S(1)}, bf16[96,512]{1,0:T(8,128)(2,1)S(1)}, u32[]{:S(2)}, u32[]{:S(2)}) collective-permute-start(bf16[96,512]{1,0:T(8,128)(2,1)S(1)} %get-tuple-element.21), channel_id=1, source_target_pairs={{0,16},{16,0},{32,48},{48,32},{1,17},{17,1},{33,49},{49,33},{2,18}... | collective-permute-start | bytes 294920 | tf_op jit(solution)/shard_map/ppermute | solution.py:269
  12.5 0.0 copy-done.3
  12.5 0.1 fusion
  12.6 0.1 copy.15
  12.7 0.1 copy.16
  12.8 3.9 %collective-permute-done.1.got_ref = bf16[96,512]{1,0:T(8,128)(2,1)S(1)} collective-permute-done((bf16[96,512]{1,0:T(8,128)(2,1)S(1)}, bf16[96,512]{1,0:T(8,128)(2,1)S(1)}, u32[]{:S(2)}, u32[]{:S(2)}) %collective-permute-start.1) | collective-permute-done | bytes 98336 | tf_op jit(solution)/shard_map/ppermute | solution.py:269
  16.6 0.6 delta_halve.1
  17.2 0.3 collective-permute-start.2
  17.5 0.1 pad_maximum_fusion.2.mom_ref
  17.6 5.0 %collective-permute-done.2.got_ref = bf16[96,256]{1,0:T(8,128)(2,1)S(1)} collective-permute-done((bf16[96,256]{1,0:T(8,128)(2,1)S(1)}, bf16[96,256]{1,0:T(8,128)(2,1)S(1)}, u32[]{:S(2)}, u32[]{:S(2)}) %collective-permute-start.2) | collective-permute-done | bytes 49184 | tf_op jit(solution)/shard_map/ppermute | solution.py:269
  22.6 3.4 %collective-permute-start.3 = (bf16[5,48,128]{2,1,0:T(8,128)(2,1)S(1)}, bf16[5,48,128]{2,1,0:T(8,128)(2,1)S(1)}, u32[]{:S(2)}, u32[]{:S(2)}) collective-permute-start(bf16[5,48,128]{2,1,0:T(8,128)(2,1)S(1)} %get-tuple-element.25.sent_ref), channel_id=1, source_target_pairs={{0,64},{64,0},{128,192},{192,128},{1,65},{65,1},{129,193},{193,129... | collective-permute-start | bytes 184328 | tf_op jit(solution)/shard_map/ppermute | solution.py:269
  26.0 2.3 %collective-permute-done.3.got_ref = bf16[5,48,128]{2,1,0:T(8,128)(2,1)S(1)} collective-permute-done((bf16[5,48,128]{2,1,0:T(8,128)(2,1)S(1)}, bf16[5,48,128]{2,1,0:T(8,128)(2,1)S(1)}, u32[]{:S(2)}, u32[]{:S(2)}) %collective-permute-start.3) | collective-permute-done | bytes 61472 | tf_op jit(solution)/shard_map/ppermute | solution.py:269
  28.3 3.6 %all-to-all-done = bf16[8,48,2048]{2,1,0:T(8,128)(2,1)S(1)} async-done(((bf16[8,48,2048]{2,1,0:T(8,128)(2,1)}), bf16[8,48,2048]{2,1,0:T(8,128)(2,1)S(1)}, u32[]{:S(2)}, u32[]{:S(2)}) %all-to-all-start) | async-done | bytes 1572896 | tf_op jit(solution)/shard_map/all_to_all | solution.py:388
  31.9 4.8 %collective-permute-start.4 = (bf16[6,48,128]{2,1,0:T(8,128)(2,1)S(1)}, bf16[6,48,128]{2,1,0:T(8,128)(2,1)S(1)}, u32[]{:S(2)}, u32[]{:S(2)}) collective-permute-start(bf16[6,48,128]{2,1,0:T(8,128)(2,1)S(1)} %get-tuple-element.29.refs_1_), channel_id=1, source_target_pairs={{0,192},{64,128},{128,64},{192,0},{1,193},{65,129},{129,65},{193,1... | collective-permute-start | bytes 221192 | tf_op jit(solution)/shard_map/ppermute | solution.py:269
  36.7 7.3 %expert_ffn.1 = bf16[384,2048]{1,0:T(8,128)(2,1)} custom-call(bf16[384,2048]{1,0:T(8,128)(2,1)S(1)} %bitcast.16, bf16[1,2048,768]{2,1,0:T(8,128)(2,1)} %gate_hbm.1, bf16[1,2048,768]{2,1,0:T(8,128)(2,1)} %up_hbm.1, bf16[1,768,2048]{2,1,0:T(8,128)(2,1)} %down_hbm.1), custom_call_target="tpu_custom_call" | custom-call | flops 3623878656 | bytes 12582912 | tf_op jit(solution)/shard_map/expert_ffn/pallas_call | solution.py:145
  44.0 0.0 collective-permute-done.4.refs_2_
  44.0 3.6 %all-to-all-start.1 = ((bf16[8,48,2048]{2,1,0:T(8,128)(2,1)}), bf16[8,48,2048]{2,1,0:T(8,128)(2,1)S(1)}, u32[]{:S(2)}, u32[]{:S(2)}) async-start(bf16[8,48,2048]{2,1,0:T(8,128)(2,1)} %bitcast.10), calls=%async_computation.1 | async-start | bytes 3145728 | tf_op jit(solution)/shard_map/all_to_all | solution.py:393
  47.6 0.0 copy-start.5
  47.6 0.3 collective-permute-start.5
  47.9 5.6 %collective-permute-done.5 = bf16[1,8,48,128]{3,2,1,0:T(8,128)(2,1)S(1)} collective-permute-done((bf16[1,8,48,128]{3,2,1,0:T(8,128)(2,1)S(1)}, bf16[1,8,48,128]{3,2,1,0:T(8,128)(2,1)S(1)}, u32[]{:S(2)}, u32[]{:S(2)}) %collective-permute-start.5) | collective-permute-done | bytes 98336 | tf_op jit(solution)/shard_map/ppermute | solution.py:269
  53.5 0.1 collective-permute-start.6
  53.6 5.7 %collective-permute-done.6 = bf16[2,8,48,128]{3,2,1,0:T(8,128)(2,1)S(1)} collective-permute-done((bf16[2,8,48,128]{3,2,1,0:T(8,128)(2,1)S(1)}, bf16[2,8,48,128]{3,2,1,0:T(8,128)(2,1)S(1)}, u32[]{:S(2)}, u32[]{:S(2)}) %collective-permute-start.6) | collective-permute-done | bytes 196640 | tf_op jit(solution)/shard_map/ppermute | solution.py:269
  59.3 0.0 copy-start.1
  59.4 0.0 copy-start.2
  59.4 0.1 collective-permute-start.7
  59.5 1.7 %collective-permute-done.7.b_ref.refs_4_ = bf16[4,8,48,128]{3,2,1,0:T(8,128)(2,1)S(1)} collective-permute-done((bf16[4,8,48,128]{3,2,1,0:T(8,128)(2,1)S(1)}, bf16[4,8,48,128]{3,2,1,0:T(8,128)(2,1)S(1)}, u32[]{:S(2)}, u32[]{:S(2)}) %collective-permute-start.7) | collective-permute-done | bytes 393248 | tf_op jit(solution)/shard_map/ppermute | solution.py:269
  61.2 0.2 delta_squares.1
  61.4 1.8 %collective-permute-start.8 = (f32[8,128]{1,0:T(8,128)S(1)}, f32[8,128]{1,0:T(8,128)S(1)}, u32[]{:S(2)}, u32[]{:S(2)}) collective-permute-start(f32[8,128]{1,0:T(8,128)S(1)} %delta_squares.1), channel_id=1, source_target_pairs={{0,193},{1,64},{64,1},{65,128},{128,65},{129,192},{192,129},{193,0... | collective-permute-start | bytes 12296 | tf_op jit(solution)/shard_map/ppermute | solution.py:345
  63.2 3.1 %collective-permute-done.8 = f32[8,128]{1,0:T(8,128)S(1)} collective-permute-done((f32[8,128]{1,0:T(8,128)S(1)}, f32[8,128]{1,0:T(8,128)S(1)}, u32[]{:S(2)}, u32[]{:S(2)}) %collective-permute-start.8) | collective-permute-done | bytes 4128 | tf_op jit(solution)/shard_map/ppermute | solution.py:345
  66.3 1.9 %collective-permute-start.9 = (f32[8,128]{1,0:T(8,128)S(1)}, f32[8,128]{1,0:T(8,128)S(1)}, u32[]{:S(2)}, u32[]{:S(2)}) collective-permute-start(f32[8,128]{1,0:T(8,128)S(1)} %add.22), channel_id=1, source_target_pairs={{0,2},{2,0},{4,6},{6,4},{1,3},{3,1},{5,7},{7,5},{8,10},{10,8},{12,... | collective-permute-start | bytes 12296 | tf_op jit(solution)/shard_map/ppermute | solution.py:269
  68.2 1.7 %collective-permute-done.9 = f32[8,128]{1,0:T(8,128)S(1)} collective-permute-done((f32[8,128]{1,0:T(8,128)S(1)}, f32[8,128]{1,0:T(8,128)S(1)}, u32[]{:S(2)}, u32[]{:S(2)}) %collective-permute-start.9) | collective-permute-done | bytes 4128 | tf_op jit(solution)/shard_map/ppermute | solution.py:269
  69.9 3.2 %collective-permute-start.10 = (f32[8,128]{1,0:T(8,128)S(1)}, f32[8,128]{1,0:T(8,128)S(1)}, u32[]{:S(2)}, u32[]{:S(2)}) collective-permute-start(f32[8,128]{1,0:T(8,128)S(1)} %add.23.refs_1_), channel_id=1, source_target_pairs={{0,6},{2,4},{4,2},{6,0},{1,7},{3,5},{5,3},{7,1},{8,14},{10,12},{12... | collective-permute-start | bytes 12296 | tf_op jit(solution)/shard_map/ppermute | solution.py:269
  73.0 0.0 all-to-all-done.1
  73.1 0.0 copy-start.4
  73.1 0.0 copy-done.5
  73.1 0.0 copy-start.6
  73.1 0.7 copy-done.6
  73.7 1.7 %combine.1 = bf16[128,2048]{1,0:T(8,128)(2,1)} custom-call(s32[2,128]{1,0:T(2,128)S(1)} %bitcast.19, f32[2,128]{1,0:T(2,128)S(1)} %bitcast.20, bf16[384,2048]{1,0:T(8,128)(2,1)S(1)} %bitcast.15), custom_call_target="tpu_custom_call" | custom-call | tf_op jit(solution)/shard_map/combine/pallas_call | solution.py:394
  75.5 0.0 collective-permute-done.10.refs_2_
  75.5 0.0 copy-done.1
  75.5 0.0 copy-done.2
  75.5 0.0 copy-done.4
  75.5 1.8 %outer_update.1 = (bf16[1,96,2048]{2,1,0:T(8,128)(2,1)}, f32[64,96]{1,0:T(8,128)}) custom-call(s32[6]{0:T(128)S(1)} %stack.27.at_ref.refs_0_, f32[8,128]{1,0:T(8,128)S(1)} %add.23.refs_1_, f32[8,128]{1,0:T(8,128)S(1)} %collective-permute-done.10.refs_2_, bf16[4,8,48,128]{3,2,1,0:T(8,128)(2,1)S(1)} %pad_maximum_fusion.a_ref.refs_3_, ...), custom_call_target="tpu_custom_call" | custom-call | tf_op jit(solution)/shard_map/outer_update/pallas_call | solution.py:352
  (8 shorter events, 0.2 us)
Async XLA Ops:
  3.4 5.8 %copy-start = (f32[1,96,2048]{2,1,0:T(8,128)S(1)}, f32[1,96,2048]{2,1,0:T(8,128)}, u32[]{:S(2)}) copy-start(f32[1,96,2048]{2,1,0:T(8,128)} %own_ref.1) | copy-start | bytes 2359300
  3.4 28.5 %all-to-all-start = ((bf16[8,48,2048]{2,1,0:T(8,128)(2,1)}), bf16[8,48,2048]{2,1,0:T(8,128)(2,1)S(1)}, u32[]{:S(2)}, u32[]{:S(2)}) async-start(bf16[8,48,2048]{2,1,0:T(8,128)(2,1)} %dispatch.1), calls=%async_computation | async-start | bytes 3145728 | tf_op jit(solution)/shard_map/all_to_all | solution.py:388
  9.2 3.3 %copy-start.3 = (f32[96,64]{0,1:T(8,128)S(1)}, f32[96,64]{0,1:T(8,128)}, u32[]{:S(2)}) copy-start(f32[96,64]{0,1:T(8,128)} %param.18) | copy-start | bytes 73732
  9.3 1.8 %collective-permute-start = (f32[96,1024]{1,0:T(8,128)S(1)}, f32[96,1024]{1,0:T(8,128)S(1)}, u32[]{:S(2)}, u32[]{:S(2)}) collective-permute-start(f32[96,1024]{1,0:T(8,128)S(1)} %dynamic-slice_bitcast_fusion), channel_id=1, source_target_pairs={{0,8},{8,0},{1,9},{9,1},{2,10},{10,2},{3,11},{11,3},{4,12},{12,4},... | collective-permute-start | bytes 1179656 | tf_op jit(solution)/shard_map/ppermute | solution.py:269
  11.7 4.9 %collective-permute-start.1 = (bf16[96,512]{1,0:T(8,128)(2,1)S(1)}, bf16[96,512]{1,0:T(8,128)(2,1)S(1)}, u32[]{:S(2)}, u32[]{:S(2)}) collective-permute-start(bf16[96,512]{1,0:T(8,128)(2,1)S(1)} %get-tuple-element.21), channel_id=1, source_target_pairs={{0,16},{16,0},{32,48},{48,32},{1,17},{17,1},{33,49},{49,33},{2,18}... | collective-permute-start | bytes 294920 | tf_op jit(solution)/shard_map/ppermute | solution.py:269
  17.2 5.4 %collective-permute-start.2 = (bf16[96,256]{1,0:T(8,128)(2,1)S(1)}, bf16[96,256]{1,0:T(8,128)(2,1)S(1)}, u32[]{:S(2)}, u32[]{:S(2)}) collective-permute-start(bf16[96,256]{1,0:T(8,128)(2,1)S(1)} %get-tuple-element.23), channel_id=1, source_target_pairs={{0,48},{16,32},{32,16},{48,0},{1,49},{17,33},{33,17},{49,1},{2,50}... | collective-permute-start | bytes 147464 | tf_op jit(solution)/shard_map/ppermute | solution.py:269
  22.6 5.7 %collective-permute-start.3 = (bf16[5,48,128]{2,1,0:T(8,128)(2,1)S(1)}, bf16[5,48,128]{2,1,0:T(8,128)(2,1)S(1)}, u32[]{:S(2)}, u32[]{:S(2)}) collective-permute-start(bf16[5,48,128]{2,1,0:T(8,128)(2,1)S(1)} %get-tuple-element.25.sent_ref), channel_id=1, source_target_pairs={{0,64},{64,0},{128,192},{192,128},{1,65},{65,1},{129,193},{193,129... | collective-permute-start | bytes 184328 | tf_op jit(solution)/shard_map/ppermute | solution.py:269
  31.9 12.1 %collective-permute-start.4 = (bf16[6,48,128]{2,1,0:T(8,128)(2,1)S(1)}, bf16[6,48,128]{2,1,0:T(8,128)(2,1)S(1)}, u32[]{:S(2)}, u32[]{:S(2)}) collective-permute-start(bf16[6,48,128]{2,1,0:T(8,128)(2,1)S(1)} %get-tuple-element.29.refs_1_), channel_id=1, source_target_pairs={{0,192},{64,128},{128,64},{192,0},{1,193},{65,129},{129,65},{193,1... | collective-permute-start | bytes 221192 | tf_op jit(solution)/shard_map/ppermute | solution.py:269
  44.0 29.1 %all-to-all-start.1 = ((bf16[8,48,2048]{2,1,0:T(8,128)(2,1)}), bf16[8,48,2048]{2,1,0:T(8,128)(2,1)S(1)}, u32[]{:S(2)}, u32[]{:S(2)}) async-start(bf16[8,48,2048]{2,1,0:T(8,128)(2,1)} %bitcast.10), calls=%async_computation.1 | async-start | bytes 3145728 | tf_op jit(solution)/shard_map/all_to_all | solution.py:393
  47.6 25.5 %copy-start.5 = (s32[128,2]{0,1:T(2,128)S(1)}, s32[128,2]{0,1:T(2,128)}, u32[]{:S(2)}) copy-start(s32[128,2]{0,1:T(2,128)} %param.11) | copy-start | bytes 3076
  47.6 5.9 %collective-permute-start.5 = (bf16[1,8,48,128]{3,2,1,0:T(8,128)(2,1)S(1)}, bf16[1,8,48,128]{3,2,1,0:T(8,128)(2,1)S(1)}, u32[]{:S(2)}, u32[]{:S(2)}) collective-permute-start(bf16[1,8,48,128]{3,2,1,0:T(8,128)(2,1)S(1)} %delta_mean.1), channel_id=1, source_target_pairs={{0,48},{16,32},{32,16},{48,0},{1,49},{17,33},{33,17},{49,1},{2,50}... | collective-permute-start | bytes 294920 | tf_op jit(solution)/shard_map/ppermute | solution.py:269
  53.5 5.8 %collective-permute-start.6 = (bf16[2,8,48,128]{3,2,1,0:T(8,128)(2,1)S(1)}, bf16[2,8,48,128]{3,2,1,0:T(8,128)(2,1)S(1)}, u32[]{:S(2)}, u32[]{:S(2)}) collective-permute-start(bf16[2,8,48,128]{3,2,1,0:T(8,128)(2,1)S(1)} %pad_maximum_fusion.1), channel_id=1, source_target_pairs={{0,16},{16,0},{32,48},{48,32},{1,17},{17,1},{33,49},{49,33},{2,18}... | collective-permute-start | bytes 589832 | tf_op jit(solution)/shard_map/ppermute | solution.py:269
  59.3 16.1 %copy-start.1 = (f32[96,2048]{1,0:T(8,128)S(1)}, f32[96,2048]{1,0:T(8,128)}, u32[]{:S(2)}) copy-start(f32[96,2048]{1,0:T(8,128)} %refs_5_.1) | copy-start | bytes 2359300
  59.4 16.1 %copy-start.2 = (bf16[1,96,2048]{2,1,0:T(8,128)(2,1)S(1)}, bf16[1,96,2048]{2,1,0:T(8,128)(2,1)}, u32[]{:S(2)}) copy-start(bf16[1,96,2048]{2,1,0:T(8,128)(2,1)} %refs_6_.1) | copy-start | bytes 1179652
  59.4 1.8 %collective-permute-start.7 = (bf16[4,8,48,128]{3,2,1,0:T(8,128)(2,1)S(1)}, bf16[4,8,48,128]{3,2,1,0:T(8,128)(2,1)S(1)}, u32[]{:S(2)}, u32[]{:S(2)}) collective-permute-start(bf16[4,8,48,128]{3,2,1,0:T(8,128)(2,1)S(1)} %pad_maximum_fusion.a_ref.refs_3_), channel_id=1, source_target_pairs={{0,8},{8,0},{1,9},{9,1},{2,10},{10,2},{3,11},{11,3},{4,12},{12,4},... | collective-permute-start | bytes 1179656 | tf_op jit(solution)/shard_map/ppermute | solution.py:269
  61.4 4.9 %collective-permute-start.8 = (f32[8,128]{1,0:T(8,128)S(1)}, f32[8,128]{1,0:T(8,128)S(1)}, u32[]{:S(2)}, u32[]{:S(2)}) collective-permute-start(f32[8,128]{1,0:T(8,128)S(1)} %delta_squares.1), channel_id=1, source_target_pairs={{0,193},{1,64},{64,1},{65,128},{128,65},{129,192},{192,129},{193,0... | collective-permute-start | bytes 12296 | tf_op jit(solution)/shard_map/ppermute | solution.py:345
  66.3 3.6 %collective-permute-start.9 = (f32[8,128]{1,0:T(8,128)S(1)}, f32[8,128]{1,0:T(8,128)S(1)}, u32[]{:S(2)}, u32[]{:S(2)}) collective-permute-start(f32[8,128]{1,0:T(8,128)S(1)} %add.22), channel_id=1, source_target_pairs={{0,2},{2,0},{4,6},{6,4},{1,3},{3,1},{5,7},{7,5},{8,10},{10,8},{12,... | collective-permute-start | bytes 12296 | tf_op jit(solution)/shard_map/ppermute | solution.py:269
  69.9 5.6 %collective-permute-start.10 = (f32[8,128]{1,0:T(8,128)S(1)}, f32[8,128]{1,0:T(8,128)S(1)}, u32[]{:S(2)}, u32[]{:S(2)}) collective-permute-start(f32[8,128]{1,0:T(8,128)S(1)} %add.23.refs_1_), channel_id=1, source_target_pairs={{0,6},{2,4},{4,2},{6,0},{1,7},{3,5},{5,3},{7,1},{8,14},{10,12},{12... | collective-permute-start | bytes 12296 | tf_op jit(solution)/shard_map/ppermute | solution.py:269
  73.1 2.4 %copy-start.4 = (f32[96,64]{0,1:T(8,128)S(1)}, f32[96,64]{0,1:T(8,128)}, u32[]{:S(2)}) copy-start(f32[96,64]{0,1:T(8,128)} %param.18) | copy-start | bytes 73732
  73.1 0.7 copy-start.6

commit v7 on v6

--- a/solution.py
+++ b/solution.py
@@ -74,15 +74,15 @@
         copy.wait()
 
 
-def combine_kernel(routes_ref, weight_ref, rows_ref, out_ref):
-    tokens = routes_ref.shape[1]
+def combine_kernel(table_ref, rows_ref, out_ref):
+    tokens = table_ref.shape[1]
     capacity = rows_ref.shape[0] // EXPERTS
-    routes = routes_ref[...]
+    routes = table_ref[0:2].astype(jnp.int32)
     place = slots(routes, tokens, capacity)
     row = lax.broadcasted_iota(jnp.int32, (capacity, tokens), 0)
     parts = []
     for e in range(EXPERTS):
-        weight = jnp.where(routes[0:1, :] == e, weight_ref[0:1, :], weight_ref[1:2, :])
+        weight = jnp.where(routes[0:1, :] == e, table_ref[2:3, :], table_ref[3:4, :])
         parts.append(jnp.where(row == place[e : e + 1, :], weight, 0.0))
     table = jnp.concatenate(parts, axis=0).T
     high = table.astype(bf16)
@@ -269,7 +269,7 @@
     return lax.ppermute(value, axis, [(i, i ^ bits) for i in range(size)])
 
 
-def outer_sum(pseudo_grad, momentum):
+def outer_sum(pseudo_grad, momentum, routes_t, weight_t):
     rows, width = pseudo_grad.shape[1:]
     core, y, zh = lax.axis_index("c"), lax.axis_index("y"), lax.axis_index("zh")
     rep = (zh * 4 + y) * 2 + core
@@ -295,6 +295,8 @@
         name="delta_halve",
     )(at, keep, got)
     got = swap(send, "y", 3)
+    got, routes_t, weight_t = lax.optimization_barrier((got, routes_t, weight_t))
+    table = jnp.concatenate([routes_t.astype(f32), weight_t], axis=0)
     part = (rows // 2, half // 8)
     mom_block = jnp.concatenate([momentum[: rows // 2], momentum[rows // 2 :]], axis=1)
     keep, send = pl.pallas_call(
@@ -314,7 +316,7 @@
         compiler_params=params(),
         name="delta_add_z",
     )(keep, send, got)
-    return at, keep, send
+    return at, keep, send, table
 
 
 def outer_mean(keep, send, got):
@@ -384,7 +386,7 @@
         compiler_params=pltpu.CompilerParams(vmem_limit_bytes=DISPATCH_LIMIT),
         name="dispatch",
     )(routes_t, tokens)
-    at, keep, send = outer_sum(pseudo_grad, momentum)
+    at, keep, send, table = outer_sum(pseudo_grad, momentum, routes_t, weight_t)
     received = lax.all_to_all(outgoing, SHARD, split_axis=0, concat_axis=0, tiled=True)
     received, keep, send = lax.optimization_barrier((received, keep, send))
     result = ffn(received.reshape(EXPERTS * capacity, feat_width), w_gate, w_up, w_down)
@@ -393,12 +395,12 @@
     returned = lax.all_to_all(result, SHARD, split_axis=0, concat_axis=0, tiled=True)
     moe_out = pl.pallas_call(
         combine_kernel,
-        in_specs=whole(3),
+        in_specs=whole(2),
         out_specs=whole(1)[0],
         out_shape=jax.ShapeDtypeStruct((tok_rows, feat_width), bf16),
         compiler_params=params(),
         name="combine",
-    )(routes_t, weight_t, returned.reshape(EXPERTS * capacity, feat_width))
+    )(table, returned.reshape(EXPERTS * capacity, feat_width))
     block = outer_mean(keep, send, got)
     momentum_next, local_next, moe_out = outer_finish(moe_out, at, block, global_params, momentum, local_params)
     return (moe_out, momentum_next, local_next)

time: 77.6 us -> 77.2 us (level)
  transfers between devices with their start and end apart: 13 -> 13, of which waited for: 10 -> 10; matrix products, arithmetic and copies ran while one was open for 1% -> 1% of each run, Pallas kernels for 13% -> 14%
where the time goes in v7:
time: 77.2 us; the launch traced here: 76.7 us
  waiting for transfers between devices  34.2 us (44%)
  starting transfers between devices  26.1 us (34%)
  Pallas kernels  15 us (19%)
  between operations  0.84 us (1%)
    ppermute x10, waiting for transfers between devices, swap(): return lax.ppermute(value, axis, [(i, i ^ bits) for i in range(size)])  27.5 us
    ppermute x10, starting transfers between devices, swap(): return lax.ppermute(value, axis, [(i, i ^ bits) for i in range(size)])  14.9 us
    pallas_call x1, Pallas kernels, ffn(): pl.pallas_call(ffn_kernel, in_specs=whole(1) + [anywhere] * 3, out_specs=...  7.28 us
    all_to_all x1, starting transfers between devices, local(): lax.all_to_all(outgoing, SHARD, split_axis=0, concat_axis=0, tiled=True)  5.78 us
    all_to_all x1, waiting for transfers between devices, local(): lax.all_to_all(outgoing, SHARD, split_axis=0, concat_axis=0, tiled=True)  3.62 us
    all_to_all x1, starting transfers between devices, local(): lax.all_to_all(result, SHARD, split_axis=0, concat_axis=0, tiled=True)  3.59 us
    ppermute x1, waiting for transfers between devices, outer_finish(): lax.ppermute(squares, ('zh', 'zl'), [(z, (z + 1 if z % 2 else z - 1) % 8)...  3.08 us
    pallas_call x1, Pallas kernels, local(): pl.pallas_call(dispatch_kernel, in_specs=[pl.BlockSpec(memory_space=pl.AN...  2.8 us
  transfers between devices with their start and end apart: 13, of which 10 were waited for; matrix products, arithmetic and copies ran while one was open for 1% of the time, Pallas kernels for 14%

profile of v7, /device:TPU:24, one launch (start us, length us, event | category | flops | bytes accessed | tf_op | source)
XLA Modules:
  0.0 76.7 jit_solution(2277783714854187728)
XLA Ops:
  0.6 2.8 %dispatch.1 = bf16[8,48,2048]{2,1,0:T(8,128)(2,1)} custom-call(s32[2,128]{1,0:T(2,128)} %bitcast.18, bf16[128,2048]{1,0:T(8,128)(2,1)} %tokens_hbm.1), custom_call_target="tpu_custom_call" | custom-call | tf_op jit(solution)/shard_map/dispatch/pallas_call | solution.py:375
  3.4 0.0 copy-start
  3.4 5.8 %all-to-all-start = ((bf16[8,48,2048]{2,1,0:T(8,128)(2,1)}), bf16[8,48,2048]{2,1,0:T(8,128)(2,1)S(1)}, u32[]{:S(2)}, u32[]{:S(2)}) async-start(bf16[8,48,2048]{2,1,0:T(8,128)(2,1)} %dispatch.1), calls=%async_computation | async-start | bytes 3145728 | tf_op jit(solution)/shard_map/all_to_all | solution.py:390
  9.2 0.0 copy-start.3
  9.2 0.0 copy-done
  9.3 0.1 collective-permute-start
  9.4 0.1 stack.27.at_ref.refs_0_
  9.5 1.6 %collective-permute-done.got_ref = f32[96,1024]{1,0:T(8,128)S(1)} collective-permute-done((f32[96,1024]{1,0:T(8,128)S(1)}, f32[96,1024]{1,0:T(8,128)S(1)}, u32[]{:S(2)}, u32[]{:S(2)}) %collective-permute-start) | collective-permute-done | bytes 393248 | tf_op jit(solution)/shard_map/ppermute | solution.py:269
  11.1 0.6 delta_halve_first.1
  11.7 0.8 %collective-permute-start.1 = (bf16[96,512]{1,0:T(8,128)(2,1)S(1)}, bf16[96,512]{1,0:T(8,128)(2,1)S(1)}, u32[]{:S(2)}, u32[]{:S(2)}) collective-permute-start(bf16[96,512]{1,0:T(8,128)(2,1)S(1)} %get-tuple-element.24), channel_id=1, source_target_pairs={{0,16},{16,0},{32,48},{48,32},{1,17},{17,1},{33,49},{49,33},{2,18}... | collective-permute-start | bytes 294920 | tf_op jit(solution)/shard_map/ppermute | solution.py:269
  12.5 0.0 copy-done.3
  12.5 0.1 fusion
  12.6 0.1 copy.15
  12.7 0.1 copy.16
  12.8 3.9 %collective-permute-done.1.got_ref = bf16[96,512]{1,0:T(8,128)(2,1)S(1)} collective-permute-done((bf16[96,512]{1,0:T(8,128)(2,1)S(1)}, bf16[96,512]{1,0:T(8,128)(2,1)S(1)}, u32[]{:S(2)}, u32[]{:S(2)}) %collective-permute-start.1) | collective-permute-done | bytes 98336 | tf_op jit(solution)/shard_map/ppermute | solution.py:269
  16.6 0.6 delta_halve.1
  17.2 0.3 collective-permute-start.2
  17.5 0.1 pad_maximum_fusion.2.mom_ref
  17.6 5.0 %collective-permute-done.2.got_ref = bf16[96,256]{1,0:T(8,128)(2,1)S(1)} collective-permute-done((bf16[96,256]{1,0:T(8,128)(2,1)S(1)}, bf16[96,256]{1,0:T(8,128)(2,1)S(1)}, u32[]{:S(2)}, u32[]{:S(2)}) %collective-permute-start.2) | collective-permute-done | bytes 49184 | tf_op jit(solution)/shard_map/ppermute | solution.py:269
  22.6 3.4 %collective-permute-start.3 = (bf16[5,48,128]{2,1,0:T(8,128)(2,1)S(1)}, bf16[5,48,128]{2,1,0:T(8,128)(2,1)S(1)}, u32[]{:S(2)}, u32[]{:S(2)}) collective-permute-start(bf16[5,48,128]{2,1,0:T(8,128)(2,1)S(1)} %get-tuple-element.29.sent_ref), channel_id=1, source_target_pairs={{0,64},{64,0},{128,192},{192,128},{1,65},{65,1},{129,193},{193,129... | collective-permute-start | bytes 184328 | tf_op jit(solution)/shard_map/ppermute | solution.py:269
  26.0 2.3 %collective-permute-done.3.got_ref = bf16[5,48,128]{2,1,0:T(8,128)(2,1)S(1)} collective-permute-done((bf16[5,48,128]{2,1,0:T(8,128)(2,1)S(1)}, bf16[5,48,128]{2,1,0:T(8,128)(2,1)S(1)}, u32[]{:S(2)}, u32[]{:S(2)}) %collective-permute-start.3) | collective-permute-done | bytes 61472 | tf_op jit(solution)/shard_map/ppermute | solution.py:269
  28.3 3.6 %all-to-all-done = bf16[8,48,2048]{2,1,0:T(8,128)(2,1)S(1)} async-done(((bf16[8,48,2048]{2,1,0:T(8,128)(2,1)}), bf16[8,48,2048]{2,1,0:T(8,128)(2,1)S(1)}, u32[]{:S(2)}, u32[]{:S(2)}) %all-to-all-start) | async-done | bytes 1572896 | tf_op jit(solution)/shard_map/all_to_all | solution.py:390
  31.9 4.8 %collective-permute-start.4 = (bf16[6,48,128]{2,1,0:T(8,128)(2,1)S(1)}, bf16[6,48,128]{2,1,0:T(8,128)(2,1)S(1)}, u32[]{:S(2)}, u32[]{:S(2)}) collective-permute-start(bf16[6,48,128]{2,1,0:T(8,128)(2,1)S(1)} %get-tuple-element.33.refs_1_), channel_id=1, source_target_pairs={{0,192},{64,128},{128,64},{192,0},{1,193},{65,129},{129,65},{193,1... | collective-permute-start | bytes 221192 | tf_op jit(solution)/shard_map/ppermute | solution.py:269
  36.7 7.3 %expert_ffn.1 = bf16[384,2048]{1,0:T(8,128)(2,1)} custom-call(bf16[384,2048]{1,0:T(8,128)(2,1)S(1)} %bitcast.16, bf16[1,2048,768]{2,1,0:T(8,128)(2,1)} %gate_hbm.1, bf16[1,2048,768]{2,1,0:T(8,128)(2,1)} %up_hbm.1, bf16[1,768,2048]{2,1,0:T(8,128)(2,1)} %down_hbm.1), custom_call_target="tpu_custom_call" | custom-call | flops 3623878656 | bytes 12582912 | tf_op jit(solution)/shard_map/expert_ffn/pallas_call | solution.py:145
  44.0 0.0 collective-permute-done.4.refs_2_
  44.0 3.6 %all-to-all-start.1 = ((bf16[8,48,2048]{2,1,0:T(8,128)(2,1)}), bf16[8,48,2048]{2,1,0:T(8,128)(2,1)S(1)}, u32[]{:S(2)}, u32[]{:S(2)}) async-start(bf16[8,48,2048]{2,1,0:T(8,128)(2,1)} %bitcast.10), calls=%async_computation.1 | async-start | bytes 3145728 | tf_op jit(solution)/shard_map/all_to_all | solution.py:395
  47.6 0.0 copy-start.5
  47.6 0.0 copy-start.6
  47.6 0.3 collective-permute-start.5
  47.9 5.6 %collective-permute-done.5 = bf16[1,8,48,128]{3,2,1,0:T(8,128)(2,1)S(1)} collective-permute-done((bf16[1,8,48,128]{3,2,1,0:T(8,128)(2,1)S(1)}, bf16[1,8,48,128]{3,2,1,0:T(8,128)(2,1)S(1)}, u32[]{:S(2)}, u32[]{:S(2)}) %collective-permute-start.5) | collective-permute-done | bytes 98336 | tf_op jit(solution)/shard_map/ppermute | solution.py:269
  53.6 0.1 collective-permute-start.6
  53.7 5.7 %collective-permute-done.6 = bf16[2,8,48,128]{3,2,1,0:T(8,128)(2,1)S(1)} collective-permute-done((bf16[2,8,48,128]{3,2,1,0:T(8,128)(2,1)S(1)}, bf16[2,8,48,128]{3,2,1,0:T(8,128)(2,1)S(1)}, u32[]{:S(2)}, u32[]{:S(2)}) %collective-permute-start.6) | collective-permute-done | bytes 196640 | tf_op jit(solution)/shard_map/ppermute | solution.py:269
  59.4 0.0 copy-start.1
  59.4 0.0 copy-start.2
  59.4 0.1 collective-permute-start.7
  59.5 1.7 %collective-permute-done.7.b_ref.refs_4_ = bf16[4,8,48,128]{3,2,1,0:T(8,128)(2,1)S(1)} collective-permute-done((bf16[4,8,48,128]{3,2,1,0:T(8,128)(2,1)S(1)}, bf16[4,8,48,128]{3,2,1,0:T(8,128)(2,1)S(1)}, u32[]{:S(2)}, u32[]{:S(2)}) %collective-permute-start.7) | collective-permute-done | bytes 393248 | tf_op jit(solution)/shard_map/ppermute | solution.py:269
  61.2 0.2 delta_squares.1
  61.4 1.8 %collective-permute-start.8 = (f32[8,128]{1,0:T(8,128)S(1)}, f32[8,128]{1,0:T(8,128)S(1)}, u32[]{:S(2)}, u32[]{:S(2)}) collective-permute-start(f32[8,128]{1,0:T(8,128)S(1)} %delta_squares.1), channel_id=1, source_target_pairs={{0,193},{1,64},{64,1},{65,128},{128,65},{129,192},{192,129},{193,0... | collective-permute-start | bytes 12296 | tf_op jit(solution)/shard_map/ppermute | solution.py:347
  63.2 3.1 %collective-permute-done.8 = f32[8,128]{1,0:T(8,128)S(1)} collective-permute-done((f32[8,128]{1,0:T(8,128)S(1)}, f32[8,128]{1,0:T(8,128)S(1)}, u32[]{:S(2)}, u32[]{:S(2)}) %collective-permute-start.8) | collective-permute-done | bytes 4128 | tf_op jit(solution)/shard_map/ppermute | solution.py:347
  66.3 1.9 %collective-permute-start.9 = (f32[8,128]{1,0:T(8,128)S(1)}, f32[8,128]{1,0:T(8,128)S(1)}, u32[]{:S(2)}, u32[]{:S(2)}) collective-permute-start(f32[8,128]{1,0:T(8,128)S(1)} %add.22), channel_id=1, source_target_pairs={{0,2},{2,0},{4,6},{6,4},{1,3},{3,1},{5,7},{7,5},{8,10},{10,8},{12,... | collective-permute-start | bytes 12296 | tf_op jit(solution)/shard_map/ppermute | solution.py:269
  68.2 0.0 copy-done.5
  68.2 1.7 %collective-permute-done.9 = f32[8,128]{1,0:T(8,128)S(1)} collective-permute-done((f32[8,128]{1,0:T(8,128)S(1)}, f32[8,128]{1,0:T(8,128)S(1)}, u32[]{:S(2)}, u32[]{:S(2)}) %collective-permute-start.9) | collective-permute-done | bytes 4128 | tf_op jit(solution)/shard_map/ppermute | solution.py:269
  69.9 3.1 %collective-permute-start.10 = (f32[8,128]{1,0:T(8,128)S(1)}, f32[8,128]{1,0:T(8,128)S(1)}, u32[]{:S(2)}, u32[]{:S(2)}) collective-permute-start(f32[8,128]{1,0:T(8,128)S(1)} %add.23.refs_1_), channel_id=1, source_target_pairs={{0,6},{2,4},{4,2},{6,0},{1,7},{3,5},{5,3},{7,1},{8,14},{10,12},{12... | collective-permute-start | bytes 12296 | tf_op jit(solution)/shard_map/ppermute | solution.py:269
  73.1 0.0 copy-done.6
  73.1 0.0 all-to-all-done.1
  73.1 0.0 copy-start.4
  73.1 1.7 %combine.1 = bf16[128,2048]{1,0:T(8,128)(2,1)} custom-call(f32[4,128]{1,0:T(4,128)S(1)} %pad_maximum_fusion.3.table_ref, bf16[384,2048]{1,0:T(8,128)(2,1)S(1)} %bitcast.15), custom_call_target="tpu_custom_call" | custom-call | tf_op jit(solution)/shard_map/combine/pallas_call | solution.py:396
  74.8 0.0 collective-permute-done.10.refs_2_
  74.8 0.0 copy-done.1
  74.8 0.0 copy-done.2
  74.8 0.0 copy-done.4
  74.8 1.8 %outer_update.1 = (bf16[1,96,2048]{2,1,0:T(8,128)(2,1)}, f32[64,96]{1,0:T(8,128)}) custom-call(s32[6]{0:T(128)S(1)} %stack.27.at_ref.refs_0_, f32[8,128]{1,0:T(8,128)S(1)} %add.23.refs_1_, f32[8,128]{1,0:T(8,128)S(1)} %collective-permute-done.10.refs_2_, bf16[4,8,48,128]{3,2,1,0:T(8,128)(2,1)S(1)} %pad_maximum_fusion.a_ref.refs_3_, ...), custom_call_target="tpu_custom_call" | custom-call | tf_op jit(solution)/shard_map/outer_update/pallas_call | solution.py:354
  (10 shorter events, 0.2 us)
Async XLA Ops:
  3.4 5.8 %copy-start = (f32[1,96,2048]{2,1,0:T(8,128)S(1)}, f32[1,96,2048]{2,1,0:T(8,128)}, u32[]{:S(2)}) copy-start(f32[1,96,2048]{2,1,0:T(8,128)} %own_ref.1) | copy-start | bytes 2359300
  3.4 28.5 %all-to-all-start = ((bf16[8,48,2048]{2,1,0:T(8,128)(2,1)}), bf16[8,48,2048]{2,1,0:T(8,128)(2,1)S(1)}, u32[]{:S(2)}, u32[]{:S(2)}) async-start(bf16[8,48,2048]{2,1,0:T(8,128)(2,1)} %dispatch.1), calls=%async_computation | async-start | bytes 3145728 | tf_op jit(solution)/shard_map/all_to_all | solution.py:390
  9.2 3.3 %copy-start.3 = (f32[96,64]{0,1:T(8,128)S(1)}, f32[96,64]{0,1:T(8,128)}, u32[]{:S(2)}) copy-start(f32[96,64]{0,1:T(8,128)} %param.18) | copy-start | bytes 73732
  9.3 1.8 %collective-permute-start = (f32[96,1024]{1,0:T(8,128)S(1)}, f32[96,1024]{1,0:T(8,128)S(1)}, u32[]{:S(2)}, u32[]{:S(2)}) collective-permute-start(f32[96,1024]{1,0:T(8,128)S(1)} %dynamic-slice_bitcast_fusion), channel_id=1, source_target_pairs={{0,8},{8,0},{1,9},{9,1},{2,10},{10,2},{3,11},{11,3},{4,12},{12,4},... | collective-permute-start | bytes 1179656 | tf_op jit(solution)/shard_map/ppermute | solution.py:269
  11.7 4.9 %collective-permute-start.1 = (bf16[96,512]{1,0:T(8,128)(2,1)S(1)}, bf16[96,512]{1,0:T(8,128)(2,1)S(1)}, u32[]{:S(2)}, u32[]{:S(2)}) collective-permute-start(bf16[96,512]{1,0:T(8,128)(2,1)S(1)} %get-tuple-element.24), channel_id=1, source_target_pairs={{0,16},{16,0},{32,48},{48,32},{1,17},{17,1},{33,49},{49,33},{2,18}... | collective-permute-start | bytes 294920 | tf_op jit(solution)/shard_map/ppermute | solution.py:269
  17.2 5.4 %collective-permute-start.2 = (bf16[96,256]{1,0:T(8,128)(2,1)S(1)}, bf16[96,256]{1,0:T(8,128)(2,1)S(1)}, u32[]{:S(2)}, u32[]{:S(2)}) collective-permute-start(bf16[96,256]{1,0:T(8,128)(2,1)S(1)} %get-tuple-element.26), channel_id=1, source_target_pairs={{0,48},{16,32},{32,16},{48,0},{1,49},{17,33},{33,17},{49,1},{2,50}... | collective-permute-start | bytes 147464 | tf_op jit(solution)/shard_map/ppermute | solution.py:269
  22.6 5.7 %collective-permute-start.3 = (bf16[5,48,128]{2,1,0:T(8,128)(2,1)S(1)}, bf16[5,48,128]{2,1,0:T(8,128)(2,1)S(1)}, u32[]{:S(2)}, u32[]{:S(2)}) collective-permute-start(bf16[5,48,128]{2,1,0:T(8,128)(2,1)S(1)} %get-tuple-element.29.sent_ref), channel_id=1, source_target_pairs={{0,64},{64,0},{128,192},{192,128},{1,65},{65,1},{129,193},{193,129... | collective-permute-start | bytes 184328 | tf_op jit(solution)/shard_map/ppermute | solution.py:269
  31.9 12.1 %collective-permute-start.4 = (bf16[6,48,128]{2,1,0:T(8,128)(2,1)S(1)}, bf16[6,48,128]{2,1,0:T(8,128)(2,1)S(1)}, u32[]{:S(2)}, u32[]{:S(2)}) collective-permute-start(bf16[6,48,128]{2,1,0:T(8,128)(2,1)S(1)} %get-tuple-element.33.refs_1_), channel_id=1, source_target_pairs={{0,192},{64,128},{128,64},{192,0},{1,193},{65,129},{129,65},{193,1... | collective-permute-start | bytes 221192 | tf_op jit(solution)/shard_map/ppermute | solution.py:269
  44.0 29.1 %all-to-all-start.1 = ((bf16[8,48,2048]{2,1,0:T(8,128)(2,1)}), bf16[8,48,2048]{2,1,0:T(8,128)(2,1)S(1)}, u32[]{:S(2)}, u32[]{:S(2)}) async-start(bf16[8,48,2048]{2,1,0:T(8,128)(2,1)} %bitcast.10), calls=%async_computation.1 | async-start | bytes 3145728 | tf_op jit(solution)/shard_map/all_to_all | solution.py:395
  47.6 20.6 %copy-start.5 = (s32[128,2]{0,1:T(2,128)S(1)}, s32[128,2]{0,1:T(2,128)}, u32[]{:S(2)}) copy-start(s32[128,2]{0,1:T(2,128)} %param.11) | copy-start | bytes 3076
  47.6 25.5 %copy-start.6 = (f32[128,2]{0,1:T(2,128)S(1)}, f32[128,2]{0,1:T(2,128)}, u32[]{:S(2)}) copy-start(f32[128,2]{0,1:T(2,128)} %param.12) | copy-start | bytes 3076
  47.6 5.9 %collective-permute-start.5 = (bf16[1,8,48,128]{3,2,1,0:T(8,128)(2,1)S(1)}, bf16[1,8,48,128]{3,2,1,0:T(8,128)(2,1)S(1)}, u32[]{:S(2)}, u32[]{:S(2)}) collective-permute-start(bf16[1,8,48,128]{3,2,1,0:T(8,128)(2,1)S(1)} %delta_mean.1), channel_id=1, source_target_pairs={{0,48},{16,32},{32,16},{48,0},{1,49},{17,33},{33,17},{49,1},{2,50}... | collective-permute-start | bytes 294920 | tf_op jit(solution)/shard_map/ppermute | solution.py:269
  53.6 5.8 %collective-permute-start.6 = (bf16[2,8,48,128]{3,2,1,0:T(8,128)(2,1)S(1)}, bf16[2,8,48,128]{3,2,1,0:T(8,128)(2,1)S(1)}, u32[]{:S(2)}, u32[]{:S(2)}) collective-permute-start(bf16[2,8,48,128]{3,2,1,0:T(8,128)(2,1)S(1)} %pad_maximum_fusion.1), channel_id=1, source_target_pairs={{0,16},{16,0},{32,48},{48,32},{1,17},{17,1},{33,49},{49,33},{2,18}... | collective-permute-start | bytes 589832 | tf_op jit(solution)/shard_map/ppermute | solution.py:269
  59.4 15.4 %copy-start.1 = (f32[96,2048]{1,0:T(8,128)S(1)}, f32[96,2048]{1,0:T(8,128)}, u32[]{:S(2)}) copy-start(f32[96,2048]{1,0:T(8,128)} %refs_5_.1) | copy-start | bytes 2359300
  59.4 15.4 %copy-start.2 = (bf16[1,96,2048]{2,1,0:T(8,128)(2,1)S(1)}, bf16[1,96,2048]{2,1,0:T(8,128)(2,1)}, u32[]{:S(2)}) copy-start(bf16[1,96,2048]{2,1,0:T(8,128)(2,1)} %refs_6_.1) | copy-start | bytes 1179652
  59.4 1.8 %collective-permute-start.7 = (bf16[4,8,48,128]{3,2,1,0:T(8,128)(2,1)S(1)}, bf16[4,8,48,128]{3,2,1,0:T(8,128)(2,1)S(1)}, u32[]{:S(2)}, u32[]{:S(2)}) collective-permute-start(bf16[4,8,48,128]{3,2,1,0:T(8,128)(2,1)S(1)} %pad_maximum_fusion.a_ref.refs_3_), channel_id=1, source_target_pairs={{0,8},{8,0},{1,9},{9,1},{2,10},{10,2},{3,11},{11,3},{4,12},{12,4},... | collective-permute-start | bytes 1179656 | tf_op jit(solution)/shard_map/ppermute | solution.py:269
  61.4 4.9 %collective-permute-start.8 = (f32[8,128]{1,0:T(8,128)S(1)}, f32[8,128]{1,0:T(8,128)S(1)}, u32[]{:S(2)}, u32[]{:S(2)}) collective-permute-start(f32[8,128]{1,0:T(8,128)S(1)} %delta_squares.1), channel_id=1, source_target_pairs={{0,193},{1,64},{64,1},{65,128},{128,65},{129,192},{192,129},{193,0... | collective-permute-start | bytes 12296 | tf_op jit(solution)/shard_map/ppermute | solution.py:347
  66.3 3.6 %collective-permute-start.9 = (f32[8,128]{1,0:T(8,128)S(1)}, f32[8,128]{1,0:T(8,128)S(1)}, u32[]{:S(2)}, u32[]{:S(2)}) collective-permute-start(f32[8,128]{1,0:T(8,128)S(1)} %add.22), channel_id=1, source_target_pairs={{0,2},{2,0},{4,6},{6,4},{1,3},{3,1},{5,7},{7,5},{8,10},{10,8},{12,... | collective-permute-start | bytes 12296 | tf_op jit(solution)/shard_map/ppermute | solution.py:269
  69.9 4.9 %collective-permute-start.10 = (f32[8,128]{1,0:T(8,128)S(1)}, f32[8,128]{1,0:T(8,128)S(1)}, u32[]{:S(2)}, u32[]{:S(2)}) collective-permute-start(f32[8,128]{1,0:T(8,128)S(1)} %add.23.refs_1_), channel_id=1, source_target_pairs={{0,6},{2,4},{4,2},{6,0},{1,7},{3,5},{5,3},{7,1},{8,14},{10,12},{12... | collective-permute-start | bytes 12296 | tf_op jit(solution)/shard_map/ppermute | solution.py:269
  73.1 1.7 %copy-start.4 = (f32[96,64]{0,1:T(8,128)S(1)}, f32[96,64]{0,1:T(8,128)}, u32[]{:S(2)}) copy-start(f32[96,64]{0,1:T(8,128)} %param.18) | copy-start | bytes 73732

commit v8 on v7

--- a/solution.py
+++ b/solution.py
@@ -390,6 +390,7 @@
     received = lax.all_to_all(outgoing, SHARD, split_axis=0, concat_axis=0, tiled=True)
     received, keep, send = lax.optimization_barrier((received, keep, send))
     result = ffn(received.reshape(EXPERTS * capacity, feat_width), w_gate, w_up, w_down)
+    result, send = lax.optimization_barrier((result, send))
     result, got = lax.optimization_barrier((result, swap(send, "zh", 3)))
     result = result.reshape(EXPERTS, capacity, feat_width)
     returned = lax.all_to_all(result, SHARD, split_axis=0, concat_axis=0, tiled=True)

time: 77.2 us -> 80.9 us (1.048)
  starting transfers between devices: 26.1 us -> 28.4 us
  waiting for transfers between devices: 34.2 us -> 35.9 us
    ppermute x10, waiting for transfers between devices: 27.5 us -> 30.7 us  [swap(): return lax.ppermute(value, axis, [(i, i ^ bits) for i in range(size)])]
    ppermute x1, starting transfers between devices: 1.82 us -> 3.91 us  [outer_finish(): lax.ppermute(squares, ('zh', 'zl'), [(z, (z + 1 if z % 2 else z - 1) % 8)...]
    ppermute x1, waiting for transfers between devices: 3.08 us -> 1.59 us  [outer_finish(): lax.ppermute(squares, ('zh', 'zl'), [(z, (z + 1 if z % 2 else z - 1) % 8)...]
    all_to_all x1, starting transfers between devices: 3.59 us -> 4.61 us  [local(): lax.all_to_all(result, SHARD, split_axis=0, concat_axis=0, tiled=True)]
  transfers between devices with their start and end apart: 13 -> 13, of which waited for: 10 -> 12; matrix products, arithmetic and copies ran while one was open for 1% -> 1% of each run, Pallas kernels for 14% -> 4%
where the time goes in v8:
time: 80.9 us; the launch traced here: 80.7 us
  waiting for transfers between devices  35.9 us (44%)
  starting transfers between devices  28.4 us (35%)
  Pallas kernels  15 us (19%)
  between operations  0.81 us (1%)
    ppermute x10, waiting for transfers between devices, swap(): return lax.ppermute(value, axis, [(i, i ^ bits) for i in range(size)])  30.7 us
    ppermute x10, starting transfers between devices, swap(): return lax.ppermute(value, axis, [(i, i ^ bits) for i in range(size)])  14.1 us
    pallas_call x1, Pallas kernels, ffn(): pl.pallas_call(ffn_kernel, in_specs=whole(1) + [anywhere] * 3, out_specs=...  7.27 us
    all_to_all x1, starting transfers between devices, local(): lax.all_to_all(outgoing, SHARD, split_axis=0, concat_axis=0, tiled=True)  5.78 us
    all_to_all x1, starting transfers between devices, local(): lax.all_to_all(result, SHARD, split_axis=0, concat_axis=0, tiled=True)  4.61 us
    ppermute x1, starting transfers between devices, outer_finish(): lax.ppermute(squares, ('zh', 'zl'), [(z, (z + 1 if z % 2 else z - 1) % 8)...  3.91 us
    all_to_all x1, waiting for transfers between devices, local(): lax.all_to_all(outgoing, SHARD, split_axis=0, concat_axis=0, tiled=True)  3.62 us
    pallas_call x1, Pallas kernels, local(): pl.pallas_call(dispatch_kernel, in_specs=[pl.BlockSpec(memory_space=pl.AN...  2.8 us
  transfers between devices with their start and end apart: 13, of which 12 were waited for; matrix products, arithmetic and copies ran while one was open for 1% of the time, Pallas kernels for 4%

profile of v8, /device:TPU:24, one launch (start us, length us, event | category | flops | bytes accessed | tf_op | source)
XLA Modules:
  0.0 80.7 jit_solution(1703420957519806985)
XLA Ops:
  0.6 2.8 %dispatch.1 = bf16[8,48,2048]{2,1,0:T(8,128)(2,1)} custom-call(s32[2,128]{1,0:T(2,128)} %bitcast.18, bf16[128,2048]{1,0:T(8,128)(2,1)} %tokens_hbm.1), custom_call_target="tpu_custom_call" | custom-call | tf_op jit(solution)/shard_map/dispatch/pallas_call | solution.py:375
  3.4 0.0 copy-start
  3.4 5.8 %all-to-all-start = ((bf16[8,48,2048]{2,1,0:T(8,128)(2,1)}), bf16[8,48,2048]{2,1,0:T(8,128)(2,1)S(1)}, u32[]{:S(2)}, u32[]{:S(2)}) async-start(bf16[8,48,2048]{2,1,0:T(8,128)(2,1)} %dispatch.1), calls=%async_computation | async-start | bytes 3145728 | tf_op jit(solution)/shard_map/all_to_all | solution.py:390
  9.2 0.0 copy-start.3
  9.2 0.0 copy-done
  9.3 0.1 collective-permute-start
  9.4 0.1 stack.27.at_ref.refs_0_
  9.5 1.6 %collective-permute-done.got_ref = f32[96,1024]{1,0:T(8,128)S(1)} collective-permute-done((f32[96,1024]{1,0:T(8,128)S(1)}, f32[96,1024]{1,0:T(8,128)S(1)}, u32[]{:S(2)}, u32[]{:S(2)}) %collective-permute-start) | collective-permute-done | bytes 393248 | tf_op jit(solution)/shard_map/ppermute | solution.py:269
  11.1 0.6 delta_halve_first.1
  11.7 0.8 %collective-permute-start.1 = (bf16[96,512]{1,0:T(8,128)(2,1)S(1)}, bf16[96,512]{1,0:T(8,128)(2,1)S(1)}, u32[]{:S(2)}, u32[]{:S(2)}) collective-permute-start(bf16[96,512]{1,0:T(8,128)(2,1)S(1)} %get-tuple-element.26), channel_id=1, source_target_pairs={{0,16},{16,0},{32,48},{48,32},{1,17},{17,1},{33,49},{49,33},{2,18}... | collective-permute-start | bytes 294920 | tf_op jit(solution)/shard_map/ppermute | solution.py:269
  12.5 0.0 copy-done.3
  12.5 0.1 fusion
  12.6 0.1 copy.15
  12.7 0.1 copy.16
  12.8 3.9 %collective-permute-done.1.got_ref = bf16[96,512]{1,0:T(8,128)(2,1)S(1)} collective-permute-done((bf16[96,512]{1,0:T(8,128)(2,1)S(1)}, bf16[96,512]{1,0:T(8,128)(2,1)S(1)}, u32[]{:S(2)}, u32[]{:S(2)}) %collective-permute-start.1) | collective-permute-done | bytes 98336 | tf_op jit(solution)/shard_map/ppermute | solution.py:269
  16.6 0.6 delta_halve.1
  17.2 0.3 collective-permute-start.2
  17.5 0.1 pad_maximum_fusion.2.mom_ref
  17.6 5.0 %collective-permute-done.2.got_ref = bf16[96,256]{1,0:T(8,128)(2,1)S(1)} collective-permute-done((bf16[96,256]{1,0:T(8,128)(2,1)S(1)}, bf16[96,256]{1,0:T(8,128)(2,1)S(1)}, u32[]{:S(2)}, u32[]{:S(2)}) %collective-permute-start.2) | collective-permute-done | bytes 49184 | tf_op jit(solution)/shard_map/ppermute | solution.py:269
  22.6 3.4 %collective-permute-start.3 = (bf16[5,48,128]{2,1,0:T(8,128)(2,1)S(1)}, bf16[5,48,128]{2,1,0:T(8,128)(2,1)S(1)}, u32[]{:S(2)}, u32[]{:S(2)}) collective-permute-start(bf16[5,48,128]{2,1,0:T(8,128)(2,1)S(1)} %get-tuple-element.31.sent_ref), channel_id=1, source_target_pairs={{0,64},{64,0},{128,192},{192,128},{1,65},{65,1},{129,193},{193,129... | collective-permute-start | bytes 184328 | tf_op jit(solution)/shard_map/ppermute | solution.py:269
  26.0 2.3 %collective-permute-done.3.got_ref = bf16[5,48,128]{2,1,0:T(8,128)(2,1)S(1)} collective-permute-done((bf16[5,48,128]{2,1,0:T(8,128)(2,1)S(1)}, bf16[5,48,128]{2,1,0:T(8,128)(2,1)S(1)}, u32[]{:S(2)}, u32[]{:S(2)}) %collective-permute-start.3) | collective-permute-done | bytes 61472 | tf_op jit(solution)/shard_map/ppermute | solution.py:269
  28.3 3.6 %all-to-all-done = bf16[8,48,2048]{2,1,0:T(8,128)(2,1)S(1)} async-done(((bf16[8,48,2048]{2,1,0:T(8,128)(2,1)}), bf16[8,48,2048]{2,1,0:T(8,128)(2,1)S(1)}, u32[]{:S(2)}, u32[]{:S(2)}) %all-to-all-start) | async-done | bytes 1572896 | tf_op jit(solution)/shard_map/all_to_all | solution.py:390
  31.9 7.3 %expert_ffn.1 = bf16[384,2048]{1,0:T(8,128)(2,1)} custom-call(bf16[384,2048]{1,0:T(8,128)(2,1)S(1)} %bitcast.16, bf16[1,2048,768]{2,1,0:T(8,128)(2,1)} %gate_hbm.1, bf16[1,2048,768]{2,1,0:T(8,128)(2,1)} %up_hbm.1, bf16[1,768,2048]{2,1,0:T(8,128)(2,1)} %down_hbm.1), custom_call_target="tpu_custom_call" | custom-call | flops 3623878656 | bytes 12582912 | tf_op jit(solution)/shard_map/expert_ffn/pallas_call | solution.py:145
  39.2 4.9 %collective-permute-start.4 = (bf16[6,48,128]{2,1,0:T(8,128)(2,1)S(1)}, bf16[6,48,128]{2,1,0:T(8,128)(2,1)S(1)}, u32[]{:S(2)}, u32[]{:S(2)}) collective-permute-start(bf16[6,48,128]{2,1,0:T(8,128)(2,1)S(1)} %get-tuple-element.37.refs_1_), channel_id=1, source_target_pairs={{0,192},{64,128},{128,64},{192,0},{1,193},{65,129},{129,65},{193,1... | collective-permute-start | bytes 221192 | tf_op jit(solution)/shard_map/ppermute | solution.py:269
  44.0 2.4 %collective-permute-done.4.refs_2_ = bf16[6,48,128]{2,1,0:T(8,128)(2,1)S(1)} collective-permute-done((bf16[6,48,128]{2,1,0:T(8,128)(2,1)S(1)}, bf16[6,48,128]{2,1,0:T(8,128)(2,1)S(1)}, u32[]{:S(2)}, u32[]{:S(2)}) %collective-permute-start.4) | collective-permute-done | bytes 73760 | tf_op jit(solution)/shard_map/ppermute | solution.py:269
  46.5 4.6 %all-to-all-start.1 = ((bf16[8,48,2048]{2,1,0:T(8,128)(2,1)}), bf16[8,48,2048]{2,1,0:T(8,128)(2,1)S(1)}, u32[]{:S(2)}, u32[]{:S(2)}) async-start(bf16[8,48,2048]{2,1,0:T(8,128)(2,1)} %bitcast.10), calls=%async_computation.1 | async-start | bytes 3145728 | tf_op jit(solution)/shard_map/all_to_all | solution.py:396
  51.1 0.0 copy-start.5
  51.1 0.0 copy-start.6
  51.1 0.3 collective-permute-start.5
  51.4 5.6 %collective-permute-done.5 = bf16[1,8,48,128]{3,2,1,0:T(8,128)(2,1)S(1)} collective-permute-done((bf16[1,8,48,128]{3,2,1,0:T(8,128)(2,1)S(1)}, bf16[1,8,48,128]{3,2,1,0:T(8,128)(2,1)S(1)}, u32[]{:S(2)}, u32[]{:S(2)}) %collective-permute-start.5) | collective-permute-done | bytes 98336 | tf_op jit(solution)/shard_map/ppermute | solution.py:269
  57.1 0.1 collective-permute-start.6
  57.2 5.7 %collective-permute-done.6 = bf16[2,8,48,128]{3,2,1,0:T(8,128)(2,1)S(1)} collective-permute-done((bf16[2,8,48,128]{3,2,1,0:T(8,128)(2,1)S(1)}, bf16[2,8,48,128]{3,2,1,0:T(8,128)(2,1)S(1)}, u32[]{:S(2)}, u32[]{:S(2)}) %collective-permute-start.6) | collective-permute-done | bytes 196640 | tf_op jit(solution)/shard_map/ppermute | solution.py:269
  62.9 0.0 copy-start.1
  62.9 0.0 copy-start.2
  62.9 0.1 collective-permute-start.7
  63.0 1.7 %collective-permute-done.7.b_ref.refs_4_ = bf16[4,8,48,128]{3,2,1,0:T(8,128)(2,1)S(1)} collective-permute-done((bf16[4,8,48,128]{3,2,1,0:T(8,128)(2,1)S(1)}, bf16[4,8,48,128]{3,2,1,0:T(8,128)(2,1)S(1)}, u32[]{:S(2)}, u32[]{:S(2)}) %collective-permute-start.7) | collective-permute-done | bytes 393248 | tf_op jit(solution)/shard_map/ppermute | solution.py:269
  64.7 0.2 delta_squares.1
  64.9 3.9 %collective-permute-start.8 = (f32[8,128]{1,0:T(8,128)S(1)}, f32[8,128]{1,0:T(8,128)S(1)}, u32[]{:S(2)}, u32[]{:S(2)}) collective-permute-start(f32[8,128]{1,0:T(8,128)S(1)} %delta_squares.1), channel_id=1, source_target_pairs={{0,193},{1,64},{64,1},{65,128},{128,65},{129,192},{192,129},{193,0... | collective-permute-start | bytes 12296 | tf_op jit(solution)/shard_map/ppermute | solution.py:347
  68.8 1.6 %collective-permute-done.8 = f32[8,128]{1,0:T(8,128)S(1)} collective-permute-done((f32[8,128]{1,0:T(8,128)S(1)}, f32[8,128]{1,0:T(8,128)S(1)}, u32[]{:S(2)}, u32[]{:S(2)}) %collective-permute-start.8) | collective-permute-done | bytes 4128 | tf_op jit(solution)/shard_map/ppermute | solution.py:347
  70.4 1.5 %collective-permute-start.9 = (f32[8,128]{1,0:T(8,128)S(1)}, f32[8,128]{1,0:T(8,128)S(1)}, u32[]{:S(2)}, u32[]{:S(2)}) collective-permute-start(f32[8,128]{1,0:T(8,128)S(1)} %add.22), channel_id=1, source_target_pairs={{0,2},{2,0},{4,6},{6,4},{1,3},{3,1},{5,7},{7,5},{8,10},{10,8},{12,... | collective-permute-start | bytes 12296 | tf_op jit(solution)/shard_map/ppermute | solution.py:269
  71.9 0.0 copy-done.5
  71.9 2.1 %collective-permute-done.9 = f32[8,128]{1,0:T(8,128)S(1)} collective-permute-done((f32[8,128]{1,0:T(8,128)S(1)}, f32[8,128]{1,0:T(8,128)S(1)}, u32[]{:S(2)}, u32[]{:S(2)}) %collective-permute-start.9) | collective-permute-done | bytes 4128 | tf_op jit(solution)/shard_map/ppermute | solution.py:269
  74.0 2.7 %collective-permute-start.10 = (f32[8,128]{1,0:T(8,128)S(1)}, f32[8,128]{1,0:T(8,128)S(1)}, u32[]{:S(2)}, u32[]{:S(2)}) collective-permute-start(f32[8,128]{1,0:T(8,128)S(1)} %add.23.refs_1_), channel_id=1, source_target_pairs={{0,6},{2,4},{4,2},{6,0},{1,7},{3,5},{5,3},{7,1},{8,14},{10,12},{12... | collective-permute-start | bytes 12296 | tf_op jit(solution)/shard_map/ppermute | solution.py:269
  76.7 0.0 copy-done.6
  76.7 0.0 all-to-all-done.1
  76.8 0.0 copy-start.4
  76.8 1.7 %combine.1 = bf16[128,2048]{1,0:T(8,128)(2,1)} custom-call(f32[4,128]{1,0:T(4,128)S(1)} %pad_maximum_fusion.3.table_ref, bf16[384,2048]{1,0:T(8,128)(2,1)S(1)} %bitcast.15), custom_call_target="tpu_custom_call" | custom-call | tf_op jit(solution)/shard_map/combine/pallas_call | solution.py:397
  78.5 0.4 collective-permute-done.10.refs_2_
  78.8 0.0 copy-done.1
  78.8 0.0 copy-done.2
  78.8 0.0 copy-done.4
  78.8 1.8 %outer_update.1 = (bf16[1,96,2048]{2,1,0:T(8,128)(2,1)}, f32[64,96]{1,0:T(8,128)}) custom-call(s32[6]{0:T(128)S(1)} %stack.27.at_ref.refs_0_, f32[8,128]{1,0:T(8,128)S(1)} %add.23.refs_1_, f32[8,128]{1,0:T(8,128)S(1)} %collective-permute-done.10.refs_2_, bf16[4,8,48,128]{3,2,1,0:T(8,128)(2,1)S(1)} %pad_maximum_fusion.a_ref.refs_3_, ...), custom_call_target="tpu_custom_call" | custom-call | tf_op jit(solution)/shard_map/outer_update/pallas_call | solution.py:354
  (10 shorter events, 0.2 us)
Async XLA Ops:
  3.4 5.8 %copy-start = (f32[1,96,2048]{2,1,0:T(8,128)S(1)}, f32[1,96,2048]{2,1,0:T(8,128)}, u32[]{:S(2)}) copy-start(f32[1,96,2048]{2,1,0:T(8,128)} %own_ref.1) | copy-start | bytes 2359300
  3.4 28.5 %all-to-all-start = ((bf16[8,48,2048]{2,1,0:T(8,128)(2,1)}), bf16[8,48,2048]{2,1,0:T(8,128)(2,1)S(1)}, u32[]{:S(2)}, u32[]{:S(2)}) async-start(bf16[8,48,2048]{2,1,0:T(8,128)(2,1)} %dispatch.1), calls=%async_computation | async-start | bytes 3145728 | tf_op jit(solution)/shard_map/all_to_all | solution.py:390
  9.2 3.3 %copy-start.3 = (f32[96,64]{0,1:T(8,128)S(1)}, f32[96,64]{0,1:T(8,128)}, u32[]{:S(2)}) copy-start(f32[96,64]{0,1:T(8,128)} %param.18) | copy-start | bytes 73732
  9.3 1.8 %collective-permute-start = (f32[96,1024]{1,0:T(8,128)S(1)}, f32[96,1024]{1,0:T(8,128)S(1)}, u32[]{:S(2)}, u32[]{:S(2)}) collective-permute-start(f32[96,1024]{1,0:T(8,128)S(1)} %dynamic-slice_bitcast_fusion), channel_id=1, source_target_pairs={{0,8},{8,0},{1,9},{9,1},{2,10},{10,2},{3,11},{11,3},{4,12},{12,4},... | collective-permute-start | bytes 1179656 | tf_op jit(solution)/shard_map/ppermute | solution.py:269
  11.7 4.9 %collective-permute-start.1 = (bf16[96,512]{1,0:T(8,128)(2,1)S(1)}, bf16[96,512]{1,0:T(8,128)(2,1)S(1)}, u32[]{:S(2)}, u32[]{:S(2)}) collective-permute-start(bf16[96,512]{1,0:T(8,128)(2,1)S(1)} %get-tuple-element.26), channel_id=1, source_target_pairs={{0,16},{16,0},{32,48},{48,32},{1,17},{17,1},{33,49},{49,33},{2,18}... | collective-permute-start | bytes 294920 | tf_op jit(solution)/shard_map/ppermute | solution.py:269
  17.2 5.4 %collective-permute-start.2 = (bf16[96,256]{1,0:T(8,128)(2,1)S(1)}, bf16[96,256]{1,0:T(8,128)(2,1)S(1)}, u32[]{:S(2)}, u32[]{:S(2)}) collective-permute-start(bf16[96,256]{1,0:T(8,128)(2,1)S(1)} %get-tuple-element.28), channel_id=1, source_target_pairs={{0,48},{16,32},{32,16},{48,0},{1,49},{17,33},{33,17},{49,1},{2,50}... | collective-permute-start | bytes 147464 | tf_op jit(solution)/shard_map/ppermute | solution.py:269
  22.6 5.7 %collective-permute-start.3 = (bf16[5,48,128]{2,1,0:T(8,128)(2,1)S(1)}, bf16[5,48,128]{2,1,0:T(8,128)(2,1)S(1)}, u32[]{:S(2)}, u32[]{:S(2)}) collective-permute-start(bf16[5,48,128]{2,1,0:T(8,128)(2,1)S(1)} %get-tuple-element.31.sent_ref), channel_id=1, source_target_pairs={{0,64},{64,0},{128,192},{192,128},{1,65},{65,1},{129,193},{193,129... | collective-permute-start | bytes 184328 | tf_op jit(solution)/shard_map/ppermute | solution.py:269
  39.2 7.3 %collective-permute-start.4 = (bf16[6,48,128]{2,1,0:T(8,128)(2,1)S(1)}, bf16[6,48,128]{2,1,0:T(8,128)(2,1)S(1)}, u32[]{:S(2)}, u32[]{:S(2)}) collective-permute-start(bf16[6,48,128]{2,1,0:T(8,128)(2,1)S(1)} %get-tuple-element.37.refs_1_), channel_id=1, source_target_pairs={{0,192},{64,128},{128,64},{192,0},{1,193},{65,129},{129,65},{193,1... | collective-permute-start | bytes 221192 | tf_op jit(solution)/shard_map/ppermute | solution.py:269
  46.5 30.3 %all-to-all-start.1 = ((bf16[8,48,2048]{2,1,0:T(8,128)(2,1)}), bf16[8,48,2048]{2,1,0:T(8,128)(2,1)S(1)}, u32[]{:S(2)}, u32[]{:S(2)}) async-start(bf16[8,48,2048]{2,1,0:T(8,128)(2,1)} %bitcast.10), calls=%async_computation.1 | async-start | bytes 3145728 | tf_op jit(solution)/shard_map/all_to_all | solution.py:396
  51.1 20.8 %copy-start.5 = (s32[128,2]{0,1:T(2,128)S(1)}, s32[128,2]{0,1:T(2,128)}, u32[]{:S(2)}) copy-start(s32[128,2]{0,1:T(2,128)} %param.11) | copy-start | bytes 3076
  51.1 25.6 %copy-start.6 = (f32[128,2]{0,1:T(2,128)S(1)}, f32[128,2]{0,1:T(2,128)}, u32[]{:S(2)}) copy-start(f32[128,2]{0,1:T(2,128)} %param.12) | copy-start | bytes 3076
  51.1 5.9 %collective-permute-start.5 = (bf16[1,8,48,128]{3,2,1,0:T(8,128)(2,1)S(1)}, bf16[1,8,48,128]{3,2,1,0:T(8,128)(2,1)S(1)}, u32[]{:S(2)}, u32[]{:S(2)}) collective-permute-start(bf16[1,8,48,128]{3,2,1,0:T(8,128)(2,1)S(1)} %delta_mean.1), channel_id=1, source_target_pairs={{0,48},{16,32},{32,16},{48,0},{1,49},{17,33},{33,17},{49,1},{2,50}... | collective-permute-start | bytes 294920 | tf_op jit(solution)/shard_map/ppermute | solution.py:269
  57.1 5.8 %collective-permute-start.6 = (bf16[2,8,48,128]{3,2,1,0:T(8,128)(2,1)S(1)}, bf16[2,8,48,128]{3,2,1,0:T(8,128)(2,1)S(1)}, u32[]{:S(2)}, u32[]{:S(2)}) collective-permute-start(bf16[2,8,48,128]{3,2,1,0:T(8,128)(2,1)S(1)} %pad_maximum_fusion.1), channel_id=1, source_target_pairs={{0,16},{16,0},{32,48},{48,32},{1,17},{17,1},{33,49},{49,33},{2,18}... | collective-permute-start | bytes 589832 | tf_op jit(solution)/shard_map/ppermute | solution.py:269
  62.9 16.0 %copy-start.1 = (f32[96,2048]{1,0:T(8,128)S(1)}, f32[96,2048]{1,0:T(8,128)}, u32[]{:S(2)}) copy-start(f32[96,2048]{1,0:T(8,128)} %refs_5_.1) | copy-start | bytes 2359300
  62.9 16.0 %copy-start.2 = (bf16[1,96,2048]{2,1,0:T(8,128)(2,1)S(1)}, bf16[1,96,2048]{2,1,0:T(8,128)(2,1)}, u32[]{:S(2)}) copy-start(bf16[1,96,2048]{2,1,0:T(8,128)(2,1)} %refs_6_.1) | copy-start | bytes 1179652
  62.9 1.8 %collective-permute-start.7 = (bf16[4,8,48,128]{3,2,1,0:T(8,128)(2,1)S(1)}, bf16[4,8,48,128]{3,2,1,0:T(8,128)(2,1)S(1)}, u32[]{:S(2)}, u32[]{:S(2)}) collective-permute-start(bf16[4,8,48,128]{3,2,1,0:T(8,128)(2,1)S(1)} %pad_maximum_fusion.a_ref.refs_3_), channel_id=1, source_target_pairs={{0,8},{8,0},{1,9},{9,1},{2,10},{10,2},{3,11},{11,3},{4,12},{12,4},... | collective-permute-start | bytes 1179656 | tf_op jit(solution)/shard_map/ppermute | solution.py:269
  64.9 5.5 %collective-permute-start.8 = (f32[8,128]{1,0:T(8,128)S(1)}, f32[8,128]{1,0:T(8,128)S(1)}, u32[]{:S(2)}, u32[]{:S(2)}) collective-permute-start(f32[8,128]{1,0:T(8,128)S(1)} %delta_squares.1), channel_id=1, source_target_pairs={{0,193},{1,64},{64,1},{65,128},{128,65},{129,192},{192,129},{193,0... | collective-permute-start | bytes 12296 | tf_op jit(solution)/shard_map/ppermute | solution.py:347
  70.4 3.6 %collective-permute-start.9 = (f32[8,128]{1,0:T(8,128)S(1)}, f32[8,128]{1,0:T(8,128)S(1)}, u32[]{:S(2)}, u32[]{:S(2)}) collective-permute-start(f32[8,128]{1,0:T(8,128)S(1)} %add.22), channel_id=1, source_target_pairs={{0,2},{2,0},{4,6},{6,4},{1,3},{3,1},{5,7},{7,5},{8,10},{10,8},{12,... | collective-permute-start | bytes 12296 | tf_op jit(solution)/shard_map/ppermute | solution.py:269
  74.0 4.8 %collective-permute-start.10 = (f32[8,128]{1,0:T(8,128)S(1)}, f32[8,128]{1,0:T(8,128)S(1)}, u32[]{:S(2)}, u32[]{:S(2)}) collective-permute-start(f32[8,128]{1,0:T(8,128)S(1)} %add.23.refs_1_), channel_id=1, source_target_pairs={{0,6},{2,4},{4,2},{6,0},{1,7},{3,5},{5,3},{7,1},{8,14},{10,12},{12... | collective-permute-start | bytes 12296 | tf_op jit(solution)/shard_map/ppermute | solution.py:269
  76.8 2.1 %copy-start.4 = (f32[96,64]{0,1:T(8,128)S(1)}, f32[96,64]{0,1:T(8,128)}, u32[]{:S(2)}) copy-start(f32[96,64]{0,1:T(8,128)} %param.18) | copy-start | bytes 73732

commit v9 on v7

--- a/solution.py
+++ b/solution.py
@@ -109,11 +109,13 @@
             rows = pl.ds(i * half, half)
             copies.append(pltpu.make_async_copy(hbm.at[0, rows], ref.at[rows], sems.at[len(copies)]))
     copies.append(pltpu.make_async_copy(down_hbm.at[0], down_ref, sems.at[4]))
-    for copy in copies:
-        copy.start()
+    copies[0].start()
+    copies[1].start()
     for i in range(2):
         rows = pl.ds(i * half, half)
         copies[i].wait()
+        for copy in copies[2:4] if i == 0 else copies[4:5]:
+            copy.start()
         for n in range(count):
             cols = pl.ds(n * block, block)
             part = jnp.dot(x_ref[:, rows], gate_ref[rows, cols], preferred_element_type=f32)

time: 77.2 us -> 77.4 us (level)
  no operation moved by 1% of the time
where the time goes in v9:
time: 77.4 us; the launch traced here: 76.8 us
  waiting for transfers between devices  34.2 us (44%)
  starting transfers between devices  26.1 us (34%)
  Pallas kernels  15.2 us (20%)
  between operations  0.84 us (1%)
    ppermute x10, waiting for transfers between devices, swap(): return lax.ppermute(value, axis, [(i, i ^ bits) for i in range(size)])  27.5 us
    ppermute x10, starting transfers between devices, swap(): return lax.ppermute(value, axis, [(i, i ^ bits) for i in range(size)])  14.9 us
    pallas_call x1, Pallas kernels, ffn(): pl.pallas_call(ffn_kernel, in_specs=whole(1) + [anywhere] * 3, out_specs=...  7.46 us
    all_to_all x1, starting transfers between devices, local(): lax.all_to_all(outgoing, SHARD, split_axis=0, concat_axis=0, tiled=True)  5.78 us
    all_to_all x1, waiting for transfers between devices, local(): lax.all_to_all(outgoing, SHARD, split_axis=0, concat_axis=0, tiled=True)  3.62 us
    all_to_all x1, starting transfers between devices, local(): lax.all_to_all(result, SHARD, split_axis=0, concat_axis=0, tiled=True)  3.59 us
    ppermute x1, waiting for transfers between devices, outer_finish(): lax.ppermute(squares, ('zh', 'zl'), [(z, (z + 1 if z % 2 else z - 1) % 8)...  3.08 us
    pallas_call x1, Pallas kernels, local(): pl.pallas_call(dispatch_kernel, in_specs=[pl.BlockSpec(memory_space=pl.AN...  2.8 us
  transfers between devices with their start and end apart: 13, of which 10 were waited for; matrix products, arithmetic and copies ran while one was open for 1% of the time, Pallas kernels for 14%

profile of v9, /device:TPU:24, one launch (start us, length us, event | category | flops | bytes accessed | tf_op | source)
XLA Modules:
  0.0 76.8 jit_solution(10865811514935662331)
XLA Ops:
  0.6 2.8 %dispatch.1 = bf16[8,48,2048]{2,1,0:T(8,128)(2,1)} custom-call(s32[2,128]{1,0:T(2,128)} %bitcast.18, bf16[128,2048]{1,0:T(8,128)(2,1)} %tokens_hbm.1), custom_call_target="tpu_custom_call" | custom-call | tf_op jit(solution)/shard_map/dispatch/pallas_call | solution.py:377
  3.4 0.0 copy-start
  3.4 5.8 %all-to-all-start = ((bf16[8,48,2048]{2,1,0:T(8,128)(2,1)}), bf16[8,48,2048]{2,1,0:T(8,128)(2,1)S(1)}, u32[]{:S(2)}, u32[]{:S(2)}) async-start(bf16[8,48,2048]{2,1,0:T(8,128)(2,1)} %dispatch.1), calls=%async_computation | async-start | bytes 3145728 | tf_op jit(solution)/shard_map/all_to_all | solution.py:392
  9.2 0.0 copy-start.3
  9.2 0.0 copy-done
  9.3 0.1 collective-permute-start
  9.4 0.1 stack.27.at_ref.refs_0_
  9.5 1.6 %collective-permute-done.got_ref = f32[96,1024]{1,0:T(8,128)S(1)} collective-permute-done((f32[96,1024]{1,0:T(8,128)S(1)}, f32[96,1024]{1,0:T(8,128)S(1)}, u32[]{:S(2)}, u32[]{:S(2)}) %collective-permute-start) | collective-permute-done | bytes 393248 | tf_op jit(solution)/shard_map/ppermute | solution.py:271
  11.1 0.6 delta_halve_first.1
  11.7 0.8 %collective-permute-start.1 = (bf16[96,512]{1,0:T(8,128)(2,1)S(1)}, bf16[96,512]{1,0:T(8,128)(2,1)S(1)}, u32[]{:S(2)}, u32[]{:S(2)}) collective-permute-start(bf16[96,512]{1,0:T(8,128)(2,1)S(1)} %get-tuple-element.24), channel_id=1, source_target_pairs={{0,16},{16,0},{32,48},{48,32},{1,17},{17,1},{33,49},{49,33},{2,18}... | collective-permute-start | bytes 294920 | tf_op jit(solution)/shard_map/ppermute | solution.py:271
  12.5 0.0 copy-done.3
  12.5 0.1 fusion
  12.6 0.1 copy.15
  12.7 0.1 copy.16
  12.8 3.9 %collective-permute-done.1.got_ref = bf16[96,512]{1,0:T(8,128)(2,1)S(1)} collective-permute-done((bf16[96,512]{1,0:T(8,128)(2,1)S(1)}, bf16[96,512]{1,0:T(8,128)(2,1)S(1)}, u32[]{:S(2)}, u32[]{:S(2)}) %collective-permute-start.1) | collective-permute-done | bytes 98336 | tf_op jit(solution)/shard_map/ppermute | solution.py:271
  16.6 0.6 delta_halve.1
  17.2 0.3 collective-permute-start.2
  17.5 0.1 pad_maximum_fusion.2.mom_ref
  17.6 5.0 %collective-permute-done.2.got_ref = bf16[96,256]{1,0:T(8,128)(2,1)S(1)} collective-permute-done((bf16[96,256]{1,0:T(8,128)(2,1)S(1)}, bf16[96,256]{1,0:T(8,128)(2,1)S(1)}, u32[]{:S(2)}, u32[]{:S(2)}) %collective-permute-start.2) | collective-permute-done | bytes 49184 | tf_op jit(solution)/shard_map/ppermute | solution.py:271
  22.6 3.4 %collective-permute-start.3 = (bf16[5,48,128]{2,1,0:T(8,128)(2,1)S(1)}, bf16[5,48,128]{2,1,0:T(8,128)(2,1)S(1)}, u32[]{:S(2)}, u32[]{:S(2)}) collective-permute-start(bf16[5,48,128]{2,1,0:T(8,128)(2,1)S(1)} %get-tuple-element.29.sent_ref), channel_id=1, source_target_pairs={{0,64},{64,0},{128,192},{192,128},{1,65},{65,1},{129,193},{193,129... | collective-permute-start | bytes 184328 | tf_op jit(solution)/shard_map/ppermute | solution.py:271
  26.0 2.3 %collective-permute-done.3.got_ref = bf16[5,48,128]{2,1,0:T(8,128)(2,1)S(1)} collective-permute-done((bf16[5,48,128]{2,1,0:T(8,128)(2,1)S(1)}, bf16[5,48,128]{2,1,0:T(8,128)(2,1)S(1)}, u32[]{:S(2)}, u32[]{:S(2)}) %collective-permute-start.3) | collective-permute-done | bytes 61472 | tf_op jit(solution)/shard_map/ppermute | solution.py:271
  28.3 3.6 %all-to-all-done = bf16[8,48,2048]{2,1,0:T(8,128)(2,1)S(1)} async-done(((bf16[8,48,2048]{2,1,0:T(8,128)(2,1)}), bf16[8,48,2048]{2,1,0:T(8,128)(2,1)S(1)}, u32[]{:S(2)}, u32[]{:S(2)}) %all-to-all-start) | async-done | bytes 1572896 | tf_op jit(solution)/shard_map/all_to_all | solution.py:392
  31.9 4.8 %collective-permute-start.4 = (bf16[6,48,128]{2,1,0:T(8,128)(2,1)S(1)}, bf16[6,48,128]{2,1,0:T(8,128)(2,1)S(1)}, u32[]{:S(2)}, u32[]{:S(2)}) collective-permute-start(bf16[6,48,128]{2,1,0:T(8,128)(2,1)S(1)} %get-tuple-element.33.refs_1_), channel_id=1, source_target_pairs={{0,192},{64,128},{128,64},{192,0},{1,193},{65,129},{129,65},{193,1... | collective-permute-start | bytes 221192 | tf_op jit(solution)/shard_map/ppermute | solution.py:271
  36.7 7.5 %expert_ffn.1 = bf16[384,2048]{1,0:T(8,128)(2,1)} custom-call(bf16[384,2048]{1,0:T(8,128)(2,1)S(1)} %bitcast.16, bf16[1,2048,768]{2,1,0:T(8,128)(2,1)} %gate_hbm.1, bf16[1,2048,768]{2,1,0:T(8,128)(2,1)} %up_hbm.1, bf16[1,768,2048]{2,1,0:T(8,128)(2,1)} %down_hbm.1), custom_call_target="tpu_custom_call" | custom-call | flops 3623878656 | bytes 12582912 | tf_op jit(solution)/shard_map/expert_ffn/pallas_call | solution.py:147
  44.1 0.0 collective-permute-done.4.refs_2_
  44.2 3.6 %all-to-all-start.1 = ((bf16[8,48,2048]{2,1,0:T(8,128)(2,1)}), bf16[8,48,2048]{2,1,0:T(8,128)(2,1)S(1)}, u32[]{:S(2)}, u32[]{:S(2)}) async-start(bf16[8,48,2048]{2,1,0:T(8,128)(2,1)} %bitcast.10), calls=%async_computation.1 | async-start | bytes 3145728 | tf_op jit(solution)/shard_map/all_to_all | solution.py:397
  47.8 0.0 copy-start.5
  47.8 0.0 copy-start.6
  47.8 0.3 collective-permute-start.5
  48.1 5.6 %collective-permute-done.5 = bf16[1,8,48,128]{3,2,1,0:T(8,128)(2,1)S(1)} collective-permute-done((bf16[1,8,48,128]{3,2,1,0:T(8,128)(2,1)S(1)}, bf16[1,8,48,128]{3,2,1,0:T(8,128)(2,1)S(1)}, u32[]{:S(2)}, u32[]{:S(2)}) %collective-permute-start.5) | collective-permute-done | bytes 98336 | tf_op jit(solution)/shard_map/ppermute | solution.py:271
  53.7 0.1 collective-permute-start.6
  53.8 5.7 %collective-permute-done.6 = bf16[2,8,48,128]{3,2,1,0:T(8,128)(2,1)S(1)} collective-permute-done((bf16[2,8,48,128]{3,2,1,0:T(8,128)(2,1)S(1)}, bf16[2,8,48,128]{3,2,1,0:T(8,128)(2,1)S(1)}, u32[]{:S(2)}, u32[]{:S(2)}) %collective-permute-start.6) | collective-permute-done | bytes 196640 | tf_op jit(solution)/shard_map/ppermute | solution.py:271
  59.5 0.0 copy-start.1
  59.6 0.0 copy-start.2
  59.6 0.1 collective-permute-start.7
  59.7 1.7 %collective-permute-done.7.b_ref.refs_4_ = bf16[4,8,48,128]{3,2,1,0:T(8,128)(2,1)S(1)} collective-permute-done((bf16[4,8,48,128]{3,2,1,0:T(8,128)(2,1)S(1)}, bf16[4,8,48,128]{3,2,1,0:T(8,128)(2,1)S(1)}, u32[]{:S(2)}, u32[]{:S(2)}) %collective-permute-start.7) | collective-permute-done | bytes 393248 | tf_op jit(solution)/shard_map/ppermute | solution.py:271
  61.4 0.2 delta_squares.1
  61.6 1.8 %collective-permute-start.8 = (f32[8,128]{1,0:T(8,128)S(1)}, f32[8,128]{1,0:T(8,128)S(1)}, u32[]{:S(2)}, u32[]{:S(2)}) collective-permute-start(f32[8,128]{1,0:T(8,128)S(1)} %delta_squares.1), channel_id=1, source_target_pairs={{0,193},{1,64},{64,1},{65,128},{128,65},{129,192},{192,129},{193,0... | collective-permute-start | bytes 12296 | tf_op jit(solution)/shard_map/ppermute | solution.py:349
  63.4 3.1 %collective-permute-done.8 = f32[8,128]{1,0:T(8,128)S(1)} collective-permute-done((f32[8,128]{1,0:T(8,128)S(1)}, f32[8,128]{1,0:T(8,128)S(1)}, u32[]{:S(2)}, u32[]{:S(2)}) %collective-permute-start.8) | collective-permute-done | bytes 4128 | tf_op jit(solution)/shard_map/ppermute | solution.py:349
  66.5 1.9 %collective-permute-start.9 = (f32[8,128]{1,0:T(8,128)S(1)}, f32[8,128]{1,0:T(8,128)S(1)}, u32[]{:S(2)}, u32[]{:S(2)}) collective-permute-start(f32[8,128]{1,0:T(8,128)S(1)} %add.22), channel_id=1, source_target_pairs={{0,2},{2,0},{4,6},{6,4},{1,3},{3,1},{5,7},{7,5},{8,10},{10,8},{12,... | collective-permute-start | bytes 12296 | tf_op jit(solution)/shard_map/ppermute | solution.py:271
  68.4 0.0 copy-done.5
  68.4 1.7 %collective-permute-done.9 = f32[8,128]{1,0:T(8,128)S(1)} collective-permute-done((f32[8,128]{1,0:T(8,128)S(1)}, f32[8,128]{1,0:T(8,128)S(1)}, u32[]{:S(2)}, u32[]{:S(2)}) %collective-permute-start.9) | collective-permute-done | bytes 4128 | tf_op jit(solution)/shard_map/ppermute | solution.py:271
  70.1 3.1 %collective-permute-start.10 = (f32[8,128]{1,0:T(8,128)S(1)}, f32[8,128]{1,0:T(8,128)S(1)}, u32[]{:S(2)}, u32[]{:S(2)}) collective-permute-start(f32[8,128]{1,0:T(8,128)S(1)} %add.23.refs_1_), channel_id=1, source_target_pairs={{0,6},{2,4},{4,2},{6,0},{1,7},{3,5},{5,3},{7,1},{8,14},{10,12},{12... | collective-permute-start | bytes 12296 | tf_op jit(solution)/shard_map/ppermute | solution.py:271
  73.2 0.0 copy-done.6
  73.2 0.0 all-to-all-done.1
  73.3 0.0 copy-start.4
  73.3 1.7 %combine.1 = bf16[128,2048]{1,0:T(8,128)(2,1)} custom-call(f32[4,128]{1,0:T(4,128)S(1)} %pad_maximum_fusion.3.table_ref, bf16[384,2048]{1,0:T(8,128)(2,1)S(1)} %bitcast.15), custom_call_target="tpu_custom_call" | custom-call | tf_op jit(solution)/shard_map/combine/pallas_call | solution.py:398
  75.0 0.0 collective-permute-done.10.refs_2_
  75.0 0.0 copy-done.1
  75.0 0.0 copy-done.2
  75.0 0.0 copy-done.4
  75.0 1.8 %outer_update.1 = (bf16[1,96,2048]{2,1,0:T(8,128)(2,1)}, f32[64,96]{1,0:T(8,128)}) custom-call(s32[6]{0:T(128)S(1)} %stack.27.at_ref.refs_0_, f32[8,128]{1,0:T(8,128)S(1)} %add.23.refs_1_, f32[8,128]{1,0:T(8,128)S(1)} %collective-permute-done.10.refs_2_, bf16[4,8,48,128]{3,2,1,0:T(8,128)(2,1)S(1)} %pad_maximum_fusion.a_ref.refs_3_, ...), custom_call_target="tpu_custom_call" | custom-call | tf_op jit(solution)/shard_map/outer_update/pallas_call | solution.py:356
  (10 shorter events, 0.2 us)
Async XLA Ops:
  3.4 5.8 %copy-start = (f32[1,96,2048]{2,1,0:T(8,128)S(1)}, f32[1,96,2048]{2,1,0:T(8,128)}, u32[]{:S(2)}) copy-start(f32[1,96,2048]{2,1,0:T(8,128)} %own_ref.1) | copy-start | bytes 2359300
  3.4 28.5 %all-to-all-start = ((bf16[8,48,2048]{2,1,0:T(8,128)(2,1)}), bf16[8,48,2048]{2,1,0:T(8,128)(2,1)S(1)}, u32[]{:S(2)}, u32[]{:S(2)}) async-start(bf16[8,48,2048]{2,1,0:T(8,128)(2,1)} %dispatch.1), calls=%async_computation | async-start | bytes 3145728 | tf_op jit(solution)/shard_map/all_to_all | solution.py:392
  9.2 3.3 %copy-start.3 = (f32[96,64]{0,1:T(8,128)S(1)}, f32[96,64]{0,1:T(8,128)}, u32[]{:S(2)}) copy-start(f32[96,64]{0,1:T(8,128)} %param.18) | copy-start | bytes 73732
  9.3 1.8 %collective-permute-start = (f32[96,1024]{1,0:T(8,128)S(1)}, f32[96,1024]{1,0:T(8,128)S(1)}, u32[]{:S(2)}, u32[]{:S(2)}) collective-permute-start(f32[96,1024]{1,0:T(8,128)S(1)} %dynamic-slice_bitcast_fusion), channel_id=1, source_target_pairs={{0,8},{8,0},{1,9},{9,1},{2,10},{10,2},{3,11},{11,3},{4,12},{12,4},... | collective-permute-start | bytes 1179656 | tf_op jit(solution)/shard_map/ppermute | solution.py:271
  11.7 4.9 %collective-permute-start.1 = (bf16[96,512]{1,0:T(8,128)(2,1)S(1)}, bf16[96,512]{1,0:T(8,128)(2,1)S(1)}, u32[]{:S(2)}, u32[]{:S(2)}) collective-permute-start(bf16[96,512]{1,0:T(8,128)(2,1)S(1)} %get-tuple-element.24), channel_id=1, source_target_pairs={{0,16},{16,0},{32,48},{48,32},{1,17},{17,1},{33,49},{49,33},{2,18}... | collective-permute-start | bytes 294920 | tf_op jit(solution)/shard_map/ppermute | solution.py:271
  17.2 5.4 %collective-permute-start.2 = (bf16[96,256]{1,0:T(8,128)(2,1)S(1)}, bf16[96,256]{1,0:T(8,128)(2,1)S(1)}, u32[]{:S(2)}, u32[]{:S(2)}) collective-permute-start(bf16[96,256]{1,0:T(8,128)(2,1)S(1)} %get-tuple-element.26), channel_id=1, source_target_pairs={{0,48},{16,32},{32,16},{48,0},{1,49},{17,33},{33,17},{49,1},{2,50}... | collective-permute-start | bytes 147464 | tf_op jit(solution)/shard_map/ppermute | solution.py:271
  22.6 5.7 %collective-permute-start.3 = (bf16[5,48,128]{2,1,0:T(8,128)(2,1)S(1)}, bf16[5,48,128]{2,1,0:T(8,128)(2,1)S(1)}, u32[]{:S(2)}, u32[]{:S(2)}) collective-permute-start(bf16[5,48,128]{2,1,0:T(8,128)(2,1)S(1)} %get-tuple-element.29.sent_ref), channel_id=1, source_target_pairs={{0,64},{64,0},{128,192},{192,128},{1,65},{65,1},{129,193},{193,129... | collective-permute-start | bytes 184328 | tf_op jit(solution)/shard_map/ppermute | solution.py:271
  31.9 12.2 %collective-permute-start.4 = (bf16[6,48,128]{2,1,0:T(8,128)(2,1)S(1)}, bf16[6,48,128]{2,1,0:T(8,128)(2,1)S(1)}, u32[]{:S(2)}, u32[]{:S(2)}) collective-permute-start(bf16[6,48,128]{2,1,0:T(8,128)(2,1)S(1)} %get-tuple-element.33.refs_1_), channel_id=1, source_target_pairs={{0,192},{64,128},{128,64},{192,0},{1,193},{65,129},{129,65},{193,1... | collective-permute-start | bytes 221192 | tf_op jit(solution)/shard_map/ppermute | solution.py:271
  44.2 29.1 %all-to-all-start.1 = ((bf16[8,48,2048]{2,1,0:T(8,128)(2,1)}), bf16[8,48,2048]{2,1,0:T(8,128)(2,1)S(1)}, u32[]{:S(2)}, u32[]{:S(2)}) async-start(bf16[8,48,2048]{2,1,0:T(8,128)(2,1)} %bitcast.10), calls=%async_computation.1 | async-start | bytes 3145728 | tf_op jit(solution)/shard_map/all_to_all | solution.py:397
  47.8 20.6 %copy-start.5 = (s32[128,2]{0,1:T(2,128)S(1)}, s32[128,2]{0,1:T(2,128)}, u32[]{:S(2)}) copy-start(s32[128,2]{0,1:T(2,128)} %param.11) | copy-start | bytes 3076
  47.8 25.5 %copy-start.6 = (f32[128,2]{0,1:T(2,128)S(1)}, f32[128,2]{0,1:T(2,128)}, u32[]{:S(2)}) copy-start(f32[128,2]{0,1:T(2,128)} %param.12) | copy-start | bytes 3076
  47.8 5.9 %collective-permute-start.5 = (bf16[1,8,48,128]{3,2,1,0:T(8,128)(2,1)S(1)}, bf16[1,8,48,128]{3,2,1,0:T(8,128)(2,1)S(1)}, u32[]{:S(2)}, u32[]{:S(2)}) collective-permute-start(bf16[1,8,48,128]{3,2,1,0:T(8,128)(2,1)S(1)} %delta_mean.1), channel_id=1, source_target_pairs={{0,48},{16,32},{32,16},{48,0},{1,49},{17,33},{33,17},{49,1},{2,50}... | collective-permute-start | bytes 294920 | tf_op jit(solution)/shard_map/ppermute | solution.py:271
  53.7 5.8 %collective-permute-start.6 = (bf16[2,8,48,128]{3,2,1,0:T(8,128)(2,1)S(1)}, bf16[2,8,48,128]{3,2,1,0:T(8,128)(2,1)S(1)}, u32[]{:S(2)}, u32[]{:S(2)}) collective-permute-start(bf16[2,8,48,128]{3,2,1,0:T(8,128)(2,1)S(1)} %pad_maximum_fusion.1), channel_id=1, source_target_pairs={{0,16},{16,0},{32,48},{48,32},{1,17},{17,1},{33,49},{49,33},{2,18}... | collective-permute-start | bytes 589832 | tf_op jit(solution)/shard_map/ppermute | solution.py:271
  59.5 15.4 %copy-start.1 = (f32[96,2048]{1,0:T(8,128)S(1)}, f32[96,2048]{1,0:T(8,128)}, u32[]{:S(2)}) copy-start(f32[96,2048]{1,0:T(8,128)} %refs_5_.1) | copy-start | bytes 2359300
  59.6 15.4 %copy-start.2 = (bf16[1,96,2048]{2,1,0:T(8,128)(2,1)S(1)}, bf16[1,96,2048]{2,1,0:T(8,128)(2,1)}, u32[]{:S(2)}) copy-start(bf16[1,96,2048]{2,1,0:T(8,128)(2,1)} %refs_6_.1) | copy-start | bytes 1179652
  59.6 1.8 %collective-permute-start.7 = (bf16[4,8,48,128]{3,2,1,0:T(8,128)(2,1)S(1)}, bf16[4,8,48,128]{3,2,1,0:T(8,128)(2,1)S(1)}, u32[]{:S(2)}, u32[]{:S(2)}) collective-permute-start(bf16[4,8,48,128]{3,2,1,0:T(8,128)(2,1)S(1)} %pad_maximum_fusion.a_ref.refs_3_), channel_id=1, source_target_pairs={{0,8},{8,0},{1,9},{9,1},{2,10},{10,2},{3,11},{11,3},{4,12},{12,4},... | collective-permute-start | bytes 1179656 | tf_op jit(solution)/shard_map/ppermute | solution.py:271
  61.6 4.9 %collective-permute-start.8 = (f32[8,128]{1,0:T(8,128)S(1)}, f32[8,128]{1,0:T(8,128)S(1)}, u32[]{:S(2)}, u32[]{:S(2)}) collective-permute-start(f32[8,128]{1,0:T(8,128)S(1)} %delta_squares.1), channel_id=1, source_target_pairs={{0,193},{1,64},{64,1},{65,128},{128,65},{129,192},{192,129},{193,0... | collective-permute-start | bytes 12296 | tf_op jit(solution)/shard_map/ppermute | solution.py:349
  66.5 3.6 %collective-permute-start.9 = (f32[8,128]{1,0:T(8,128)S(1)}, f32[8,128]{1,0:T(8,128)S(1)}, u32[]{:S(2)}, u32[]{:S(2)}) collective-permute-start(f32[8,128]{1,0:T(8,128)S(1)} %add.22), channel_id=1, source_target_pairs={{0,2},{2,0},{4,6},{6,4},{1,3},{3,1},{5,7},{7,5},{8,10},{10,8},{12,... | collective-permute-start | bytes 12296 | tf_op jit(solution)/shard_map/ppermute | solution.py:271
  70.1 4.9 %collective-permute-start.10 = (f32[8,128]{1,0:T(8,128)S(1)}, f32[8,128]{1,0:T(8,128)S(1)}, u32[]{:S(2)}, u32[]{:S(2)}) collective-permute-start(f32[8,128]{1,0:T(8,128)S(1)} %add.23.refs_1_), channel_id=1, source_target_pairs={{0,6},{2,4},{4,2},{6,0},{1,7},{3,5},{5,3},{7,1},{8,14},{10,12},{12... | collective-permute-start | bytes 12296 | tf_op jit(solution)/shard_map/ppermute | solution.py:271
  73.3 1.7 %copy-start.4 = (f32[96,64]{0,1:T(8,128)S(1)}, f32[96,64]{0,1:T(8,128)}, u32[]{:S(2)}) copy-start(f32[96,64]{0,1:T(8,128)} %param.18) | copy-start | bytes 73732
